TPU v7x, 128 devices: a whole 4x4x4 slice. The times are simulated.
128 devices in a mesh: fsdp: 64 (over x_hi, z, y, core), seq: 2 (over x_lo).
Axes of the slice: x: 4 (x_hi: 2, x_lo: 2; x = x_hi * 2 + x_lo), y: 4, z: 4, core: 2. Of those that a mesh axis runs over, the one named last changes fastest.
Arguments:
- hidden_in: bfloat16 [64, 256, 2048], P('fsdp', 'seq'), may hold values from -6 to 6
- norm_gain: bfloat16 [2048], P('fsdp'), may hold values from 0.099609375 to 1.8984375
- norm_shift: bfloat16 [2048], P('fsdp'), may hold values from -4 to 4
- qkv_weight: bfloat16 [2048, 6144], P('fsdp'), may hold values from -0.125 to 0.125
- qkv_bias: bfloat16 [6144], P('fsdp'), may hold values from -4 to 4
- proj_weight: bfloat16 [2048, 2048], P('fsdp'), may hold values from -0.5 to 0.5
- proj_bias: bfloat16 [2048], P('fsdp'), may hold values from -4 to 4
- up_weight: bfloat16 [2048, 8192], P('fsdp'), may hold values from -0.125 to 0.125
- up_bias: bfloat16 [8192], P('fsdp'), may hold values from -6 to 6
- down_weight: bfloat16 [8192, 2048], P('fsdp'), may hold values from -0.0625 to 0.0625
- down_bias: bfloat16 [2048], P('fsdp'), may hold values from -4 to 4
- segment_ids: int32 [64, 256], P('fsdp'), may hold values from 0 to 2, as said below
- positions: int32 [64, 256], P('fsdp', 'seq'), may hold values from 0 to 1023, as said below
- cotangent: bfloat16 [64, 256, 2048], P('fsdp', 'seq'), may hold values from -16 to 16
Outputs:
- block_out: bfloat16 [64, 256, 2048], P('fsdp', 'seq')
- grad_hidden: float32 [64, 256, 2048], P('fsdp', 'seq')
- grad_gain: float32 [2048], P('fsdp')
- grad_shift: float32 [2048], P('fsdp')
- grad_qkv: float32 [2048, 6144], P('fsdp')
- grad_qkv_bias: float32 [6144], P('fsdp')
- grad_proj: float32 [2048, 2048], P('fsdp')
- grad_proj_bias: float32 [2048], P('fsdp')
- grad_up: float32 [2048, 8192], P('fsdp')
- grad_up_bias: float32 [8192], P('fsdp')
- grad_down: float32 [8192, 2048], P('fsdp')
- grad_down_bias: float32 [2048], P('fsdp')
Inputs may be any that keep to these rules, and one draw needn't show every extreme that they name: `segment_ids`: ids never fall along a sequence; every sequence holds three documents, ids 0, 1 and 2; the first and the last have 256/8 to 95 tokens. `positions`: within a document the position rises by one from token to token; the first document of a sequence starts at 0; the last token of every sequence has the largest position.
All inputs are finite; a program needn't handle non-finite values.
Results may differ from a plain program's by a relative error of at most 0.009.
Values may be sent and summed in bfloat16 or wider, within the bound.
No kernel may reach another device: no remote copies, remote signals or barrier semaphores. Data moves between devices by JAX's collectives and lax.ppermute only.
A program may use at most 896 MiB of HBM per device.

v0:
```python
import math

import jax
import jax.numpy as jnp
from jax import lax
from jax.sharding import PartitionSpec as P

H = 32
HD = 64
ROT = 32


norm_eps = 1e-05


def normalize(hidden):
    mean = jnp.mean(hidden, axis=-1, keepdims=True)
    centered = hidden - mean
    spread = jnp.mean(centered * centered, axis=-1, keepdims=True)
    return centered * lax.rsqrt(spread + norm_eps)


def rotary(values, position):
    half_rot = ROT // 2
    freqs = 10000.0 ** (-jnp.arange(half_rot, dtype=jnp.float32) * (2.0 / ROT))
    angles = position.astype(jnp.float32)[..., None] * freqs
    cosine = jnp.cos(angles)[..., None, :]
    sine = jnp.sin(angles)[..., None, :]
    first = values[..., :half_rot]
    second = values[..., half_rot:ROT]
    rest = values[..., ROT:]
    return jnp.concatenate(
        [first * cosine - second * sine, second * cosine + first * sine, rest], axis=-1
    )


def contract_rows(left, right):
    return lax.dot_general(
        left, right, (((0,), (0,)), ((), ())), preferred_element_type=jnp.float32
    )


def contract_cols(left, right):
    return lax.dot_general(
        left, right, (((1,), (1,)), ((), ())), preferred_element_type=jnp.float32
    )


def local(
    hidden_in,
    norm_gain,
    norm_shift,
    qkv_weight,
    qkv_bias,
    proj_weight,
    proj_bias,
    up_weight,
    up_bias,
    down_weight,
    down_bias,
    segment_ids,
    positions,
    cotangent,
):
    seq_count, half, width = hidden_in.shape
    hidden_units = up_weight.shape[1]
    rows = seq_count * half
    shards = lax.axis_size("fsdp")
    d_share = width // shards
    f_share = hidden_units // shards
    place = lax.axis_index("seq") * half
    scale = 1.0 / math.sqrt(HD)
    hidden = hidden_in.reshape(rows, width).astype(jnp.float32)
    normal = normalize(hidden)
    gain_all, shift_all, qkv_all, qkv_bias_all, up_all, up_bias_all = (
        lax.all_gather(norm_gain[None], "fsdp", axis=0, tiled=True),
        lax.all_gather(norm_shift[None], "fsdp", axis=0, tiled=True),
        lax.all_gather(qkv_weight[None], "fsdp", axis=0, tiled=True),
        lax.all_gather(qkv_bias[None], "fsdp", axis=0, tiled=True),
        lax.all_gather(up_weight[None], "fsdp", axis=0, tiled=True),
        lax.all_gather(up_bias[None], "fsdp", axis=0, tiled=True),
    )
    gain_row = gain_all.reshape(-1).astype(jnp.float32)
    shift_row = shift_all.reshape(-1).astype(jnp.float32)
    normed = (normal * gain_row + shift_row).astype(jnp.bfloat16)
    merged = jnp.dot(normed, qkv_all.reshape(width, 3 * width), preferred_element_type=jnp.float32)
    merged = merged + qkv_bias_all.reshape(-1).astype(jnp.float32)
    upper = jnp.dot(normed, up_all.reshape(width, hidden_units), preferred_element_type=jnp.float32)
    upper = upper + up_bias_all.reshape(-1).astype(jnp.float32)
    query = merged[:, :width].reshape(seq_count, half, H, HD)
    keys = merged[:, width : 2 * width].reshape(seq_count, half, H, HD)
    query_b = rotary(query, positions).astype(jnp.bfloat16)
    keys_b = rotary(keys, positions).astype(jnp.bfloat16)
    values_b = merged[:, 2 * width :].reshape(seq_count, half, H, HD).astype(jnp.bfloat16)
    all_keys, all_values = (
        lax.all_gather(keys_b, "seq", axis=1, tiled=True),
        lax.all_gather(values_b, "seq", axis=1, tiled=True),
    )
    length = segment_ids.shape[1]
    query_segment = lax.dynamic_slice_in_dim(segment_ids, place, half, 1)
    query_index = place + jnp.arange(half)
    causal = jnp.arange(length)[None, :] <= query_index[:, None]
    allowed = (causal[None] & (segment_ids[:, None, :] == query_segment[:, :, None]))[:, None]

    def scores_of():
        raw = jnp.einsum("nqhd,nkhd->nhqk", query_b, all_keys, preferred_element_type=jnp.float32)
        return jnp.where(allowed, scale * raw, -1e30)

    scores = scores_of()
    top = jnp.max(scores, axis=-1, keepdims=True)
    expo = jnp.exp(scores - top)
    total = jnp.sum(expo, axis=-1, keepdims=True)
    log_total = top + jnp.log(total)
    probs_b = (expo / total).astype(jnp.bfloat16)
    context = jnp.einsum("nhqk,nkhd->nqhd", probs_b, all_values, preferred_element_type=jnp.float32)
    context_b = context.reshape(rows, width).astype(jnp.bfloat16)
    active_b = jax.nn.gelu(upper, approximate=True).astype(jnp.bfloat16)
    proj_all, proj_bias_all, down_all, down_bias_all = (
        lax.all_gather(proj_weight[None], "fsdp", axis=0, tiled=True),
        lax.all_gather(proj_bias[None], "fsdp", axis=0, tiled=True),
        lax.all_gather(down_weight[None], "fsdp", axis=0, tiled=True),
        lax.all_gather(down_bias[None], "fsdp", axis=0, tiled=True),
    )
    branch = jnp.dot(context_b, proj_all.reshape(width, width), preferred_element_type=jnp.float32)
    branch = branch + jnp.dot(
        active_b, down_all.reshape(hidden_units, width), preferred_element_type=jnp.float32
    )
    output = (
        hidden
        + branch
        + proj_bias_all.reshape(-1).astype(jnp.float32)
        + down_bias_all.reshape(-1).astype(jnp.float32)
    )
    block_out = output.astype(jnp.bfloat16).reshape(seq_count, half, width)
    grad_out_b = cotangent.reshape(rows, width)
    grad_out = grad_out_b.astype(jnp.float32)
    out_sum = jnp.sum(grad_out, axis=0)
    proj_piece = lax.all_gather(proj_weight[None], "fsdp", axis=0, tiled=True)
    down_piece = lax.all_gather(down_weight[None], "fsdp", axis=0, tiled=True)
    count = proj_piece.shape[0]
    part_context = contract_cols(grad_out_b, proj_piece.reshape(count * d_share, width))
    part_active = contract_cols(grad_out_b, down_piece.reshape(count * f_share, width))
    grad_context = part_context
    grad_active = part_active
    grad_context, grad_active = (grad_context, grad_active)

    def shard_rows(vector, share):
        return vector.reshape(shards, share)

    def pad_rows(pieces, count):
        joined = jnp.concatenate(pieces, axis=1)
        filler = jnp.zeros((count, 8 * width - joined.shape[1]), jnp.float32)
        return jnp.concatenate([joined, filler], axis=1).reshape(count, 8, width)

    out_rows = d_share + f_share + 8
    in_rows = 3 * d_share + f_share + 8
    _, gelu_pull = jax.vjp(lambda value: jax.nn.gelu(value, approximate=True), upper)
    grad_upper_b = gelu_pull(grad_active)[0].astype(jnp.bfloat16)
    grad_context_b = grad_context.reshape(seq_count, half, H, HD).astype(jnp.bfloat16)
    scores = scores_of()
    probs = jnp.exp(scores - log_total)
    probs_b = probs.astype(jnp.bfloat16)
    grad_values_all = jnp.einsum(
        "nhqk,nqhd->nkhd", probs_b, grad_context_b, preferred_element_type=jnp.float32
    )
    grad_probs = jnp.einsum(
        "nqhd,nkhd->nhqk", grad_context_b, all_values, preferred_element_type=jnp.float32
    )
    grad_scores = probs * (grad_probs - jnp.sum(probs * grad_probs, axis=-1, keepdims=True))
    grad_scores_b = grad_scores.astype(jnp.bfloat16)
    grad_query = scale * jnp.einsum(
        "nhqk,nkhd->nqhd", grad_scores_b, all_keys, preferred_element_type=jnp.float32
    )
    grad_keys_all = scale * jnp.einsum(
        "nhqk,nqhd->nkhd", grad_scores_b, query_b, preferred_element_type=jnp.float32
    )
    grad_keys, grad_values = (
        lax.psum_scatter(grad_keys_all, "seq", scatter_dimension=1, tiled=True),
        lax.psum_scatter(grad_values_all, "seq", scatter_dimension=1, tiled=True),
    )
    _, rotary_pull = jax.vjp(lambda value: rotary(value, positions), query)
    grad_query_pre = rotary_pull(grad_query)[0].reshape(rows, width)
    grad_keys_pre = rotary_pull(grad_keys)[0].reshape(rows, width)
    grad_merged_b = jnp.concatenate(
        [grad_query_pre, grad_keys_pre, grad_values.reshape(rows, width)], axis=1
    ).astype(jnp.bfloat16)
    gain_piece = lax.all_gather(norm_gain[None], "fsdp", axis=0, tiled=True)
    qkv_piece = lax.all_gather(qkv_weight[None], "fsdp", axis=0, tiled=True)
    up_piece = lax.all_gather(up_weight[None], "fsdp", axis=0, tiled=True)
    count = gain_piece.shape[0]
    part = contract_cols(grad_merged_b, qkv_piece.reshape(count * d_share, 3 * width))
    part = part + contract_cols(grad_upper_b, up_piece.reshape(count * d_share, hidden_units))
    grad_normed = part
    gain_full = gain_piece.reshape(-1)
    grad_normed, gain_full = (grad_normed, gain_full)
    _, norm_pull = jax.vjp(normalize, hidden)
    grad_hidden = grad_out + norm_pull(grad_normed * gain_full.astype(jnp.float32))[0]
    grad_hidden = grad_hidden.reshape(seq_count, half, width)
    gain_sum = jnp.sum(grad_normed * normal, axis=0)
    shift_sum = jnp.sum(grad_normed, axis=0)
    qkv_bias_sum = jnp.sum(grad_merged_b.astype(jnp.float32), axis=0)
    up_bias_sum = jnp.sum(grad_upper_b.astype(jnp.float32), axis=0)

    def in_block(count):
        grad_qkv_part = contract_rows(normed, grad_merged_b).reshape(count, 3 * d_share, width)
        grad_up_part = contract_rows(normed, grad_upper_b).reshape(count, f_share, width)
        small = pad_rows(
            [
                shard_rows(gain_sum, d_share),
                shard_rows(shift_sum, d_share),
                shard_rows(qkv_bias_sum, 3 * d_share),
                shard_rows(up_bias_sum, f_share),
            ],
            count,
        )
        return jnp.concatenate([grad_qkv_part, grad_up_part, small], axis=1)

    number = (out_rows + in_rows) * lax.axis_size("fsdp") // (out_rows + in_rows)
    grad_proj_part = contract_rows(context_b, grad_out_b).reshape(number, d_share, width)
    grad_down_part = contract_rows(active_b, grad_out_b).reshape(number, f_share, width)
    bias_part = shard_rows(out_sum, d_share)
    small = pad_rows([bias_part, bias_part], number)
    summed = lax.psum_scatter(
        jnp.concatenate(
            [jnp.concatenate([grad_proj_part, grad_down_part, small], axis=1), in_block(number)],
            axis=1,
        ).reshape((out_rows + in_rows) * lax.axis_size("fsdp"), width),
        "fsdp",
        scatter_dimension=0,
        tiled=True,
    )
    summed = lax.psum(summed, "seq")
    out_part = summed[:out_rows]
    in_part = summed[out_rows:]
    grad_proj = out_part[:d_share]
    grad_down = out_part[d_share : d_share + f_share]
    out_small = out_part[d_share + f_share :].reshape(-1)
    grad_proj_bias = out_small[:d_share]
    grad_down_bias = out_small[d_share : 2 * d_share]
    grad_qkv = in_part[: 3 * d_share].reshape(d_share, 3 * width)
    grad_up = in_part[3 * d_share : 3 * d_share + f_share].reshape(d_share, hidden_units)
    in_small = in_part[3 * d_share + f_share :].reshape(-1)
    grad_gain = in_small[:d_share]
    grad_shift = in_small[d_share : 2 * d_share]
    grad_qkv_bias = in_small[2 * d_share : 5 * d_share]
    grad_up_bias = in_small[5 * d_share : 5 * d_share + f_share]
    return (
        block_out,
        grad_hidden,
        grad_gain,
        grad_shift,
        grad_qkv,
        grad_qkv_bias,
        grad_proj,
        grad_proj_bias,
        grad_up,
        grad_up_bias,
        grad_down,
        grad_down_bias,
    )


def solution(mesh):
    return jax.shard_map(
        local,
        mesh=mesh,
        in_specs=(
            P("fsdp", "seq", None),
            P("fsdp"),
            P("fsdp"),
            P("fsdp", None),
            P("fsdp"),
            P("fsdp", None),
            P("fsdp"),
            P("fsdp", None),
            P("fsdp"),
            P("fsdp", None),
            P("fsdp"),
            P("fsdp", None),
            P("fsdp", "seq"),
            P("fsdp", "seq", None),
        ),
        out_specs=(
            P("fsdp", "seq", None),
            P("fsdp", "seq", None),
            P("fsdp"),
            P("fsdp"),
            P("fsdp", None),
            P("fsdp"),
            P("fsdp", None),
            P("fsdp"),
            P("fsdp", None),
            P("fsdp"),
            P("fsdp", None),
            P("fsdp"),
        ),
        check_vma=False,
    )
```

profile of v0, /device:TPU:1, one launch (start us, length us, event | category | flops | bytes accessed | tf_op | source)
XLA Modules:
  0.0 2332.1 jit_solution(7620275130348464895)
XLA Ops:
  15.5 327.2 %all-reduce.12 = (bf16[6144]{0:T(1024)(128)(2,1)S(1)}, bf16[2048]{0:T(1024)(128)(2,1)S(1)}, bf16[2048]{0:T(1024)(128)(2,1)S(1)}, bf16[2048]{0:T(1024)(128)(2,1)}, bf16[2048]{0:T(1024)(128)(2,1)}) all-reduce(bf16[6144]{0:T(1024)(128)(2,1)S(1)} %dynamic-update-slice.2, ...), channel_id=5, replica_groups=mesh['fsdp'=64,'seq'=2] {'fsdp'}, use_global_device_ids=true, to_apply=%add.8 | all-reduce | flops 14336 | bytes 57344
  347.7 10.3 convolution_add_fusion.1
  358.1 1.5 fusion.86
  359.5 2.5 copy.40
  363.1 2.5 copy.39
  365.7 2.0 fusion.66
  370.1 6.7 convolution_convert_fusion
  377.7 2.0 copy.38
  381.0 13.6 all-gather.20.cloned.1.call-done
  394.5 2.4 fusion.89
  398.9 2.1 fusion.30
  401.4 20.0 all-gather.18.cloned.1.call-done
  421.4 4.2 multiply_reduce_fusion
  427.1 1.9 multiply_bitcast_fusion
  430.6 95.6 %all-gather.10 = bf16[64,1,128]{2,1,0:T(2,128)(2,1)S(1)} all-gather(bf16[1,1,128]{2,1,0:T(2,128)(2,1)S(1)} %bitcast.181), channel_id=8, replica_groups=mesh['fsdp'=64,'seq'=2] {'fsdp'}, dimensions={0}, use_global_device_ids=true | all-gather | bytes 16640 | tf_op jit(solution)/shard_map/all_gather | solution.py:81
  526.3 2.1 fusion.33
  529.3 2.7 fusion.39
  532.9 8.2 convolution_dynamic-update-slice_fusion.1
  545.2 21.2 fusion.80
  566.3 53.3 %reshape.568 = f32[64,96,2048]{2,1,0:T(8,128)} reshape(f32[2048,6144]{1,0:T(8,128)} %fusion.80) | data formatting | bytes 100663296 | tf_op jit(solution)/shard_map/reshape | solution.py:205
  620.2 20.8 fusion.82
  641.1 18.6 all-gather.26.cloned.1.call-done
  659.6 16.6 fusion.14
  676.2 142.8 %all-gather.28.cloned.1.call-done = bf16[8192,2048]{1,0:T(8,128)(2,1)} async-done(((bf16[128,2048]{1,0:T(8,128)(2,1)}), bf16[8192,2048]{1,0:T(8,128)(2,1)}) %all-gather.28.cloned.1.call-update) | async-done | bytes 33554448 | tf_op jit(solution)/shard_map/all_gather | solution.py:121
  819.0 18.2 convert_reduce_fusion
  837.2 23.2 fusion.78
  860.4 15.9 fusion.84
  876.9 1.5 convert_reduce_fusion.3
  878.4 3.2 copy.42
  881.7 2.3 broadcast_in_dim.58
  884.0 7.4 concatenate.45
  891.4 6.6 copy.43
  898.1 74.5 %reshape.569 = f32[64,128,2048]{2,1,0:T(8,128)} reshape(f32[2048,8192]{1,0:T(8,128)} %fusion.78) | data formatting | bytes 134217728 | tf_op jit(solution)/shard_map/reshape | solution.py:206
  972.7 2.3 broadcast_in_dim.110
  975.1 7.2 concatenate.46
  982.3 6.7 copy.44
  989.1 23.9 %convolution_dynamic-update-slice_fusion = f32[64,400,2048]{2,1,0:T(8,128)} fusion(f32[64,400,2048]{2,1,0:T(8,128)} %convolution_dynamic-update-slice_fusion.1, bf16[64,128,128]{2,1,0:T(8,128)(2,1)S(1)} %bitcast.157, bf16[1,128,2048]{2,1,0:T(8,128)(2,1)S(1)} %copy-done.6), kind=kOutput, calls=%fused_computation | convolution fusion | flops 4294967296 | bytes 69730304 | tf_op jit(solution)/shard_map/dot_general | solution.py:38
  1012.9 2.2 constant_dynamic-update-slice_fusion.3
  1015.2 34.5 %constant_dynamic-update-slice_fusion.2 = f32[64,400,2048]{2,1,0:T(8,128)} fusion(f32[64,400,2048]{2,1,0:T(8,128)} %constant_dynamic-update-slice_fusion.3, f32[64,96,2048]{2,1,0:T(8,128)} %reshape.568), kind=kLoop, calls=%fused_computation.113 | loop fusion | bytes 100663296
  1049.7 43.7 %constant_dynamic-update-slice_fusion.1 = f32[64,400,2048]{2,1,0:T(8,128)} fusion(f32[64,400,2048]{2,1,0:T(8,128)} %constant_dynamic-update-slice_fusion.2, f32[64,128,2048]{2,1,0:T(8,128)} %reshape.569), kind=kLoop, calls=%fused_computation.112 | loop fusion | bytes 134217728
  1093.3 4.7 constant_dynamic-update-slice_fusion
  1098.3 1116.0 %reduce-scatter.11.cloned.1.call-done = f32[400,2048]{1,0:T(8,128)} async-done(((f32[25600,2048]{1,0:T(8,128)}), f32[400,2048]{1,0:T(8,128)}) %reduce-scatter.11.cloned.1.call-update) | async-done | bytes 3276816
  2214.4 4.7 fusion.90
  2219.1 19.0 fusion.21
  2238.1 75.3 %all-reduce.15.cloned.1.call-done = f32[400,2048]{1,0:T(8,128)} async-done(((f32[400,2048]{1,0:T(8,128)}), f32[400,2048]{1,0:T(8,128)}) %all-reduce.15.cloned.1.call-update) | async-done | bytes 3276816 | tf_op jit(solution)/shard_map/psum | solution.py:232
  2319.0 2.7 fusion.85
  2321.7 1.4 reshape.579
  2323.1 1.7 slice.109
  (131 shorter events, 35.7 us)
Async XLA Ops:
  7.2 340.6 %all-gather.22.cloned.1.call-start = ((), (), s32[]{:S(2)}) async-start(), calls=%async_computation.8 | async-start | bytes 25559040 | tf_op jit(solution)/shard_map/all_gather | solution.py:78
  7.9 362.2 %all-gather.24.cloned.1.call-start = ((), (), s32[]{:S(2)}) async-start(), calls=%async_computation.9 | async-start | bytes 8519680 | tf_op jit(solution)/shard_map/all_gather | solution.py:119
  8.7 385.9 %all-gather.20.cloned.1.call-start = ((), (), s32[]{:S(2)}) async-start(), calls=%async_computation.4 | async-start | bytes 1572864 | tf_op jit(solution)/shard_map/all_gather | solution.py:96
  344.5 13.5 copy-start.14
  345.8 0.5 copy-start.23
  346.4 11.7 copy-start.16
  368.6 52.8 %all-gather.18.cloned.1.call-start = ((), (), s32[]{:S(2)}) async-start(), calls=%async_computation.3 | async-start | bytes 1572864 | tf_op jit(solution)/shard_map/all_gather | solution.py:97
  370.1 24.4 %copy-start.13 = (bf16[128,32,16]{0,2,1:T(8,128)(2,1)S(1)}, bf16[128,32,16]{0,2,1:T(8,128)(2,1)}, u32[]{:S(2)}) copy-start(bf16[128,32,16]{0,2,1:T(8,128)(2,1)} %get-tuple-element.32) | copy-start | bytes 393220
  380.9 160.2 %reduce-scatter.9.cloned.1.call-start = ((), (), s32[]{:S(2)}) async-start(), calls=%async_computation.6 | async-start | bytes 3145728 | tf_op jit(solution)/shard_map/reduce_scatter | solution.py:179
  394.5 4.4 copy-start.7
  397.0 2.0 copy-start
  401.1 141.5 %reduce-scatter.7.cloned.1.call-start = ((), (), s32[]{:S(2)}) async-start(), calls=%async_computation.5 | async-start | bytes 3145728 | tf_op jit(solution)/shard_map/reduce_scatter | solution.py:178
  421.4 4.2 copy-start.1
  427.1 3.5 copy-start.22
  429.0 230.6 %all-gather.26.cloned.1.call-start = ((), (), s32[]{:S(2)}) async-start(), calls=%async_computation.10 | async-start | bytes 34078720 | tf_op jit(solution)/shard_map/all_gather | solution.py:80
  429.8 389.2 %all-gather.28.cloned.1.call-start = ((), (), s32[]{:S(2)}) async-start(), calls=%async_computation.11 | async-start | bytes 34078720 | tf_op jit(solution)/shard_map/all_gather | solution.py:121
  430.5 1783.8 %reduce-scatter.11.cloned.1.call-start = ((), (), s32[]{:S(2)}) async-start(), calls=%async_computation.12 | async-start | bytes 212992000
  430.6 98.7 %copy-start.2 = (f32[32,128,256]{2,1,0:T(8,128)S(1)}, f32[32,128,256]{2,1,0:T(8,128)}, u32[]{:S(2)}) copy-start(f32[32,128,256]{2,1,0:T(8,128)} %copy-done) | copy-start | bytes 12582916
  528.3 1.0 copy-start.8
  529.3 3.6 copy-start.6
  532.1 0.8 copy-start.10
  532.9 10.8 copy-start.9
  532.9 10.8 copy-start.18
  532.9 10.8 copy-start.19
  541.1 3.8 slice-start
  541.1 4.0 copy-start.3
  541.1 4.0 copy-start.15
  541.1 4.0 copy-start.17
  837.2 23.3 copy-start.12
  860.4 15.9 copy-start.24
  989.1 23.9 %copy-start.5 = (f32[8,8,8,2048]{3,2,1,0:T(8,128)S(1)}, f32[8,8,8,2048]{3,2,1,0:T(8,128)}, u32[]{:S(2)}) copy-start(f32[8,8,8,2048]{3,2,1,0:T(8,128)} %copy.43) | copy-start | bytes 12582916
  1098.0 1116.3 %copy-start.21 = (bf16[2048]{0:T(1024)(128)(2,1)S(1)}, bf16[2048]{0:T(1024)(128)(2,1)}, u32[]{:S(2)}) copy-start(bf16[2048]{0:T(1024)(128)(2,1)} %get-tuple-element.19) | copy-start | bytes 12292
  1098.0 1116.4 %copy-start.20 = (bf16[2048]{0:T(1024)(128)(2,1)S(1)}, bf16[2048]{0:T(1024)(128)(2,1)}, u32[]{:S(2)}) copy-start(bf16[2048]{0:T(1024)(128)(2,1)} %get-tuple-element.20) | copy-start | bytes 12292
  1098.0 1116.4 %copy-start.11 = (bf16[32,64,128]{2,1,0:T(8,128)(2,1)S(1)}, bf16[32,64,128]{2,1,0:T(8,128)(2,1)}, u32[]{:S(2)}) copy-start(bf16[32,64,128]{2,1,0:T(8,128)(2,1)} %copy-done.10) | copy-start | bytes 1572868
  1098.0 1215.4 %all-reduce.15.cloned.1.call-start = ((), (), s32[]{:S(2)}) async-start(), calls=%async_computation.7 | async-start | bytes 6553600 | tf_op jit(solution)/shard_map/psum | solution.py:232
  2214.4 4.7 copy-start.4
Sparse Core Ops, SparseCore 0:
  11.2 135.5 all-gather.21
  150.1 79.5 all-gather.23
  368.7 25.7 all-gather.19
  396.6 24.7 all-gather.17
  423.6 35.3 reduce-scatter.8
  461.3 35.3 reduce-scatter.6
  500.0 159.5 all-gather.25
  663.0 155.9 all-gather.27
  1098.1 1116.1 reduce-scatter.10
  2216.6 96.7 all-reduce.14
where the time goes:
time: 2340 us; the launch traced here: 2330 us
  waiting for transfers between devices  1390 us (59%)
  blocking collectives  423 us (18%)
  local copies, waits for them, and re-layouts  282 us (12%)
  matrix products  204 us (9%)
    unnamed x11, waiting for transfers between devices  1120 us
    unnamed x1, blocking collectives  327 us
    all_gather x1, waiting for transfers between devices, local(): lax.all_gather(down_weight[None], 'fsdp', axis=0, tiled=True)  143 us
    unnamed x69, local copies, waits for them, and re-layouts  103 us
    all_gather x1, blocking collectives, local(): lax.all_gather(up_bias[None], 'fsdp', axis=0, tiled=True)  95.6 us
    dot_general x4, matrix products, contract_rows(): lax.dot_general(left, right, (((0,), (0,)), ((), ())), preferred_element_...  76.5 us
    psum x1, waiting for transfers between devices, local(): summed = lax.psum(summed, 'seq')  75.3 us
    reshape x1, local copies, waits for them, and re-layouts, in_block(): contract_rows(normed, grad_upper_b).reshape(count, f_share, width)  74.5 us
  transfers between devices with their start and end apart: 10, of which 6 were waited for; matrix products, arithmetic and copies ran while one was open for 9% of the time, Pallas kernels for 0%

commit v1 on v0

v1 whole, which is shorter than its diff:
```python
import math

import jax
import jax.numpy as jnp
from jax import lax
from jax.experimental import pallas as pl
from jax.experimental.pallas import tpu as pltpu
from jax.sharding import Mesh, PartitionSpec as P

D = 2048
H = 32
HD = 64
ROT = 32
FF = 8192
SEQ = 256
SCALE = HD**-0.5
EPS = 1e-5
AXES = ("xh", "z", "y", "core", "xl")
SHARD = ("xh", "z", "y", "core")
PLANE = ("z", "y")
GROUP = ("xh", "core", "xl")
TOKENS = 1024
BF = jnp.bfloat16
F32 = jnp.float32


def swap(value, axis):
    return lax.ppermute(value, axis, [(0, 1), (1, 0)])


def exchange(value, axis):
    me = lax.axis_index(axis)
    other = swap(lax.dynamic_index_in_dim(value, 1 - me, 0, keepdims=False), axis)
    mine = lax.dynamic_index_in_dim(value, me, 0, keepdims=False)
    first = jnp.where(me == 0, mine, other)
    second = jnp.where(me == 0, other, mine)
    return jnp.stack([first, second])


def pair_gather(value, axis):
    me = lax.axis_index(axis)
    other = swap(value, axis)
    return jnp.stack([jnp.where(me == 0, value, other), jnp.where(me == 0, other, value)])


def dot(left, right):
    return jnp.dot(left, right, preferred_element_type=F32)


def dot_rows(left, right):
    return lax.dot_general(left, right, (((0,), (0,)), ((), ())), preferred_element_type=F32)


def dot_cols(left, right):
    return lax.dot_general(left, right, (((1,), (1,)), ((), ())), preferred_element_type=F32)


def attention_body(q_ref, k_ref, v_ref, g_ref, c_ref, s1_ref, s2_ref, row_ref, col_ref,
                   ctx_ref, gq_ref, gk_ref, gv_ref):
    cosine, sin1, sin2 = c_ref[...], s1_ref[...], s2_ref[...]
    width = 4 * HD
    half = ROT // 2

    def turn(value):
        return (
            value * cosine
            - pltpu.roll(value, width - half, 1) * sin1
            + pltpu.roll(value, half, 1) * sin2
        )

    def turn_back(value):
        return (
            value * cosine
            + pltpu.roll(value, width - half, 1) * sin1
            - pltpu.roll(value, half, 1) * sin2
        )

    query = turn(q_ref[...]).astype(BF)
    key = turn(k_ref[...]).astype(BF)
    values = v_ref[...].astype(BF)
    grad = g_ref[...].astype(BF)
    rows = lax.broadcasted_iota(jnp.int32, (SEQ, SEQ), 0)
    cols = lax.broadcasted_iota(jnp.int32, (SEQ, SEQ), 1)
    allowed = (cols <= rows) & (col_ref[...] == row_ref[0])
    contexts, gqs, gks, gvs = [], [], [], []
    for head in range(4):
        part = slice(head * HD, (head + 1) * HD)
        qh, kh, vh, gh = query[:, part], key[:, part], values[:, part], grad[:, part]
        scores = jnp.where(allowed, SCALE * dot_cols(qh, kh), -1e30)
        top = jnp.max(scores, axis=-1, keepdims=True)
        expo = jnp.exp(scores - top)
        probs = expo * (1.0 / jnp.sum(expo, axis=-1, keepdims=True))
        probs_b = probs.astype(BF)
        contexts.append(dot(probs_b, vh))
        grad_probs = dot_cols(gh, vh)
        gvs.append(dot_rows(probs_b, gh))
        inner = jnp.sum(probs * grad_probs, axis=-1, keepdims=True)
        grad_scores = (probs * (grad_probs - inner)).astype(BF)
        gqs.append(SCALE * dot(grad_scores, kh))
        gks.append(SCALE * dot_rows(grad_scores, qh))
    ctx_ref[...] = jnp.concatenate(contexts, axis=1).astype(BF)
    gv_ref[...] = jnp.concatenate(gvs, axis=1).astype(BF)
    gq_ref[...] = turn_back(jnp.concatenate(gqs, axis=1)).astype(BF)
    gk_ref[...] = turn_back(jnp.concatenate(gks, axis=1)).astype(BF)


def attention(query, key, values, grad, cosine, sin1, sin2, segment):
    block = pl.BlockSpec((SEQ, 4 * HD), lambda i: (i, 0))
    out = jax.ShapeDtypeStruct((TOKENS, 4 * HD), BF)
    return pl.pallas_call(
        attention_body,
        grid=(TOKENS // SEQ,),
        in_specs=[block] * 7
        + [
            pl.BlockSpec((1, 1, SEQ), lambda i: (i, 0, 0)),
            pl.BlockSpec((SEQ, 1), lambda i: (i, 0)),
        ],
        out_specs=[block] * 4,
        out_shape=[out] * 4,
        compiler_params=pltpu.CompilerParams(vmem_limit_bytes=40 << 20),
        cost_estimate=pl.CostEstimate(
            flops=7 * 2 * 16 * SEQ * SEQ * HD, bytes_accessed=12 << 20, transcendentals=16 * SEQ * SEQ
        ),
        name="attention",
    )(query, key, values, grad, cosine, sin1, sin2, segment.reshape(4, 1, SEQ), segment.reshape(TOKENS, 1))


def gather_plane(value):
    return lax.all_gather(value, PLANE, axis=0, tiled=False)


def scatter_plane(value):
    return lax.psum_scatter(value, PLANE, scatter_dimension=0, tiled=False)


def gather_group(value):
    return lax.all_gather(value, GROUP, axis=0, tiled=True)


def scatter_group(value):
    return lax.psum_scatter(value, GROUP, scatter_dimension=0, tiled=True)


def owner_order(vector):
    lead = vector.shape[:-1]
    size = vector.shape[-1] // 32
    return jnp.swapaxes(vector.reshape(*lead, 2, 16, size), -3, -2).reshape(*lead, -1)


def plain_order(vector):
    lead = vector.shape[:-1]
    size = vector.shape[-1] // 32
    return jnp.swapaxes(vector.reshape(*lead, 16, 2, size), -3, -2).reshape(*lead, -1)


def local(
    hidden_in, norm_gain, norm_shift, qkv_weight, qkv_bias, proj_weight, proj_bias,
    up_weight, up_bias, down_weight, down_bias, segment_ids, positions, cotangent,
):
    xh, core, xl = lax.axis_index("xh"), lax.axis_index("core"), lax.axis_index("xl")
    hidden_own = hidden_in.reshape(128, D)
    cot_own = cotangent.reshape(128, D)

    hid = gather_group(owner_order(hidden_own))
    marks = jnp.stack(
        [positions.reshape(128), lax.dynamic_slice_in_dim(segment_ids.reshape(SEQ), xl * 128, 128)]
    )
    marks = pair_gather(pair_gather(pair_gather(marks, "xl"), "core"), "xh")
    marks = marks.transpose(3, 0, 1, 2, 4).reshape(2, TOKENS)
    position_all, segment_all = marks[0], marks[1]
    cot = gather_group(cot_own)

    qkv_parts = lax.dynamic_index_in_dim(
        qkv_weight.reshape(32, 3, 2, 2, 2, 256), xl, 4, keepdims=False
    ).transpose(2, 3, 1, 0, 4).reshape(2, 2, 96, 256)
    small = jnp.concatenate([norm_gain, norm_shift, proj_bias, down_bias, qkv_bias, up_bias])
    small = jnp.pad(small, (0, 16 * 256 - 352)).reshape(1, 1, 16, 256)
    pre2 = jnp.concatenate([qkv_parts, jnp.broadcast_to(small, (2, 2, 16, 256))], axis=2)
    pre2 = exchange(pre2, "xh")
    pre2 = exchange(pre2.swapaxes(0, 1), "core").swapaxes(0, 1)
    proj_part = lax.dynamic_slice_in_dim(proj_weight, xl * 16, 16, 0)
    proj_part = proj_part.reshape(16, 8, 256).swapaxes(0, 1).reshape(128, 256)
    pack2 = gather_plane(jnp.concatenate([pre2.reshape(448, 256), proj_part], axis=0))

    pre1 = lax.dynamic_index_in_dim(
        up_weight.reshape(32, 2, 16, 2, 2, 64), xl, 4, keepdims=False
    ).transpose(1, 3, 0, 2, 4).reshape(2, 2, 32, 1024)
    pre1 = exchange(pre1, "xh")
    pre1 = exchange(pre1.swapaxes(0, 1), "core").swapaxes(0, 1)
    down_part = lax.dynamic_slice_in_dim(down_weight, xl * 64, 64, 0)
    pack1 = gather_plane(
        jnp.concatenate([pre1.reshape(128, 1024), down_part[:, :1024], down_part[:, 1024:]], axis=0)
    )

    columns = pack2[:, :448].reshape(16, 4, 112, 256)
    q_w = columns[:, :, :32].reshape(D, 256)
    k_w = columns[:, :, 32:64].reshape(D, 256)
    v_w = columns[:, :, 64:96].reshape(D, 256)
    small = columns[:, :, 96:98].reshape(16, 2, 2, 512).astype(F32)
    gain = small[..., :32].reshape(D)
    shift = small[..., 32:64].reshape(D)
    out_bias = plain_order((small[..., 64:96] + small[..., 96:128]).reshape(D))
    qkv_b = plain_order(small[..., 128:224].reshape(3 * D)).reshape(3, 2, 2, 2, 256)
    qkv_b = qkv_b[:, xh, core, xl]
    up_b = lax.dynamic_slice_in_dim(small[:, xh, core, 224:352], xl * 64, 64, 1).reshape(1024)
    proj_rows = pack2[:, 448:].reshape(2, 2, 4, 8, 16, 256)
    proj_rows = exchange(proj_rows, "core")
    proj_rows = exchange(proj_rows.swapaxes(0, 1), "xl")
    proj_w = proj_rows.transpose(2, 1, 0, 4, 3, 5).reshape(256, D)
    up_w = pack1[:, :128].reshape(D, 1024)
    down_w = jnp.concatenate(
        [pack1[:, 128:192].reshape(1024, 1024), pack1[:, 192:].reshape(1024, 1024)], axis=1
    )

    lane = jnp.arange(128) % HD
    freqs = 10000.0 ** (-(lane % 16).astype(F32) * (2.0 / ROT))
    angles = position_all.astype(F32)[:, None] * freqs
    cosine = jnp.where(lane < ROT, jnp.cos(angles), 1.0)
    sine = jnp.sin(angles)
    sin1 = jnp.where(lane < 16, sine, 0.0)
    sin2 = jnp.where((lane >= 16) & (lane < ROT), sine, 0.0)
    cosine, sin1, sin2 = (jnp.concatenate([t, t], axis=1) for t in (cosine, sin1, sin2))

    hid_f = hid.astype(F32)
    mean = jnp.mean(hid_f, axis=-1, keepdims=True)
    centered = hid_f - mean
    rstd = lax.rsqrt(jnp.mean(centered * centered, axis=-1, keepdims=True) + EPS)
    normal = centered * rstd
    normed = (normal * gain + shift).astype(BF)
    query = dot(normed, q_w) + qkv_b[0]
    key = dot(normed, k_w) + qkv_b[1]
    values = dot(normed, v_w) + qkv_b[2]
    grad_context = dot_cols(cot, proj_w).astype(BF)
    context, grad_q, grad_k, grad_v = attention(
        query, key, values, grad_context, cosine, sin1, sin2, segment_all
    )
    upper = dot(normed, up_w) + up_b
    active, gelu_pull = jax.vjp(lambda value: jax.nn.gelu(value, approximate=True), upper)
    active = active.astype(BF)
    grad_upper = gelu_pull(dot_cols(cot, down_w))[0].astype(BF)
    branch = dot(context, proj_w) + dot(active, down_w)
    branch = scatter_group(branch.astype(BF))
    block_out = hidden_own.astype(F32) + branch.astype(F32) + out_bias
    block_out = block_out.astype(BF).reshape(1, 128, D)

    grad_normed = (
        dot_cols(grad_q, q_w) + dot_cols(grad_k, k_w) + dot_cols(grad_v, v_w) + dot_cols(grad_upper, up_w)
    )
    gain_sum = jnp.sum(grad_normed * normal, axis=0)
    shift_sum = jnp.sum(grad_normed, axis=0)
    out_sum = owner_order(jnp.sum(cot_own.astype(F32), axis=0))
    grad_own = scatter_group(grad_normed.astype(BF)).astype(F32)

    own = owner_order(hidden_own).astype(F32)
    mean = jnp.mean(own, axis=-1, keepdims=True)
    centered = own - mean
    rstd = lax.rsqrt(jnp.mean(centered * centered, axis=-1, keepdims=True) + EPS)
    normal_own = centered * rstd
    scaled = grad_own * gain
    inner = jnp.mean(scaled * normal_own, axis=-1, keepdims=True)
    pulled = (scaled - jnp.mean(scaled, axis=-1, keepdims=True) - normal_own * inner) * rstd
    grad_hidden = (cot_own.astype(F32) + plain_order(pulled)).reshape(1, 128, D)

    grad_proj = dot_rows(context, cot).astype(BF)
    grad_down = dot_rows(active, cot).astype(BF)
    grad_up = dot_rows(normed, grad_upper).astype(BF)
    grad_qw, grad_kw, grad_vw = (
        dot_rows(normed, g).astype(BF).reshape(16, 4, 32, 256) for g in (grad_q, grad_k, grad_v)
    )
    bias_sums = [jnp.sum(g.astype(F32), axis=0) for g in (grad_q, grad_k, grad_v)]
    qkv_sum = jnp.zeros((3, 2, 2, 2, 256), F32)
    qkv_sum = lax.dynamic_update_slice(
        qkv_sum, jnp.stack(bias_sums).reshape(3, 1, 1, 1, 256), (0, xh, core, xl, 0)
    )
    qkv_sum = owner_order(qkv_sum.reshape(3 * D)).reshape(16, 4, 96)
    up_sum = jnp.zeros((16, 2, 2, 2, 64), F32)
    up_sum = lax.dynamic_update_slice(
        up_sum, jnp.sum(grad_upper.astype(F32), axis=0).reshape(16, 1, 1, 1, 64), (0, xh, core, xl, 0)
    ).reshape(16, 4, 128)
    sums = jnp.concatenate(
        [s.reshape(16, 4, 32) for s in (gain_sum, shift_sum, out_sum)] + [qkv_sum, up_sum], axis=2
    )
    sums = jnp.pad(sums, ((0, 0), (0, 0), (0, 16 * 256 - 320))).reshape(16, 4, 16, 256).astype(BF)
    cols2 = jnp.concatenate([grad_qw, grad_kw, grad_vw, sums], axis=2).reshape(16, 448, 256)
    grad_proj = grad_proj.reshape(4, 2, 2, 16, 8, 256).transpose(1, 2, 0, 4, 3, 5)
    grad_proj = exchange(grad_proj, "core")
    grad_proj = exchange(grad_proj.swapaxes(0, 1), "xl").swapaxes(0, 1).reshape(16, 128, 256)
    back2 = scatter_plane(jnp.concatenate([cols2, grad_proj], axis=1))
    back1 = scatter_plane(
        jnp.concatenate(
            [
                grad_up.reshape(16, 128, 1024),
                grad_down[:, :1024].reshape(16, 64, 1024),
                grad_down[:, 1024:].reshape(16, 64, 1024),
            ],
            axis=1,
        )
    )

    def to_owner(value):
        value = exchange(value.swapaxes(0, 1), "core")
        value = exchange(value.swapaxes(0, 1), "xh")
        return pair_gather(value, "xl")

    own1 = to_owner(back1[:128].reshape(2, 2, 32, 1024))
    grad_up = own1.reshape(2, 2, 2, 32, 16, 64).transpose(3, 1, 4, 2, 0, 5).reshape(32, FF)
    own2 = to_owner(back2[:448].reshape(2, 2, 112, 256))
    grad_qkv = own2[:, :, :, :96].reshape(2, 2, 2, 3, 32, 256).transpose(4, 3, 1, 2, 0, 5)
    grad_qkv = grad_qkv.reshape(32, 3 * D)
    sums = jnp.sum(own2[:, :, :, 96:98].astype(F32), axis=(0, 1, 2)).reshape(512)
    grad_down = pair_gather(
        jnp.concatenate([back1[128:192], back1[192:]], axis=1), "xl"
    ).reshape(128, D)
    grad_proj = pair_gather(
        back2[448:].reshape(8, 16, 256).swapaxes(0, 1).reshape(16, D), "xl"
    ).reshape(32, D)
    return (
        block_out,
        grad_hidden,
        sums[:32],
        sums[32:64],
        grad_qkv.astype(F32),
        sums[96:192],
        grad_proj.astype(F32),
        sums[64:96],
        grad_up.astype(F32),
        sums[192:320],
        grad_down.astype(F32),
        sums[64:96],
    )


def solution(mesh):
    cut = Mesh(mesh.devices.reshape(2, 4, 4, 2, 2), AXES)
    row, vec = P(SHARD, None), P(SHARD)
    tok = P(SHARD, "xl", None)
    return jax.shard_map(
        local,
        mesh=cut,
        in_specs=(
            tok, vec, vec, row, vec, row, vec, row, vec, row, vec, row, P(SHARD, "xl"), tok,
        ),
        out_specs=(tok, tok, vec, vec, row, vec, row, vec, row, vec, row, vec),
        check_vma=False,
    )
```

time: 2340 us -> 741 us (0.32)
  waiting for transfers between devices: 1390 us -> 489 us
  blocking collectives: 423 us -> 0 us
  local copies, waits for them, and re-layouts: 282 us -> 64.6 us
  matrix products: 204 us -> 88.2 us
  starting transfers between devices: 0.86 us -> 25.8 us
    unnamed x11 -> x8, waiting for transfers between devices: 1120 us -> 188 us
    unnamed x1 -> x0, blocking collectives: 327 us -> none
    reshape x8 -> x10, local copies, waits for them, and re-layouts: 131 us -> 4.18 us  [the longest x1 1.28 us: local(): qkv_weight.reshape(32, 3, 2, 2, 2, 256)]
    dot_general x18, matrix products: 204 us -> 88.2 us  [the longest x6 39.4 us: dot_cols(): lax.dot_general(left, right, (((1,), (1,)), ((), ())), preferred_element_...]
    all_gather x1 -> x0, blocking collectives: 95.6 us -> none  [local(): lax.all_gather(up_bias[None], 'fsdp', axis=0, tiled=True)]
    unnamed x69 -> x117, local copies, waits for them, and re-layouts: 103 us -> 20.8 us
    psum x1 -> x0, waiting for transfers between devices: 75.3 us -> none  [local(): summed = lax.psum(summed, 'seq')]
    reduce_scatter x2, waiting for transfers between devices: 0.04 us -> 73 us  [scatter_group(): return lax.psum_scatter(value, GROUP, scatter_dimension=0, tiled=True)]
  transfers between devices with their start and end apart: 10 -> 26, of which waited for: 6 -> 20; matrix products, arithmetic and copies ran while one was open for 9% -> 17% of each run, Pallas kernels for 0% -> 2%
where the time goes in v1:
time: 741 us; the launch traced here: 729 us
  waiting for transfers between devices  489 us (66%)
  matrix products  88.2 us (12%)
  local copies, waits for them, and re-layouts  64.6 us (9%)
  other arithmetic  31.2 us (4%)
  starting transfers between devices  25.8 us (3%)
  between operations  15.6 us (2%)
  Pallas kernels  14.9 us (2%)
    unnamed x8, waiting for transfers between devices  188 us
    all_gather x2, waiting for transfers between devices, gather_plane(): return lax.all_gather(value, PLANE, axis=0, tiled=False)  101 us
    reduce_scatter x2, waiting for transfers between devices, scatter_group(): return lax.psum_scatter(value, GROUP, scatter_dimension=0, tiled=True)  73 us
    all_gather x2, waiting for transfers between devices, gather_group(): return lax.all_gather(value, GROUP, axis=0, tiled=True)  68.6 us
    ppermute x19, waiting for transfers between devices, swap(): return lax.ppermute(value, axis, [(0, 1), (1, 0)])  58.5 us
    dot_general x6, matrix products, dot_cols(): lax.dot_general(left, right, (((1,), (1,)), ((), ())), preferred_element_...  39.4 us
    dot_general x6, matrix products, dot(): return jnp.dot(left, right, preferred_element_type=F32)  25.8 us
    ppermute x19, starting transfers between devices, swap(): return lax.ppermute(value, axis, [(0, 1), (1, 0)])  25.4 us
  transfers between devices with their start and end apart: 26, of which 20 were waited for; matrix products, arithmetic and copies ran while one was open for 17% of the time, Pallas kernels for 2%

profile of v1, /device:TPU:1, one launch (start us, length us, event | category | flops | bytes accessed | tf_op | source)
XLA Modules:
  0.0 729.5 jit_solution(12718352388392261302)
XLA Ops:
  9.7 4.1 concatenate.41
  15.7 3.7 collective-permute-start
  19.3 2.2 collective-permute-done
  29.1 3.2 collective-permute-start.7
  32.4 6.6 collective-permute-done.7
  42.7 2.3 collective-permute-done.4
  47.1 2.3 collective-permute-start.6
  54.3 31.4 %all-gather.8.cloned.1.call-done = bf16[1024,2048]{1,0:T(8,128)(2,1)} async-done(((bf16[128,2048]{1,0:T(8,128)(2,1)}), bf16[1024,2048]{1,0:T(8,128)(2,1)}) %all-gather.8.cloned.1.call-update) | async-done | bytes 4194320 | tf_op jit(solution)/shard_map/all_gather | solution.py:137
  85.7 3.0 convert_reduce_fusion
  90.4 53.8 %all-gather.10.cloned.1.call-done = bf16[9216,256]{1,0:T(8,128)(2,1)} async-done(((bf16[576,256]{1,0:T(8,128)(2,1)}), bf16[9216,256]{1,0:T(8,128)(2,1)}) %all-gather.10.cloned.1.call-update) | async-done | bytes 4718608 | tf_op jit(solution)/shard_map/all_gather | solution.py:129
  144.2 2.3 slice.165
  146.5 2.4 slice.157
  153.8 3.4 fusion.97
  159.1 2.3 convolution_add_fusion.v_ref
  164.4 2.2 convolution_add_fusion.1.k_ref
  166.8 4.8 convolution_add_fusion.2.q_ref
  171.6 14.4 %collective-permute-done.3 = bf16[2,4,8,16,256]{4,3,2,1,0:T(8,128)(2,1)} collective-permute-done((bf16[2,4,8,16,256]{4,3,2,1,0:T(8,128)(2,1)}, bf16[2,4,8,16,256]{4,3,2,1,0:T(8,128)(2,1)}, u32[]{:S(2)}, u32[]{:S(2)}) %collective-permute-start.3) | collective-permute-done | bytes 524320 | tf_op jit(solution)/shard_map/ppermute | solution.py:28
  188.9 37.1 %all-gather.12.cloned.1.call-done = bf16[1,1024,2048]{2,1,0:T(8,128)(2,1)} async-done(((bf16[1,128,2048]{2,1,0:T(8,128)(2,1)}), bf16[1,1024,2048]{2,1,0:T(8,128)(2,1)}) %all-gather.12.cloned.1.call-update) | async-done | bytes 4194320 | tf_op jit(solution)/shard_map/all_gather | solution.py:137
  226.1 3.9 fusion.38.g_ref
  230.1 14.9 %attention.1 = (bf16[1024,256]{1,0:T(8,128)(2,1)S(1)}, bf16[1024,256]{1,0:T(8,128)(2,1)S(1)}, bf16[1024,256]{1,0:T(8,128)(2,1)S(1)}, bf16[1024,256]{1,0:T(8,128)(2,1)S(1)}) custom-call(f32[1024,256]{1,0:T(8,128)S(1)} %copy-done.11, f32[1024,256]{1,0:T(8,128)S(1)} %copy-done.10, f32[1024,256]{1,0:T(8,128)S(1)} %copy-done.9, ...), custom_call_target="tpu_custom_call" | custom-call | flops 939524096 | bytes 12582912 | tf_op jit(solution)/shard_map/attention/pallas_call | solution.py:110
  245.0 4.6 fusion.103
  249.7 4.6 fusion.102
  254.2 47.0 %all-gather.14.cloned.1.call-done = bf16[4096,1024]{1,0:T(8,128)(2,1)} async-done(((bf16[256,1024]{1,0:T(8,128)(2,1)}), bf16[4096,1024]{1,0:T(8,128)(2,1)}) %all-gather.14.cloned.1.call-update) | async-done | bytes 8388624 | tf_op jit(solution)/shard_map/all_gather | solution.py:129
  301.3 2.8 slice.168
  306.6 2.8 copy-done.28
  309.4 4.5 fusion.101
  313.9 7.5 %convert_reduce_fusion.1 = (bf16[1024]{0:T(1024)(128)(2,1)S(1)}, bf16[1024,1024]{1,0:T(8,128)(2,1)S(1)}) fusion(f32[1024,1024]{1,0:T(8,128)S(1)} %fusion.101, f32[1024]{0:T(1024)S(1)} %add.243, bf16[1,1024,2048]{2,1,0:T(8,128)(2,1)S(1)} %copy-done.45, bf16[1024,1024]{1,0:T(8,128)(2,1)S(1)} %bitcast.399, bf16[1024,1024]{1,0:T(8,128)(2,1)S(1)} %bitcast.397), kind=kOutput, calls=%fused_computation.37 | convolution fusion | flops 4327472128 | bytes 14686208 | tf_op jit(solution)/shard_map/dot_general | solution.py:55
  321.5 6.9 fusion.104
  328.4 12.0 %fusion.94 = (bf16[2048]{0:T(1024)(128)(2,1)S(1)}, bf16[2048]{0:T(1024)(128)(2,1)S(1)}, bf16[1024,2048]{1,0:T(8,128)(2,1)}) fusion(f32[1024]{0:T(1024)S(1)} %add_rsqrt_fusion, f32[1024]{0:T(1024)S(1)} %broadcast_multiply_fusion, bf16[1024,2048]{1,0:T(8,128)(2,1)S(1)} %copy-done.16, f32[1024,2048]{1,0:T(8,128)} %fusion.104, ...), kind=kOutput, calls=%fused_computation.249 | convolution fusion | flops 1094709248 | bytes 35143680 | tf_op jit(solution)/shard_map/dot_general | solution.py:55
  340.4 8.5 %fusion.31 = f32[1024,2048]{1,0:T(8,128)S(1)} fusion(bf16[1024,1024]{1,0:T(8,128)(2,1)} %bitcast.400, bf16[1024,1024]{1,0:T(8,128)(2,1)} %bitcast.398, f32[1024,1024]{1,0:T(8,128)} %copy-done.49, f32[1024]{0:T(1024)S(1)} %add.243), kind=kOutput, calls=%fused_computation.42 | convolution fusion | flops 4313841664 | bytes 16781312 | tf_op jit(solution)/shard_map/dot_general | solution.py:47
  349.0 3.5 add_convert_fusion
  353.7 3.5 fusion.32
  359.7 2.4 convolution_convert_fusion.3
  362.2 2.4 convolution_convert_fusion.2
  366.4 4.5 convolution_convert_fusion.1
  371.0 16.6 %collective-permute-done.10 = bf16[2,4,8,16,256]{4,3,2,1,0:T(8,128)(2,1)S(1)} collective-permute-done((bf16[2,4,8,16,256]{4,3,2,1,0:T(8,128)(2,1)S(1)}, bf16[2,4,8,16,256]{4,3,2,1,0:T(8,128)(2,1)S(1)}, u32[]{:S(2)}, u32[]{:S(2)}) %collective-permute-start.10) | collective-permute-done | bytes 524320 | tf_op jit(solution)/shard_map/ppermute | solution.py:28
  391.5 2.7 pad_maximum_fusion.1
  396.7 5.4 fusion.26
  405.0 4.9 convolution_convert_fusion
  410.0 3.8 pad_maximum_fusion
  416.2 5.0 reduce-scatter.5.cloned.1.call-done
  427.0 68.0 %reduce-scatter.3.cloned.1.call-done = bf16[128,2048]{1,0:T(8,128)(2,1)} async-done(((bf16[1024,2048]{1,0:T(8,128)(2,1)}), bf16[128,2048]{1,0:T(8,128)(2,1)}) %reduce-scatter.3.cloned.1.call-update) | async-done | bytes 524304 | tf_op jit(solution)/shard_map/reduce_scatter | solution.py:141
  497.0 187.5 %all-reduce.7.cloned.1.call-done = (bf16[16,576,256]{2,1,0:T(8,128)(2,1)}, bf16[16,256,1024]{2,1,0:T(8,128)(2,1)}) async-done(((bf16[16,576,256]{2,1,0:T(8,128)(2,1)}, bf16[16,256,1024]{2,1,0:T(8,128)(2,1)}), (bf16[16,576,256]{2,1,0:T(8,128)(2,1)}, bf16[16,256,1024]{2,1,0:T(8,128)(2,1)})) %all-reduce.7.cloned.1.call-update) | async-done | bytes 13107216
  694.6 2.8 collective-permute-start.12
  697.8 7.0 collective-permute-done.12
  705.3 2.4 collective-permute-done.16
  713.9 2.4 collective-permute-done.17
  719.0 2.9 reshape.361
  (304 shorter events, 84.9 us)
Async XLA Ops:
  7.2 16.5 %copy-start = (bf16[32,2048]{1,0:T(8,128)(2,1)S(1)}, bf16[32,2048]{1,0:T(8,128)(2,1)}, u32[]{:S(2)}) copy-start(bf16[32,2048]{1,0:T(8,128)(2,1)} %param.19) | copy-start | bytes 393220
  7.2 78.5 %all-gather.8.cloned.1.call-start = ((), (), s32[]{:S(2)}) async-start(), calls=%async_computation.2 | async-start | bytes 4718592 | tf_op jit(solution)/shard_map/all_gather | solution.py:137
  8.6 16.9 %copy-start.20 = (bf16[1,128,2048]{1,2,0:T(8,128)(2,1)}, bf16[1,128,2048]{1,2,0:T(8,128)(2,1)S(1)}, u32[]{:S(2)}) copy-start(bf16[1,128,2048]{1,2,0:T(8,128)(2,1)S(1)} %copy.119) | copy-start | bytes 1572868
  8.6 17.6 %copy-start.41 = (bf16[32,8192]{1,0:T(8,128)(2,1)S(1)}, bf16[32,8192]{1,0:T(8,128)(2,1)}, u32[]{:S(2)}) copy-start(bf16[32,8192]{1,0:T(8,128)(2,1)} %param.21) | copy-start | bytes 1572868
  9.7 134.6 %all-gather.10.cloned.1.call-start = ((), (), s32[]{:S(2)}) async-start(), calls=%async_computation.5 | async-start | bytes 5013504 | tf_op jit(solution)/shard_map/all_gather | solution.py:129
  15.7 5.8 collective-permute-start
  21.6 3.0 collective-permute-start.1
  24.7 15.5 %copy-start.42 = (bf16[128,2048]{1,0:T(8,128)(2,1)S(1)}, bf16[128,2048]{1,0:T(8,128)(2,1)}, u32[]{:S(2)}) copy-start(bf16[128,2048]{1,0:T(8,128)(2,1)} %param.23) | copy-start | bytes 1572868
  25.5 200.6 %all-gather.12.cloned.1.call-start = ((), (), s32[]{:S(2)}) async-start(), calls=%async_computation.6 | async-start | bytes 4718592 | tf_op jit(solution)/shard_map/all_gather | solution.py:137
  26.2 275.0 %all-gather.14.cloned.1.call-start = ((), (), s32[]{:S(2)}) async-start(), calls=%async_computation.7 | async-start | bytes 8912896 | tf_op jit(solution)/shard_map/all_gather | solution.py:129
  27.4 14.7 %copy-start.47 = (s32[1,256]{1,0:T(1,128)S(1)}, s32[1,256]{1,0:T(1,128)}, u32[]{:S(2)}) copy-start(s32[1,256]{1,0:T(1,128)} %param.25) | copy-start | bytes 3076
  27.4 14.7 %copy-start.43 = (s32[1,128]{1,0:T(1,128)S(1)}, s32[1,128]{1,0:T(1,128)}, u32[]{:S(2)}) copy-start(s32[1,128]{1,0:T(1,128)} %param.26) | copy-start | bytes 1540
  29.1 9.8 %collective-permute-start.7 = (bf16[2,32,1024]{2,1,0:T(8,128)(2,1)S(1)}, bf16[2,32,1024]{2,1,0:T(8,128)(2,1)S(1)}, u32[]{:S(2)}, u32[]{:S(2)}) collective-permute-start(bf16[2,32,1024]{2,1,0:T(8,128)(2,1)S(1)} %dynamic-slice_bitcast_fusion.4), channel_id=1, source_target_pairs={{0,64},{64,0},{1,65},{65,1},{2,66},{66,2},{3,67},{67,3},{4,68},{68... | collective-permute-start | bytes 393224 | tf_op jit(solution)/shard_map/ppermute | solution.py:28
  39.0 2.1 collective-permute-start.8
  42.1 379.1 %reduce-scatter.5.cloned.1.call-start = ((), (), s32[]{:S(2)}) async-start(), calls=%async_computation.4 | async-start | bytes 4718592 | tf_op jit(solution)/shard_map/reduce_scatter | solution.py:141
  42.2 2.9 collective-permute-start.4
  45.1 2.0 collective-permute-start.5
  47.1 4.0 collective-permute-start.6
  152.7 8.6 %collective-permute-start.2 = (bf16[2,4,8,16,256]{4,3,2,1,0:T(8,128)(2,1)S(1)}, bf16[2,4,8,16,256]{4,3,2,1,0:T(8,128)(2,1)S(1)}, u32[]{:S(2)}, u32[]{:S(2)}) collective-permute-start(bf16[2,4,8,16,256]{4,3,2,1,0:T(8,128)(2,1)S(1)} %dynamic-slice_bitcast_fusion), channel_id=1, source_target_pairs={{0,2},{2,0},{1,3},{3,1},{4,6},{6,4},{5,7},{7,5},{8,10},{10,8},{9,1... | collective-permute-start | bytes 1572872 | tf_op jit(solution)/shard_map/ppermute | solution.py:28
  157.2 7.2 copy-start.35
  163.1 22.8 %collective-permute-start.3 = (bf16[2,4,8,16,256]{4,3,2,1,0:T(8,128)(2,1)}, bf16[2,4,8,16,256]{4,3,2,1,0:T(8,128)(2,1)}, u32[]{:S(2)}, u32[]{:S(2)}) collective-permute-start(bf16[2,4,8,16,256]{4,3,2,1,0:T(8,128)(2,1)} %fusion.55), channel_id=1, source_target_pairs={{0,1},{1,0},{2,3},{3,2},{4,5},{5,4},{6,7},{7,6},{8,9},{9,8},{10,11... | collective-permute-start | bytes 1572872 | tf_op jit(solution)/shard_map/ppermute | solution.py:28
  166.8 19.2 %copy-start.24 = (bf16[1,2,4,8,16,256]{5,4,3,2,1,0:T(8,128)(2,1)S(1)}, bf16[1,2,4,8,16,256]{5,4,3,2,1,0:T(8,128)(2,1)}, u32[]{:S(2)}) copy-start(bf16[1,2,4,8,16,256]{5,4,3,2,1,0:T(8,128)(2,1)} %copy-done.23) | copy-start | bytes 1572868
  166.8 19.2 %copy-start.26 = (bf16[1,2,4,8,16,256]{5,4,3,2,1,0:T(8,128)(2,1)S(1)}, bf16[1,2,4,8,16,256]{5,4,3,2,1,0:T(8,128)(2,1)}, u32[]{:S(2)}) copy-start(bf16[1,2,4,8,16,256]{5,4,3,2,1,0:T(8,128)(2,1)} %copy-done.25) | copy-start | bytes 1572868
  230.0 15.0 %copy-start.36 = (bf16[16,4,32,256]{3,2,1,0:T(8,128)(2,1)S(1)}, bf16[16,4,32,256]{3,2,1,0:T(8,128)(2,1)}, u32[]{:S(2)}) copy-start(bf16[16,4,32,256]{3,2,1,0:T(8,128)(2,1)} %copy-done.35) | copy-start | bytes 3145732
  306.6 7.3 %copy-start.39 = (bf16[16,64,1024]{2,1,0:T(8,128)(2,1)}, bf16[16,64,1024]{2,1,0:T(8,128)(2,1)S(1)}, u32[]{:S(2)}) copy-start(bf16[16,64,1024]{2,1,0:T(8,128)(2,1)S(1)} %get-tuple-element.77) | copy-start | bytes 6291460
  306.6 7.3 %copy-start.40 = (bf16[16,64,1024]{2,1,0:T(8,128)(2,1)}, bf16[16,64,1024]{2,1,0:T(8,128)(2,1)S(1)}, u32[]{:S(2)}) copy-start(bf16[16,64,1024]{2,1,0:T(8,128)(2,1)S(1)} %get-tuple-element.78) | copy-start | bytes 6291460
  313.9 7.5 %copy-start.49 = (f32[1024,1024]{1,0:T(8,128)}, f32[1024,1024]{1,0:T(8,128)S(1)}, u32[]{:S(2)}) copy-start(f32[1024,1024]{1,0:T(8,128)S(1)} %fusion.101) | copy-start | bytes 12582916
  321.4 6.9 copy-start.51
  321.4 6.9 copy-start.7
  321.5 6.9 copy-start.16
  321.5 6.9 copy-start.33
  340.4 8.6 %copy-start.13 = (bf16[1024,256]{1,0:T(8,128)(2,1)S(1)}, bf16[1024,256]{1,0:T(8,128)(2,1)}, u32[]{:S(2)}) copy-start(bf16[1024,256]{1,0:T(8,128)(2,1)} %copy-done.12) | copy-start | bytes 1572868
  340.4 8.6 %copy-start.31 = (bf16[32,8,8,256]{3,1,2,0:T(8,128)(2,1)S(1)}, bf16[32,8,8,256]{3,1,2,0:T(8,128)(2,1)}, u32[]{:S(2)}) copy-start(bf16[32,8,8,256]{3,1,2,0:T(8,128)(2,1)} %copy.162) | copy-start | bytes 3145732
  340.4 154.6 %reduce-scatter.3.cloned.1.call-start = ((), (), s32[]{:S(2)}) async-start(), calls=%async_computation.3 | async-start | bytes 4718592 | tf_op jit(solution)/shard_map/reduce_scatter | solution.py:141
  352.4 332.1 %all-reduce.7.cloned.1.call-start = ((), (), s32[]{:S(2)}) async-start(), calls=%async_computation.8 | async-start | bytes 26214400
  357.7 6.8 collective-permute-start.9
  364.8 22.7 %collective-permute-start.10 = (bf16[2,4,8,16,256]{4,3,2,1,0:T(8,128)(2,1)S(1)}, bf16[2,4,8,16,256]{4,3,2,1,0:T(8,128)(2,1)S(1)}, u32[]{:S(2)}, u32[]{:S(2)}) collective-permute-start(bf16[2,4,8,16,256]{4,3,2,1,0:T(8,128)(2,1)S(1)} %fusion.51), channel_id=1, source_target_pairs={{0,1},{1,0},{2,3},{3,2},{4,5},{5,4},{6,7},{7,6},{8,9},{9,8},{10,11... | collective-permute-start | bytes 1572872 | tf_op jit(solution)/shard_map/ppermute | solution.py:28
  413.8 7.4 %copy-start.18 = (bf16[128,2048]{1,0:T(8,128)(2,1)S(1)}, bf16[128,2048]{1,0:T(8,128)(2,1)}, u32[]{:S(2)}) copy-start(bf16[128,2048]{1,0:T(8,128)(2,1)} %copy.121) | copy-start | bytes 1572868
  424.1 70.9 %copy-start.38 = (bf16[1,128,2048]{2,1,0:T(8,128)(2,1)S(1)}, bf16[1,128,2048]{2,1,0:T(8,128)(2,1)}, u32[]{:S(2)}) copy-start(bf16[1,128,2048]{2,1,0:T(8,128)(2,1)} %param.14) | copy-start | bytes 1572868
  687.6 6.1 collective-permute-start.14
  688.9 5.6 collective-permute-start.11
  691.6 5.8 collective-permute-start.15
  693.4 14.8 %collective-permute-start.18 = (bf16[64,2048]{1,0:T(8,128)(2,1)S(1)}, bf16[64,2048]{1,0:T(8,128)(2,1)S(1)}, u32[]{:S(2)}, u32[]{:S(2)}) collective-permute-start(bf16[64,2048]{1,0:T(8,128)(2,1)S(1)} %pad_maximum_fusion.15), channel_id=1, source_target_pairs={{0,1},{1,0},{2,3},{3,2},{4,5},{5,4},{6,7},{7,6},{8,9},{9,8},{10,11... | collective-permute-start | bytes 786440 | tf_op jit(solution)/shard_map/ppermute | solution.py:28
  694.6 10.2 %collective-permute-start.12 = (bf16[2,112,256]{2,1,0:T(8,128)(2,1)S(1)}, bf16[2,112,256]{2,1,0:T(8,128)(2,1)S(1)}, u32[]{:S(2)}, u32[]{:S(2)}) collective-permute-start(bf16[2,112,256]{2,1,0:T(8,128)(2,1)S(1)} %fusion.77), channel_id=1, source_target_pairs={{0,64},{64,0},{1,65},{65,1},{2,66},{66,2},{3,67},{67,3},{4,68},{68... | collective-permute-start | bytes 344072 | tf_op jit(solution)/shard_map/ppermute | solution.py:28
  697.4 10.2 %collective-permute-start.16 = (bf16[2,32,1024]{2,1,0:T(8,128)(2,1)S(1)}, bf16[2,32,1024]{2,1,0:T(8,128)(2,1)S(1)}, u32[]{:S(2)}, u32[]{:S(2)}) collective-permute-start(bf16[2,32,1024]{2,1,0:T(8,128)(2,1)S(1)} %fusion.61), channel_id=1, source_target_pairs={{0,64},{64,0},{1,65},{65,1},{2,66},{66,2},{3,67},{67,3},{4,68},{68... | collective-permute-start | bytes 393224 | tf_op jit(solution)/shard_map/ppermute | solution.py:28
  704.9 5.0 collective-permute-start.13
  707.7 8.6 %collective-permute-start.17 = (bf16[2,2,32,1024]{3,2,1,0:T(8,128)(2,1)S(1)}, bf16[2,2,32,1024]{3,2,1,0:T(8,128)(2,1)S(1)}, u32[]{:S(2)}, u32[]{:S(2)}) collective-permute-start(bf16[2,2,32,1024]{3,2,1,0:T(8,128)(2,1)S(1)} %pad_maximum_fusion.14), channel_id=1, source_target_pairs={{0,1},{1,0},{2,3},{3,2},{4,5},{5,4},{6,7},{7,6},{8,9},{9,8},{10,11... | collective-permute-start | bytes 786440 | tf_op jit(solution)/shard_map/ppermute | solution.py:28
  710.5 11.4 %copy-start.44 = (f32[32]{0:T(128)}, f32[32]{0:T(128)S(1)}, u32[]{:S(2)}) copy-start(f32[32]{0:T(128)S(1)} %get-tuple-element.169) | copy-start | bytes 388
  (31 other events, 103.7 us)
Sparse Core Ops, SparseCore 0:
  10.2 75.4 all-gather.7
  88.4 55.7 all-gather.9
  145.9 80.1 all-gather.11
  228.6 72.5 all-gather.13
  340.5 80.6 reduce-scatter.4
  423.4 71.5 reduce-scatter.2
  498.9 185.5 all-reduce.6

commit v2 on v1

v2 whole, which is shorter than its diff:
```python
import math

import jax
import jax.numpy as jnp
from jax import lax
from jax.experimental import pallas as pl
from jax.experimental.pallas import tpu as pltpu
from jax.sharding import Mesh, PartitionSpec as P

D = 2048
H = 32
HD = 64
ROT = 32
FF = 8192
SEQ = 256
SCALE = HD**-0.5
EPS = 1e-5
VMEM = 60 << 20
AXES = ("xh", "z", "y", "core", "xl")
SHARD = ("xh", "z", "y", "core")
PLANE = ("z", "y")
TOKENS = 1024
BF = jnp.bfloat16
F32 = jnp.float32


def shift(value, axis, step):
    names, size = (("xh", "xl"), 4) if axis == "x" else (axis, lax.axis_size(axis))
    return lax.ppermute(value, names, [(i, (i + step) % size) for i in range(size)])


def pick(value, index, axis=0):
    return lax.dynamic_index_in_dim(value, index, axis, keepdims=False)


def tie(*values):
    return lax.optimization_barrier(values)


def ring_first(value):
    return shift(value, "x", 1), shift(value, "x", -1)


def ring_second(below, above):
    return shift(below[:64], "x", 1), shift(above[64:], "x", -1)


def fold_first(parts):
    far = parts[2].astype(BF)
    return shift(far[:64], "x", 1), shift(far[64:], "x", -1)


def fold_second(parts, low, high):
    after_me = jnp.concatenate([parts[1][:64] + low.astype(F32), parts[1][64:]]).astype(BF)
    before_me = jnp.concatenate([parts[3][:64], parts[3][64:] + high.astype(F32)]).astype(BF)
    return shift(after_me, "x", 1), shift(before_me, "x", -1)


def sum_parts(near, other):
    near, other = near.reshape(4, 128, D), other.reshape(4, 128, D)
    return [near[k].astype(F32) + other[k].astype(F32) for k in range(4)]


def exchange4(parts):
    xh, core = lax.axis_index("xh"), lax.axis_index("core")
    rel = [parts[0]]
    for turn in (1, 2, 3):
        rel.append(lax.ppermute(parts[turn], ("xh", "core"), [(i, i ^ turn) for i in range(4)]))
    me = 2 * xh + core
    rel = jnp.stack(rel)
    return jnp.concatenate([pick(rel, me ^ source) for source in range(4)])


def pair_gather(value, axis):
    me = lax.axis_index(axis)
    rel = jnp.stack([value, shift(value, axis, 1)])
    return jnp.where(me == 0, rel, rel[::-1])


def gather_plane(value):
    return lax.all_gather(value, PLANE, axis=0, tiled=False)


def scatter_plane_whole(value):
    flat = value.reshape(-1, value.shape[-1])
    return lax.psum_scatter(flat, PLANE, scatter_dimension=0, tiled=True)


STEPS = (("core", 1), ("y", 1), ("y", 2), ("z", 1), ("z", 2), ("xh", 1))


def toward(value, axis, bit):
    size = lax.axis_size(axis)
    return lax.ppermute(value, axis, [(i, i ^ bit) for i in range(size)])


def gather_step(value, step):
    axis, bit = STEPS[step]
    other = toward(value, axis, bit)
    high = (lax.axis_index(axis) & bit) != 0
    return jnp.concatenate([jnp.where(high, other, value), jnp.where(high, value, other)])


def reduce_step(value, step):
    axis, bit = STEPS[step]
    parts = value.reshape(2, value.shape[0] // 2, value.shape[1])
    mine = jnp.where((lax.axis_index(axis) & bit) != 0, 1, 0)
    return pick(parts, mine) + toward(pick(parts, 1 - mine), axis, bit)


def rehome(value, back=False):
    pairs = []
    for z in range(4):
        for y in range(4):
            for core in range(2):
                for xl in range(2):
                    owner = ((z * 4 + y) * 2 + core) * 2 + xl
                    user = ((y * 4 + 2 * core + xl) * 2 + z // 2) * 2 + z % 2
                    pairs.append((user, owner) if back else (owner, user))
    return lax.ppermute(value, ("z", "y", "core", "xl"), pairs)


def after(value, *others):
    return lax.optimization_barrier((value, *others))[0]


def owner_order(vector):
    lead = vector.shape[:-1]
    size = vector.shape[-1] // 32
    return jnp.swapaxes(vector.reshape(*lead, 2, 16, size), -3, -2).reshape(*lead, -1)


def plain_order(vector):
    lead = vector.shape[:-1]
    size = vector.shape[-1] // 32
    return jnp.swapaxes(vector.reshape(*lead, 16, 2, size), -3, -2).reshape(*lead, -1)


def dot(left, right):
    return jnp.dot(left, right, preferred_element_type=F32)


def dot_rows(left, right):
    return lax.dot_general(left, right, (((0,), (0,)), ((), ())), preferred_element_type=F32)


def dot_cols(left, right):
    return lax.dot_general(left, right, (((1,), (1,)), ((), ())), preferred_element_type=F32)


def deal_body(place_ref, up_ref, qkv_ref, out_ref):
    me, xl = place_ref[0], place_ref[1]
    lane = lax.broadcasted_iota(jnp.int32, (32, 128), 1)
    for turn in range(4):
        target = me ^ turn
        xh, core = lax.div(target, 2), lax.rem(target, 2)
        for pair in range(8):
            start = xh * 4096 + core * 128 + pair * 512
            left = up_ref[:, pl.ds(pl.multiple_of(start, 128), 128)].astype(F32)
            right = up_ref[:, pl.ds(pl.multiple_of(start + 256, 128), 128)].astype(F32)
            left = jnp.where(xl == 0, left, pltpu.roll(left, 64, 1))
            right = jnp.where(xl == 0, pltpu.roll(right, 64, 1), right)
            both = jnp.where(lane < 64, left, right).astype(BF)
            out_ref[turn, :, pair * 128 : (pair + 1) * 128] = both
        for block in range(3):
            start = block * D + xh * 1024 + core * 512 + xl * 256
            out_ref[turn, :, 1024 + block * 256 : 1280 + block * 256] = qkv_ref[
                :, pl.ds(pl.multiple_of(start, 256), 256)
            ]


def deal(me, xl, up, qkv):
    vmem = pl.BlockSpec(memory_space=pltpu.VMEM)
    return pl.pallas_call(
        deal_body,
        in_specs=[pl.BlockSpec(memory_space=pltpu.SMEM), vmem, vmem],
        out_specs=vmem,
        out_shape=jax.ShapeDtypeStruct((4, 32, 1792), BF),
        name="deal",
    )(jnp.stack([me, xl]).astype(jnp.int32), up, qkv)


def spread_body(place_ref, *refs):
    pieces, up_ref, qkv_ref, held = refs[:4], refs[4], refs[5], refs[6]
    place, core = place_ref[0], place_ref[1]
    for step in range(4):
        source = lax.rem(place - step + 4, 4)
        for side in range(2):
            held[source, core ^ side] = pieces[step][side]
    for xh in range(2):
        for unit in range(16):
            for core in range(2):
                block = [
                    held[2 * xh + xl, core, :32, unit * 64 : (unit + 1) * 64].astype(F32) for xl in range(2)
                ]
                start = xh * 4096 + unit * 256 + core * 128
                up_ref[:, start : start + 128] = jnp.concatenate(block, axis=1)
        for core in range(2):
            for xl in range(2):
                for block in range(3):
                    start = block * D + xh * 1024 + core * 512 + xl * 256
                    qkv_ref[:, start : start + 256] = held[
                        2 * xh + xl, core, 32:, block * 256 : (block + 1) * 256
                    ].astype(F32)


def spread(place, core, pieces):
    vmem = pl.BlockSpec(memory_space=pltpu.VMEM)
    return pl.pallas_call(
        spread_body,
        in_specs=[pl.BlockSpec(memory_space=pltpu.SMEM)] + [vmem] * 4,
        out_specs=[vmem] * 2,
        out_shape=[jax.ShapeDtypeStruct((32, FF), F32), jax.ShapeDtypeStruct((32, 3 * D), F32)],
        scratch_shapes=[pltpu.VMEM((4, 2, 64, 1024), BF)],
        name="spread",
    )(jnp.stack([place, core]).astype(jnp.int32), *pieces)


def sort_body(core_ref, in_ref, near_ref, far_ref, down_ref, proj_ref):
    core = core_ref[0]
    for xh in range(2):
        for ref, which in ((near_ref, core), (far_ref, 1 - core)):
            start = pl.multiple_of(xh * 64 + which * 32, 32)
            ref[xh, :32] = in_ref[pl.ds(start, 32), :]
            ref[xh, 32:] = in_ref[pl.ds(pl.multiple_of(start + 256, 32), 32), :]
    down_ref[:, :1024] = in_ref[128:192, :]
    down_ref[:, 1024:] = in_ref[192:256, :]
    for block in range(8):
        proj_ref[:, block * 256 : (block + 1) * 256] = in_ref[
            256 + block * 16 : 272 + block * 16, 768:
        ]


def sort(core, summed):
    vmem = pl.BlockSpec(memory_space=pltpu.VMEM)
    return pl.pallas_call(
        sort_body,
        in_specs=[pl.BlockSpec(memory_space=pltpu.SMEM), vmem],
        out_specs=[vmem] * 4,
        out_shape=[
            jax.ShapeDtypeStruct((2, 64, 1024), BF),
            jax.ShapeDtypeStruct((2, 64, 1024), BF),
            jax.ShapeDtypeStruct((64, D), BF),
            jax.ShapeDtypeStruct((16, D), BF),
        ],
        name="sort",
    )(core.reshape(1).astype(jnp.int32), summed)


def norm_body(near_ref, far_ref, gain_ref, shift_ref, normed_ref, turned_ref, mean_ref, rstd_ref):
    hidden = jnp.where(pl.program_id(0) < 2, near_ref[...], far_ref[...]).astype(F32)
    mean = jnp.mean(hidden, axis=-1, keepdims=True)
    centered = hidden - mean
    rstd = lax.rsqrt(jnp.mean(centered * centered, axis=-1, keepdims=True) + EPS)
    normed = (centered * rstd * gain_ref[...] + shift_ref[...]).astype(BF)
    normed_ref[...] = normed
    turned_ref[...] = normed.T
    mean_ref[...] = mean
    rstd_ref[...] = rstd


def norm(near, far, gain, shift_row):
    step = 256
    row = pl.BlockSpec((step, D), lambda i: (i, 0))
    vec = pl.BlockSpec((1, D), lambda i: (0, 0))
    one = pl.BlockSpec((step, 1), lambda i: (i, 0))
    return pl.pallas_call(
        norm_body,
        grid=(TOKENS // step,),
        in_specs=[
            pl.BlockSpec((step, D), lambda i: (jnp.minimum(i, 1), 0)),
            pl.BlockSpec((step, D), lambda i: (jnp.maximum(i - 2, 0), 0)),
            vec,
            vec,
        ],
        out_specs=[row, pl.BlockSpec((D, step), lambda i: (0, i)), one, one],
        out_shape=[
            jax.ShapeDtypeStruct((TOKENS, D), BF),
            jax.ShapeDtypeStruct((D, TOKENS), BF),
            jax.ShapeDtypeStruct((TOKENS, 1), F32),
            jax.ShapeDtypeStruct((TOKENS, 1), F32),
        ],
        compiler_params=pltpu.CompilerParams(vmem_limit_bytes=VMEM),
        cost_estimate=pl.CostEstimate(flops=20 << 20, bytes_accessed=12 << 20, transcendentals=0),
        name="norm",
    )(near, far, gain.reshape(1, D), shift_row.reshape(1, D))


def heads_body(odd_ref, normed_hbm, turned_hbm, near_hbm, far_hbm, weights_hbm, bias_ref, cos_hbm,
               sin1_hbm, sin2_hbm, row_ref, col_hbm, ctx_hbm, out_hbm, pack_hbm,
               cos_ref, sin1_ref, sin2_ref, col_ref, normed, turned, cot, ctx_ref, out_ref, weights, proj, merged, queries, keys, values, grads, mask, raw, pulled,
               probs, slopes, back_q, back_k, packed, sem, out_sems):
    width = 4 * HD
    half = ROT // 2
    loads = [
        pltpu.make_async_copy(weights_hbm.at[:, pl.ds(256, 128), :], weights, sem.at[0]),
        pltpu.make_async_copy(normed_hbm, normed, sem.at[1]),
        pltpu.make_async_copy(near_hbm, cot.at[pl.ds(0, 512)], sem.at[2]),
        pltpu.make_async_copy(far_hbm, cot.at[pl.ds(512, 512)], sem.at[3]),
        pltpu.make_async_copy(turned_hbm, turned, sem.at[4]),
        pltpu.make_async_copy(cos_hbm, cos_ref, sem.at[5]),
        pltpu.make_async_copy(sin1_hbm, sin1_ref, sem.at[6]),
        pltpu.make_async_copy(sin2_hbm, sin2_ref, sem.at[7]),
        pltpu.make_async_copy(col_hbm, col_ref, sem.at[8]),
    ]
    for place in (0, 1, 5, 6, 7, 8, 2, 3, 4):
        loads[place].start()
    odd = odd_ref[0]
    for k in range(2):
        probs[k, :128, 128:] = jnp.zeros((128, 128), BF)
        slopes[k, :128, 128:] = jnp.zeros((128, 128), BF)

    def sides(item):
        pair, base = lax.rem(item, 2), lax.div(item, 2) * 512
        first = pl.multiple_of(base + lax.rem(2 * pair + 3 * odd, 4) * 128, 128)
        second = pl.multiple_of(base + lax.rem(2 * pair + 3 * odd + 1, 4) * 128, 128)
        return first, second

    for place in (0, 1, 5, 6, 7, 8):
        loads[place].wait()
    for block in range(8):
        proj[:, block * 256 : (block + 1) * 256] = weights[
            :, block * 16 : (block + 1) * 16, 768:
        ].reshape(256, 256)

    @pl.loop(0, 4)
    def _(step):
        rows = pl.ds(pl.multiple_of(step * 256, 256), 256)
        merged[...] = dot(normed[rows, :], weights[:, :, :768].reshape(D, 768)) + bias_ref[...]
        @pl.loop(0, 8)
        def _(part):
            here = pl.ds(pl.multiple_of(part * 32, 32), 32)
            there = pl.ds(pl.multiple_of(step * 256 + part * 32, 32), 32)
            cosine, sin1, sin2 = cos_ref[there, :], sin1_ref[there, :], sin2_ref[there, :]
            for pair in range(2):
                for ref, base in ((queries, 0), (keys, width)):
                    value = merged[here, base + pair * 128 : base + (pair + 1) * 128]
                    value = (
                        value * cosine
                        - pltpu.roll(value, 128 - half, 1) * sin1
                        + pltpu.roll(value, half, 1) * sin2
                    )
                    ref[pair, there, :] = (value * SCALE if base == 0 else value).astype(BF)
                start = 2 * width + pair * 128
                values[pair, there, :] = merged[here, start : start + 128].astype(BF)

    loads[2].wait()
    loads[3].wait()

    @pl.loop(0, 2)
    def _(step):
        rows = pl.ds(pl.multiple_of(step * 512, 512), 512)
        pulls = dot_cols(cot[rows, :], proj[...]).astype(BF)
        for pair in range(2):
            grads[pair, rows, :] = pulls[:, pair * 128 : (pair + 1) * 128]

    lane = lax.broadcasted_iota(jnp.int32, (SEQ, 128), 1)
    low = lane < HD

    @pl.loop(0, 4)
    def _(item):
        first, second = sides(item)
        segment = row_ref[item]
        for start in range(0, SEQ, 64):
            side = first if start < 128 else second
            rows = lax.broadcasted_iota(jnp.int32, (64, SEQ), 0) + start
            cols = lax.broadcasted_iota(jnp.int32, (64, SEQ), 1)
            own = col_ref[pl.ds(pl.multiple_of(side + start % 128, 64), 64), :]
            allowed = (cols <= rows) & (own == segment)
            mask[start : start + 64, :] = jnp.where(allowed, 0.0, -1e30)

        for pair in range(2):

            def load(ref):
                return jnp.concatenate([ref[pair, pl.ds(first, 128), :], ref[pair, pl.ds(second, 128), :]])

            query, key, value, grad = load(queries), load(keys), load(values), load(grads)
            for k in range(2):
                own = low if k == 0 else ~low
                raw[k] = dot_cols(jnp.where(own, query, 0), key)
                pulled[k] = dot_cols(jnp.where(own, grad, 0), value)
            for k in range(2):
                for start in range(0, SEQ, 32):
                    size = 128 if start < 128 else SEQ
                    rows = slice(start, start + 32)
                    scores = raw[k, rows, :size] + mask[rows, :size]
                    top = jnp.max(scores, axis=-1, keepdims=True)
                    expo = jnp.exp(scores - top)
                    prob = expo * (1.0 / jnp.sum(expo, axis=-1, keepdims=True))
                    probs[k, rows, :size] = prob.astype(BF)
                    grad_prob = pulled[k, rows, :size]
                    inner = jnp.sum(prob * grad_prob, axis=-1, keepdims=True)
                    slopes[k, rows, :size] = (prob * (grad_prob - inner)).astype(BF)
            context = jnp.where(low, dot(probs[0], value), dot(probs[1], value)).astype(BF)
            grad_v = jnp.where(low, dot_rows(probs[0], grad), dot_rows(probs[1], grad)).astype(BF)
            back_q[...] = SCALE * jnp.where(low, dot(slopes[0], key), dot(slopes[1], key))
            back_k[...] = jnp.where(low, dot_rows(slopes[0], query), dot_rows(slopes[1], query))
            lanes = slice(pair * 128, (pair + 1) * 128)
            for at, side in ((0, first), (128, second)):
                rows = pl.ds(side, 128)
                ctx_ref[rows, lanes] = context[at : at + 128]
                out_ref[rows, 2 * width + pair * 128 : 2 * width + (pair + 1) * 128] = grad_v[at : at + 128]
                for start in range(0, 128, 32):
                    there = pl.ds(pl.multiple_of(side + start, 32), 32)
                    cosine, sin1, sin2 = cos_ref[there, :], sin1_ref[there, :], sin2_ref[there, :]
                    for ref, base in ((back_q, 0), (back_k, width)):
                        turned_back = ref[at + start : at + start + 32, :]
                        turned_back = (
                            turned_back * cosine
                            + pltpu.roll(turned_back, 128 - half, 1) * sin1
                            - pltpu.roll(turned_back, half, 1) * sin2
                        )
                        out_ref[there, base + pair * 128 : base + (pair + 1) * 128] = turned_back.astype(BF)

    def store(step):
        owners = pl.ds(step * 2, 2)
        return pltpu.make_async_copy(
            packed.at[owners], pack_hbm.at[owners, pl.ds(256, 128), :], out_sems.at[step]
        )

    ctx_store = pltpu.make_async_copy(ctx_ref, ctx_hbm, sem.at[0])
    out_store = pltpu.make_async_copy(out_ref, out_hbm, sem.at[1])
    ctx_store.start()
    out_store.start()

    total = dot_rows(ctx_ref[...], cot[...]).astype(BF)
    for block in range(8):
        packed[:, block * 16 : (block + 1) * 16, 768:] = total[
            :, block * 256 : (block + 1) * 256
        ].reshape(16, 16, 256)
    loads[4].wait()

    @pl.loop(0, 8)
    def _(step):
        rows = pl.ds(pl.multiple_of(step * 256, 256), 256)
        total = dot(turned[rows, :], out_ref[...]).astype(BF)
        packed[pl.ds(step * 2, 2), :, :768] = total.reshape(2, 128, 768)
        store(step).start()

    ctx_store.wait()
    out_store.wait()

    @pl.loop(0, 8)
    def _(step):
        store(step).wait()


def heads(odd, normed, turned, near, far, weights, bias, cosine, sin1, sin2, segment):
    blocks = segment.reshape(2, 4, 128)
    rows = jnp.where(odd == 0, blocks, jnp.roll(blocks, 1, axis=1)).reshape(4, 1, SEQ)
    vmem, hbm = pl.BlockSpec(memory_space=pltpu.VMEM), pl.BlockSpec(memory_space=pltpu.HBM)
    table = pltpu.VMEM((TOKENS, 128), F32)
    head_b = pltpu.VMEM((2, TOKENS, 128), BF)
    head_f = pltpu.VMEM((SEQ, 128), F32)
    return pl.pallas_call(
        heads_body,
        in_specs=[pl.BlockSpec(memory_space=pltpu.SMEM)] + [hbm] * 5 + [vmem] + [hbm] * 3 + [vmem, hbm],
        out_specs=[hbm] * 3,
        out_shape=[
            jax.ShapeDtypeStruct((TOKENS, 4 * HD), BF),
            jax.ShapeDtypeStruct((TOKENS, 12 * HD), BF),
            jax.ShapeDtypeStruct((16, 384, 1024), BF),
        ],
        scratch_shapes=[
            table,
            table,
            table,
            pltpu.VMEM((TOKENS, 1), jnp.int32),
            pltpu.VMEM((TOKENS, D), BF),
            pltpu.VMEM((D, TOKENS), BF),
            pltpu.VMEM((TOKENS, D), BF),
            pltpu.VMEM((TOKENS, 4 * HD), BF),
            pltpu.VMEM((TOKENS, 12 * HD), BF),
            pltpu.VMEM((16, 128, 1024), BF),
            pltpu.VMEM((256, D), BF),
            pltpu.VMEM((256, 12 * HD), F32),
            head_b,
            head_b,
            head_b,
            head_b,
            pltpu.VMEM((SEQ, SEQ), F32),
            pltpu.VMEM((2, SEQ, SEQ), F32),
            pltpu.VMEM((2, SEQ, SEQ), F32),
            pltpu.VMEM((2, SEQ, SEQ), BF),
            pltpu.VMEM((2, SEQ, SEQ), BF),
            head_f,
            head_f,
            pltpu.VMEM((16, 128, 1024), BF),
            pltpu.SemaphoreType.DMA((9,)),
            pltpu.SemaphoreType.DMA((8,)),
        ],
        compiler_params=pltpu.CompilerParams(vmem_limit_bytes=VMEM),
        cost_estimate=pl.CostEstimate(
            flops=14 << 30, bytes_accessed=40 << 20, transcendentals=16 * SEQ * SEQ
        ),
        name="heads",
    )(
        odd.reshape(1), normed, turned, near, far, weights, bias, cosine, sin1, sin2, rows,
        segment.reshape(TOKENS, 1),
    )


def feed_body(normed_hbm, turned_hbm, near_hbm, far_hbm, weights_hbm, bias_ref, pack_in,
              act_hbm, grad_hbm, pack_hbm,
              normed, turned, cot, up, down, act, grads, upper_ref, slope_ref, up_out, down_out,
              sems, act_sems, grad_sems, up_sems, down_sems):
    up_load = pltpu.make_async_copy(weights_hbm.at[:, pl.ds(0, 128), :], up, sems.at[0])
    down_load = pltpu.make_async_copy(weights_hbm.at[:, pl.ds(128, 128), :], down, sems.at[1])
    normed_load = pltpu.make_async_copy(normed_hbm, normed, sems.at[2])
    near_load = pltpu.make_async_copy(near_hbm, cot.at[pl.ds(0, 512)], sems.at[3])
    far_load = pltpu.make_async_copy(far_hbm, cot.at[pl.ds(512, 512)], sems.at[4])
    turned_load = pltpu.make_async_copy(turned_hbm, turned, sems.at[5])
    for load in (up_load, normed_load, down_load, near_load, far_load, turned_load):
        load.start()

    def act_store(step):
        rows = pl.ds(pl.multiple_of(step * 256, 256), 256)
        return pltpu.make_async_copy(act.at[rows, :], act_hbm.at[rows, :], act_sems.at[step])

    def grad_store(step):
        rows = pl.ds(pl.multiple_of(step * 256, 256), 256)
        return pltpu.make_async_copy(grads.at[rows, :], grad_hbm.at[rows, :], grad_sems.at[step])

    def up_store(step):
        owners = pl.ds(step * 2, 2)
        return pltpu.make_async_copy(
            up_out.at[owners], pack_hbm.at[owners, pl.ds(0, 128), :], up_sems.at[step]
        )

    def down_store(step):
        owners = pl.ds(step * 4, 4)
        return pltpu.make_async_copy(
            down_out.at[owners], pack_hbm.at[owners, pl.ds(128, 128), :], down_sems.at[step]
        )

    root = math.sqrt(2.0 / math.pi)
    up_load.wait()
    normed_load.wait()

    @pl.loop(0, 4)
    def _(step):
        rows = pl.ds(pl.multiple_of(step * 256, 256), 256)
        upper_ref[rows, :] = dot(normed[rows, :], up[...].reshape(D, 1024)) + bias_ref[...]

    down_load.wait()
    near_load.wait()
    far_load.wait()

    @pl.loop(0, 4)
    def _(step):
        rows = pl.ds(pl.multiple_of(step * 256, 256), 256)
        slope_ref[...] = dot_cols(cot[rows, :1024], down[:, :64].reshape(1024, 1024)) + dot_cols(
            cot[rows, 1024:], down[:, 64:].reshape(1024, 1024)
        )

        @pl.loop(0, 16)
        def _(part):
            here = pl.ds(pl.multiple_of(part * 16, 16), 16)
            there = pl.ds(pl.multiple_of(step * 256 + part * 16, 16), 16)
            for side in range(2):
                lanes = slice(side * 512, side * 512 + 512)
                upper = upper_ref[there, lanes]
                square = upper * upper
                bend = jnp.tanh(upper * (root + (root * 0.044715) * square))
                half = 0.5 + 0.5 * bend
                slope = half + upper * (0.5 - 0.5 * (bend * bend)) * (root + (root * 3 * 0.044715) * square)
                act[there, lanes] = (upper * half).astype(BF)
                grads[there, lanes] = (slope_ref[here, lanes] * slope).astype(BF)

        act_store(step).start()
        grad_store(step).start()

    turned_load.wait()

    @pl.loop(0, 8)
    def _(step):
        rows = pl.ds(pl.multiple_of(step * 256, 256), 256)
        total = dot(turned[rows, :], grads[...]).astype(BF)
        up_out[pl.ds(step * 2, 2)] = total.reshape(2, 128, 1024)
        up_store(step).start()

    @pl.loop(0, 4)
    def _(step):
        lanes = pl.ds(pl.multiple_of(step * 256, 256), 256)
        total = dot_rows(act[:, lanes], cot[...]).astype(BF)
        down_out[pl.ds(step * 4, 4), :64] = total[:, :1024].reshape(4, 64, 1024)
        down_out[pl.ds(step * 4, 4), 64:] = total[:, 1024:].reshape(4, 64, 1024)
        down_store(step).start()

    @pl.loop(0, 4)
    def _(step):
        act_store(step).wait()
        grad_store(step).wait()
        down_store(step).wait()

    @pl.loop(0, 8)
    def _(step):
        up_store(step).wait()


def feed(normed, turned, near, far, weights, bias, pack):
    vmem, hbm = pl.BlockSpec(memory_space=pltpu.VMEM), pl.BlockSpec(memory_space=pltpu.HBM)
    return pl.pallas_call(
        feed_body,
        in_specs=[hbm] * 5 + [vmem, hbm],
        out_specs=[hbm] * 3,
        out_shape=[
            jax.ShapeDtypeStruct((TOKENS, 1024), BF),
            jax.ShapeDtypeStruct((TOKENS, 1024), BF),
            jax.ShapeDtypeStruct((16, 384, 1024), BF),
        ],
        input_output_aliases={6: 2},
        scratch_shapes=[
            pltpu.VMEM((TOKENS, D), BF),
            pltpu.VMEM((D, TOKENS), BF),
            pltpu.VMEM((TOKENS, D), BF),
            pltpu.VMEM((16, 128, 1024), BF),
            pltpu.VMEM((16, 128, 1024), BF),
            pltpu.VMEM((TOKENS, 1024), BF),
            pltpu.VMEM((TOKENS, 1024), BF),
            pltpu.VMEM((TOKENS, 1024), F32),
            pltpu.VMEM((256, 1024), F32),
            pltpu.VMEM((16, 128, 1024), BF),
            pltpu.VMEM((16, 128, 1024), BF),
            pltpu.SemaphoreType.DMA((6,)),
            pltpu.SemaphoreType.DMA((4,)),
            pltpu.SemaphoreType.DMA((4,)),
            pltpu.SemaphoreType.DMA((8,)),
            pltpu.SemaphoreType.DMA((4,)),
        ],
        compiler_params=pltpu.CompilerParams(vmem_limit_bytes=VMEM),
        cost_estimate=pl.CostEstimate(
            flops=8 * TOKENS * D * 1024, bytes_accessed=32 << 20, transcendentals=TOKENS * 1024
        ),
        name="feed",
    )(normed, turned, near, far, weights, bias, pack)


def branch_body(context_ref, proj_ref, act_ref, down_ref, near_ref, far_ref):
    total = dot(act_ref[...], down_ref[...].reshape(1024, 256))
    total = (total + dot(context_ref[...], proj_ref[...].reshape(256, 256))).astype(BF)
    near_ref[...] = total[:512]
    far_ref[...] = total[512:]


def branch_out(context, active, weights):
    return pl.pallas_call(
        branch_body,
        grid=(8,),
        in_specs=[
            pl.BlockSpec((TOKENS, 256), lambda n: (0, 0), pipeline_mode=pl.Buffered(1)),
            pl.BlockSpec((16, 16, 256), lambda n: (0, 16 + n, 3)),
            pl.BlockSpec((TOKENS, 1024), lambda n: (0, 0), pipeline_mode=pl.Buffered(1)),
            pl.BlockSpec((16, 64, 256), lambda n: (0, 2 + n // 4, n % 4)),
        ],
        out_specs=[pl.BlockSpec((512, 256), lambda n: (0, n))] * 2,
        out_shape=[jax.ShapeDtypeStruct((512, D), BF)] * 2,
        compiler_params=pltpu.CompilerParams(vmem_limit_bytes=VMEM),
        cost_estimate=pl.CostEstimate(
            flops=2 * TOKENS * D * 1280, bytes_accessed=12 << 20, transcendentals=0
        ),
        name="branch",
    )(context, weights, active, weights)


def pull_body(grad_ref, merged_ref, up_ref, qkv_ref, hid_near_ref, hid_far_ref, mean_ref, rstd_ref,
              near_ref, far_ref, gain_ref, shift_ref, up_ref_sum, qkv_ref_sum):
    total = dot_cols(grad_ref[...], up_ref[...].reshape(256, 1024))
    total = total + dot_cols(merged_ref[...], qkv_ref[...].reshape(256, 1024)[:, :768])
    near_ref[...] = total[:512].astype(BF)
    far_ref[...] = total[512:].astype(BF)
    hidden = jnp.concatenate([hid_near_ref[...], hid_far_ref[...]]).astype(F32)
    normal = (hidden - mean_ref[...]) * rstd_ref[...]
    gain_ref[...] = jnp.sum(total * normal, axis=0, keepdims=True)
    shift_ref[...] = jnp.sum(total, axis=0, keepdims=True)

    @pl.when(pl.program_id(0) == 0)
    def _():
        ones = jnp.ones((16, TOKENS), BF)
        up_ref_sum[...] = dot(ones, grad_ref[...])[:1]
        qkv_ref_sum[...] = dot(ones, merged_ref[...])[:1]


def pull(grad_upper, grad_merged, weights, near, far, mean, rstd):
    def whole(width):
        return pl.BlockSpec((TOKENS, width), lambda n: (0, 0), pipeline_mode=pl.Buffered(1))

    half = pl.BlockSpec((512, 256), lambda n: (0, n))
    vec = pl.BlockSpec((1, 256), lambda n: (0, n))
    return pl.pallas_call(
        pull_body,
        grid=(8,),
        in_specs=[
            whole(1024),
            whole(768),
            pl.BlockSpec((2, 128, 1024), lambda n: (n, 0, 0)),
            pl.BlockSpec((2, 128, 1024), lambda n: (n, 2, 0)),
            half,
            half,
            whole(1),
            whole(1),
        ],
        out_specs=[half] * 2
        + [vec, vec, pl.BlockSpec((1, 1024), lambda n: (0, 0)), pl.BlockSpec((1, 768), lambda n: (0, 0))],
        out_shape=[
            jax.ShapeDtypeStruct((512, D), BF),
            jax.ShapeDtypeStruct((512, D), BF),
            jax.ShapeDtypeStruct((1, D), F32),
            jax.ShapeDtypeStruct((1, D), F32),
            jax.ShapeDtypeStruct((1, 1024), F32),
            jax.ShapeDtypeStruct((1, 768), F32),
        ],
        compiler_params=pltpu.CompilerParams(vmem_limit_bytes=VMEM),
        cost_estimate=pl.CostEstimate(
            flops=2 * TOKENS * D * 1792, bytes_accessed=16 << 20, transcendentals=0
        ),
        name="pull",
    )(grad_upper, grad_merged, weights, weights, near, far, mean, rstd)


def local(
    hidden_in, norm_gain, norm_shift, qkv_weight, qkv_bias, proj_weight, proj_bias,
    up_weight, up_bias, down_weight, down_bias, segment_ids, positions, cotangent,
):
    xh, core, xl = lax.axis_index("xh"), lax.axis_index("core"), lax.axis_index("xl")
    place = 2 * xh + xl
    hidden_own = hidden_in.reshape(128, D)
    cot_own = cotangent.reshape(128, D)

    parts = exchange4(deal(2 * xh + core, xl, up_weight, qkv_weight))
    down_part = lax.dynamic_slice_in_dim(down_weight, xl * 64, 64, 0)
    proj_part = rehome(lax.dynamic_slice_in_dim(proj_weight, xl * 16, 16, 0))
    proj_part = proj_part.reshape(16, 8, 256).swapaxes(0, 1).reshape(128, 256)
    send = jnp.concatenate(
        [
            parts[:, :1024],
            down_part[:, :1024],
            down_part[:, 1024:],
            jnp.concatenate([parts[:, 1024:], proj_part], axis=1),
        ]
    )
    weights = gather_plane(send)

    small = jnp.concatenate([norm_gain, norm_shift, proj_bias, down_bias, qkv_bias, up_bias])[None]
    hidden_turned = owner_order(hidden_own)
    marks = jnp.stack(
        [positions.reshape(128), lax.dynamic_slice_in_dim(segment_ids.reshape(SEQ), xl * 128, 128)]
    )
    small, hidden_turned, cot_sent, marks, _ = tie(small, hidden_turned, cot_own, marks, send)
    hid_below, hid_above = ring_first(hidden_turned)
    small = gather_step(small, 0)
    small, hid_below, hid_above = tie(small, hid_below, hid_above)
    hid_low, hid_high = ring_second(hid_below, hid_above)
    small = gather_step(small, 1)
    small, hid_low, hid_high, cot_sent = tie(small, hid_low, hid_high, cot_sent)
    hid = jnp.concatenate([hidden_turned, hid_above, hid_low, hid_high, hid_below])
    hid_far = shift(hid, "core", 1)
    cot_below, cot_above = ring_first(cot_sent)
    small = gather_step(small, 2)
    small, marks, cot_below, cot_above = tie(small, marks, cot_below, cot_above)
    cot_low, cot_high = ring_second(cot_below, cot_above)
    small = gather_step(small, 3)
    small, marks, cot_low, cot_high = tie(small, marks, cot_low, cot_high)
    cot = jnp.concatenate([cot_sent, cot_above, cot_low, cot_high, cot_below])
    cot_far = shift(cot, "core", 1)
    small = gather_step(small, 4)
    marks = pair_gather(marks, "xl")
    small, marks = tie(small, marks)
    small = gather_step(small, 5).astype(F32)
    marks = pair_gather(marks, "xh").reshape(4, 2, 128)
    marks = jnp.stack([pick(marks, (place + k) % 4) for k in range(4)])
    marks = jnp.stack([marks, shift(marks, "core", 1)]).transpose(2, 0, 1, 3).reshape(2, TOKENS)
    position_all, segment_all = marks[0], marks[1]

    gain = owner_order(small[:, :32].reshape(D))
    shift_row = owner_order(small[:, 32:64].reshape(D))
    out_bias = (small[:, 64:96] + small[:, 96:128]).reshape(D)
    qkv_b = small[:, 128:224].reshape(3, 2, 2, 2, 256)[:, xh, core, xl].reshape(1, 768)
    up_b = small[:, 224:352].reshape(2, 16, 2, 128)[xh, :, core]
    up_b = lax.dynamic_slice_in_dim(up_b, xl * 64, 64, 1).reshape(1, 1024)
    normed, turned, mean, rstd = norm(hid, hid_far, gain, shift_row)

    lane = jnp.arange(128) % HD
    freqs = 10000.0 ** (-(lane % 16).astype(F32) * (2.0 / ROT))
    angles = position_all.astype(F32)[:, None] * freqs
    cosine = jnp.where(lane < ROT, jnp.cos(angles), 1.0)
    sine = jnp.sin(angles)
    sin1 = jnp.where(lane < 16, sine, 0.0)
    sin2 = jnp.where((lane >= 16) & (lane < ROT), sine, 0.0)

    context, grad_merged, pack = heads(
        xl, normed, turned, cot, cot_far, weights, qkv_b, cosine, sin1, sin2, segment_all
    )
    active, grad_upper, pack = feed(normed, turned, cot, cot_far, weights, up_b, pack)
    back = scatter_plane_whole(pack)

    pulled, pulled_far, gain_sum, shift_sum, up_sum, qkv_sum = pull(
        grad_upper, grad_merged, weights, hid, hid_far, mean, rstd
    )
    out_sum = jnp.sum(cot_own.astype(F32), axis=0)
    qkv_full = lax.dynamic_update_slice(
        jnp.zeros((3, 2, 2, 2, 256), F32), qkv_sum.reshape(3, 1, 1, 1, 256), (0, xh, core, xl, 0)
    )
    up_full = lax.dynamic_update_slice(
        jnp.zeros((2, 16, 2, 2, 64), F32), up_sum.reshape(1, 16, 1, 1, 64), (xh, 0, core, xl, 0)
    )
    sums = jnp.concatenate(
        [plain_order(s.reshape(D)).reshape(64, 32) for s in (gain_sum, shift_sum)]
        + [out_sum.reshape(64, 32), qkv_full.reshape(64, 96), up_full.reshape(64, 128)],
        axis=1,
    )
    pulled_far = shift(pulled_far, "core", 1)
    sums = reduce_step(sums, 5)
    branch, branch_far = branch_out(context, after(active, gain_sum), weights)
    sums, branch_far, pulled_far = tie(sums, branch_far, pulled_far)
    pulled = sum_parts(pulled, pulled_far)
    low, high = fold_first(pulled)
    branch_far = shift(branch_far, "core", 1)
    sums = reduce_step(sums, 4)
    sums, branch_far, low, high = tie(sums, branch_far, low, high)
    from_below, from_above = fold_second(pulled, low, high)
    branch = sum_parts(branch, branch_far)
    low, high = fold_first(branch)
    sums = reduce_step(sums, 3)
    sums, low, high, from_below, from_above = tie(sums, low, high, from_below, from_above)
    branch_below, branch_above = fold_second(branch, low, high)
    sums = reduce_step(sums, 2)
    grad_own = pulled[0] + from_below.astype(F32) + from_above.astype(F32)

    own = owner_order(hidden_own).astype(F32)
    mean = jnp.mean(own, axis=-1, keepdims=True)
    centered = own - mean
    rstd = lax.rsqrt(jnp.mean(centered * centered, axis=-1, keepdims=True) + EPS)
    normal_own = centered * rstd
    scaled = grad_own * gain
    inner = jnp.mean(scaled * normal_own, axis=-1, keepdims=True)
    lifted = (scaled - jnp.mean(scaled, axis=-1, keepdims=True) - normal_own * inner) * rstd
    grad_hidden = (cot_own.astype(F32) + plain_order(lifted)).reshape(1, 128, D)

    sums, branch_below, branch_above, grad_hidden = tie(sums, branch_below, branch_above, grad_hidden)
    sums = reduce_step(reduce_step(sums, 1), 0)
    sums = (sums + shift(sums, "xl", 1))[0]
    branch = branch[0] + branch_below.astype(F32) + branch_above.astype(F32)
    block_out = hidden_own.astype(F32) + branch + out_bias
    block_out = block_out.astype(BF).reshape(1, 128, D)

    back = after(back, grad_hidden, block_out, sums)
    near, far, down_rows, proj_rows = sort(core, back)
    far = shift(far, "core", 1)
    down_rows, proj_rows = after((down_rows, proj_rows), far)
    pair = jnp.stack([near, far], axis=1)
    pieces = [pick(pair, xh)]
    for step in (1, 2, 3):
        pieces.append(shift(pick(pair, ((place + step) % 4) // 2), "x", step))
    grad_up, grad_qkv = spread(place, core, pieces)
    grad_down = pair_gather(down_rows, "xl").reshape(128, D)
    grad_proj = pair_gather(rehome(proj_rows, back=True), "xl").reshape(32, D)
    return (
        block_out,
        grad_hidden,
        sums[:32],
        sums[32:64],
        grad_qkv,
        sums[96:192],
        grad_proj.astype(F32),
        sums[64:96],
        grad_up,
        sums[192:320],
        grad_down.astype(F32),
        sums[64:96],
    )


def solution(mesh):
    cut = Mesh(mesh.devices.reshape(2, 4, 4, 2, 2), AXES)
    row, vec = P(SHARD, None), P(SHARD)
    tok = P(SHARD, "xl", None)
    return jax.shard_map(
        local,
        mesh=cut,
        in_specs=(
            tok, vec, vec, row, vec, row, vec, row, vec, row, vec, row, P(SHARD, "xl"), tok,
        ),
        out_specs=(tok, tok, vec, vec, row, vec, row, vec, row, vec, row, vec),
        check_vma=False,
    )
```

time: 741 us -> 327 us (0.44); the launches traced: 729 us -> 325 us
  waiting for transfers between devices: 489 us -> 74 us
  matrix products: 88.2 us -> 0 us
  Pallas kernels: 14.9 us -> 98.5 us
  starting transfers between devices: 25.8 us -> 78.3 us
  local copies, waits for them, and re-layouts: 64.6 us -> 25.5 us
    unnamed x8 -> x2, waiting for transfers between devices: 188 us -> 0.03 us
    all_gather x2 -> x1, waiting for transfers between devices: 101 us -> 10.9 us  [gather_plane(): return lax.all_gather(value, PLANE, axis=0, tiled=False)]
    dot_general x18 -> x0, matrix products: 88.2 us -> none  [the longest x6 39.4 us: dot_cols(): lax.dot_general(left, right, (((1,), (1,)), ((), ())), preferred_element_...]
    pallas_call x1 -> x8, Pallas kernels: 14.9 us -> 98.5 us  [the longest x1 29.4 us: feed(): pl.pallas_call(feed_body, in_specs=[hbm] * 5 + [vmem, hbm], out_specs=[hb...]
    reduce_scatter x2 -> x1, waiting for transfers between devices: 73 us -> 0.01 us  [scatter_plane_whole(): return lax.psum_scatter(flat, PLANE, scatter_dimension=0, tiled=True)]
    all_gather x2 -> x0, waiting for transfers between devices: 68.6 us -> none  [gather_group(): return lax.all_gather(value, GROUP, axis=0, tiled=True)]
    ppermute x19 -> x47, starting transfers between devices: 25.4 us -> 78.3 us  [the longest x30 39.6 us: shift(): lax.ppermute(value, names, [(i, (i + step) % size) for i in range(size)])]
    slice x13 -> x15, local copies, waits for them, and re-layouts: 18.7 us -> 4.84 us  [the longest x2 1.71 us: fold_first(): return (shift(far[:64], 'x', 1), shift(far[64:], 'x', -1))]
  transfers between devices with their start and end apart: 26 -> 49, of which waited for: 20 -> 21; matrix products, arithmetic and copies ran while one was open for 17% -> 16% of each run, Pallas kernels for 2% -> 10%
where the time goes in v2:
time: 327 us; the launch traced here: 325 us
  Pallas kernels  98.5 us (30%)
  starting transfers between devices  78.3 us (24%)
  waiting for transfers between devices  74 us (23%)
  other arithmetic  33.5 us (10%)
  local copies, waits for them, and re-layouts  25.5 us (8%)
  between operations  15 us (5%)
    ppermute x30, waiting for transfers between devices, shift(): lax.ppermute(value, names, [(i, (i + step) % size) for i in range(size)])  51.3 us
    ppermute x30, starting transfers between devices, shift(): lax.ppermute(value, names, [(i, (i + step) % size) for i in range(size)])  39.6 us
    pallas_call x1, Pallas kernels, feed(): pl.pallas_call(feed_body, in_specs=[hbm] * 5 + [vmem, hbm], out_specs=[hb...  29.4 us
    pallas_call x1, Pallas kernels, heads(): pl.pallas_call(heads_body, in_specs=[pl.BlockSpec(memory_space=pltpu.SMEM...  28 us
    ppermute x12, starting transfers between devices, toward(): return lax.ppermute(value, axis, [(i, i ^ bit) for i in range(size)])  24.5 us
    pallas_call x1, Pallas kernels, pull(): pl.pallas_call(pull_body, grid=(8,), in_specs=[whole(1024), whole(768), p...  15.2 us
    pallas_call x1, Pallas kernels, branch_out(): pl.pallas_call(branch_body, grid=(8,), in_specs=[pl.BlockSpec((TOKENS, 25...  11.1 us
    all_gather x1, waiting for transfers between devices, gather_plane(): return lax.all_gather(value, PLANE, axis=0, tiled=False)  10.9 us
  transfers between devices with their start and end apart: 49, of which 21 were waited for; matrix products, arithmetic and copies ran while one was open for 16% of the time, Pallas kernels for 10%

profile of v2, /device:TPU:1, one launch (start us, length us, event | category | flops | bytes accessed | tf_op | source)
XLA Modules:
  0.0 324.9 jit_solution(9230011389024876770)
XLA Ops:
  7.8 2.2 deal.1
  11.2 3.7 %collective-permute-start.1 = (bf16[32,1792]{1,0:T(8,128)(2,1)S(1)}, bf16[32,1792]{1,0:T(8,128)(2,1)S(1)}, u32[]{:S(2)}, u32[]{:S(2)}) collective-permute-start(bf16[32,1792]{1,0:T(8,128)(2,1)S(1)} %get-tuple-element.191), channel_id=1, source_target_pairs={{0,64},{2,66},{64,0},{66,2},{1,65},{3,67},{65,1},{67,3},{4,68},{6,... | collective-permute-start | bytes 344072 | tf_op jit(solution)/shard_map/ppermute | solution.py:68
  15.8 5.3 %collective-permute-start.3 = (bf16[16,2048]{1,0:T(8,128)(2,1)S(1)}, bf16[16,2048]{1,0:T(8,128)(2,1)S(1)}, u32[]{:S(2)}, u32[]{:S(2)}) collective-permute-start(bf16[16,2048]{1,0:T(8,128)(2,1)S(1)} %constant_dynamic-slice_fusion.13), channel_id=1, source_target_pairs={{0,0},{1,4},{2,8},{3,12},{4,16},{5,20},{6,24},{7,28},{8,32},{9,36}... | collective-permute-start | bytes 196616 | tf_op jit(solution)/shard_map/ppermute | solution.py:120
  21.2 2.6 collective-permute-done.3
  26.8 2.7 collective-permute-start.5
  30.9 10.7 %collective-permute-done.5 = bf16[128,2048]{1,0:T(8,128)(2,1)S(1)} collective-permute-done((bf16[128,2048]{1,0:T(8,128)(2,1)}, bf16[128,2048]{1,0:T(8,128)(2,1)S(1)}, u32[]{:S(2)}, u32[]{:S(2)}) %collective-permute-start.5) | collective-permute-done | bytes 524320 | tf_op jit(solution)/shard_map/ppermute | solution.py:29
  47.0 6.1 %collective-permute-done.8 = bf16[64,2048]{1,0:T(8,128)(2,1)S(1)} collective-permute-done((bf16[64,2048]{1,0:T(8,128)(2,1)S(1)}, bf16[64,2048]{1,0:T(8,128)(2,1)S(1)}, u32[]{:S(2)}, u32[]{:S(2)}) %collective-permute-start.8) | collective-permute-done | bytes 262176 | tf_op jit(solution)/shard_map/ppermute | solution.py:29
  53.4 2.4 collective-permute-start.13
  55.9 3.8 %collective-permute-start.11 = (bf16[4,352]{1,0:T(4,128)(2,1)S(1)}, bf16[4,352]{1,0:T(4,128)(2,1)S(1)}, u32[]{:S(2)}, u32[]{:S(2)}) collective-permute-start(bf16[4,352]{1,0:T(4,128)(2,1)S(1)} %pad_maximum_fusion.14), channel_id=1, source_target_pairs={{0,8},{4,12},{8,0},{12,4},{1,9},{5,13},{9,1},{13,5},{2,10},{6,14},... | collective-permute-start | bytes 8456 | tf_op jit(solution)/shard_map/ppermute | solution.py:94
  60.6 2.1 collective-permute-start.10
  62.7 4.1 %collective-permute-done.12 = bf16[128,2048]{1,0:T(8,128)(2,1)S(1)} collective-permute-done((bf16[128,2048]{1,0:T(8,128)(2,1)S(1)}, bf16[128,2048]{1,0:T(8,128)(2,1)S(1)}, u32[]{:S(2)}, u32[]{:S(2)}) %collective-permute-start.12) | collective-permute-done | bytes 524320 | tf_op jit(solution)/shard_map/ppermute | solution.py:29
  67.1 2.6 collective-permute-start.16
  70.5 2.1 collective-permute-done.14
  74.4 3.0 collective-permute-start.17
  78.9 3.4 %collective-permute-start.21 = (s32[2,2,128]{2,1,0:T(2,128)S(1)}, s32[2,2,128]{2,1,0:T(2,128)S(1)}, u32[]{:S(2)}, u32[]{:S(2)}) collective-permute-start(s32[2,2,128]{2,1,0:T(2,128)S(1)} %reverse_select_fusion.3), channel_id=1, source_target_pairs={{0,64},{64,0},{1,65},{65,1},{2,66},{66,2},{3,67},{67,3},{4,68},{68... | collective-permute-start | bytes 6152 | tf_op jit(solution)/shard_map/ppermute | solution.py:29
  83.1 4.8 %collective-permute-start.20 = (bf16[512,2048]{1,0:T(8,128)(2,1)}, bf16[512,2048]{1,0:T(8,128)(2,1)}, u32[]{:S(2)}, u32[]{:S(2)}) collective-permute-start(bf16[512,2048]{1,0:T(8,128)(2,1)} %constant_dynamic-update-slice_fusion.5.near_hbm), channel_id=1, source_target_pairs={{0,2},{2,0},{1,3},{3,1},{4,6},{6,4},{5,7},{7,5},{8,10},{10,8},{9,1... | collective-permute-start | bytes 6291464 | tf_op jit(solution)/shard_map/ppermute | solution.py:29
  89.0 3.0 collective-permute-start.19
  92.0 3.2 fusion.6
  100.7 7.8 %norm.1 = (bf16[1024,2048]{1,0:T(8,128)(2,1)}, bf16[2048,1024]{1,0:T(8,128)(2,1)}, f32[1024,1]{1,0:T(8,128)}, f32[1024,1]{1,0:T(8,128)}) custom-call(bf16[512,2048]{1,0:T(8,128)(2,1)} %copy-done.2, bf16[512,2048]{1,0:T(8,128)(2,1)} %collective-permute-done.10.far_ref.hid_far_ref, f32[1,2048]{1,0:T(1,128)} %reshape_reshape.26.gain_ref, ...), custom_call_target="tpu_custom_call" | custom-call | flops 20971520 | bytes 12582912 | tf_op jit(solution)/shard_map/norm/pallas_call | solution.py:267
  108.4 10.9 %all-gather.3.cloned.1.call-done = bf16[6144,1024]{1,0:T(8,128)(2,1)} async-done(((bf16[384,1024]{1,0:T(8,128)(2,1)}), bf16[6144,1024]{1,0:T(8,128)(2,1)}) %all-gather.3.cloned.1.call-update) | async-done | bytes 12582928 | tf_op jit(solution)/shard_map/all_gather | solution.py:81
  119.3 28.0 %heads.1 = (bf16[1024,256]{1,0:T(8,128)(2,1)}, bf16[1024,768]{1,0:T(8,128)(2,1)}, bf16[16,384,1024]{2,1,0:T(8,128)(2,1)}) custom-call(s32[1]{0:T(128)} %bitcast.1.odd_ref, bf16[1024,2048]{1,0:T(8,128)(2,1)} %get-tuple-element.95.normed_hbm, bf16[2048,1024]{1,0:T(8,128)(2,1)} %get-tuple-element.96.turned_hbm, ...), custom_call_target="tpu_custom_call" | custom-call | flops 15032385536 | bytes 41943040 | tf_op jit(solution)/shard_map/heads/pallas_call | solution.py:455
  147.3 29.4 %feed.1 = (bf16[1024,1024]{1,0:T(8,128)(2,1)}, bf16[1024,1024]{1,0:T(8,128)(2,1)}, bf16[16,384,1024]{2,1,0:T(8,128)(2,1)}) custom-call(bf16[1024,2048]{1,0:T(8,128)(2,1)} %get-tuple-element.95.normed_hbm, bf16[2048,1024]{1,0:T(8,128)(2,1)} %get-tuple-element.96.turned_hbm, ...), custom_call_target="tpu_custom_call", output_to_operand_aliasing={{2}: (6, {})} | custom-call | flops 17179869184 | bytes 33554432 | tf_op jit(solution)/shard_map/feed/pallas_call | solution.py:603
  176.7 15.2 %pull.1 = (bf16[512,2048]{1,0:T(8,128)(2,1)}, bf16[512,2048]{1,0:T(8,128)(2,1)}, f32[1,2048]{1,0:T(1,128)}, f32[1,2048]{1,0:T(1,128)}, f32[1,1024]{1,0:T(1,128)}, /*index=5*/f32[1,768]{1,0:T(1,128)}) custom-call(bf16[1024,1024]{1,0:T(8,128)(2,1)} %get-tuple-element.103.grad_ref, bf16[1024,768]{1,0:T(8,128)(2,1)} %get-tuple-element.104.merged_ref, ...), custom_call_target="tpu_custom_call" | custom-call | flops 7516192768 | bytes 16777216 | tf_op jit(solution)/shard_map/pull/pallas_call | solution.py:690
  199.1 2.8 collective-permute-start.23
  202.0 11.1 %branch.1 = (bf16[512,2048]{1,0:T(8,128)(2,1)}, bf16[512,2048]{1,0:T(8,128)(2,1)}) custom-call(bf16[1024,256]{1,0:T(8,128)(2,1)} %get-tuple-element.100.context_ref, bf16[16,384,1024]{2,1,0:T(8,128)(2,1)} %bitcast.138, bf16[1024,1024]{1,0:T(8,128)(2,1)} %get-tuple-element.108.act_ref, bf16[16,384,1024]{2,1,0:T(8,128)(2,1)} %bitcast.139), custom_call_target="tpu_custom_call" | custom-call | flops 5368709120 | bytes 12582912 | tf_op jit(solution)/shard_map/branch/pallas_call | solution.py:647
  215.1 2.6 convert_add_fusion.4
  218.9 2.3 collective-permute-start.28
  221.2 2.4 collective-permute-start.25
  223.9 1.9 collective-permute-done.25
  225.8 1.9 collective-permute-done.27
  229.6 2.3 collective-permute-start.33
  232.8 3.0 convert_add_fusion.2
  236.6 2.7 collective-permute-start.31
  243.1 8.5 %collective-permute-done.30 = bf16[64,2048]{1,0:T(8,128)(2,1)} collective-permute-done((bf16[64,2048]{1,0:T(8,128)(2,1)}, bf16[64,2048]{1,0:T(8,128)(2,1)}, u32[]{:S(2)}, u32[]{:S(2)}) %collective-permute-start.30) | collective-permute-done | bytes 262176 | tf_op jit(solution)/shard_map/ppermute | solution.py:29
  251.6 1.9 fusion.36
  260.5 2.5 collective-permute-start.34
  263.0 1.6 collective-permute-done.34
  264.6 3.6 %collective-permute-done.36 = bf16[128,2048]{1,0:T(8,128)(2,1)} collective-permute-done((bf16[128,2048]{1,0:T(8,128)(2,1)}, bf16[128,2048]{1,0:T(8,128)(2,1)}, u32[]{:S(2)}, u32[]{:S(2)}) %collective-permute-start.36) | collective-permute-done | bytes 524320 | tf_op jit(solution)/shard_map/ppermute | solution.py:29
  268.2 3.1 collective-permute-done.35
  274.3 4.4 %collective-permute-start.38 = (f32[1,320]{1,0:T(1,128)S(1)}, f32[1,320]{1,0:T(1,128)S(1)}, u32[]{:S(2)}, u32[]{:S(2)}) collective-permute-start(f32[1,320]{1,0:T(1,128)S(1)} %constant_dynamic-slice_fusion.1), channel_id=1, source_target_pairs={{0,2},{2,0},{1,3},{3,1},{4,6},{6,4},{5,7},{7,5},{8,10},{10,8},{9,1... | collective-permute-start | bytes 3848 | tf_op jit(solution)/shard_map/ppermute | solution.py:94
  279.7 2.8 fusion.9
  283.8 2.1 sort.1
  287.9 4.3 %collective-permute-start.44 = (bf16[16,2048]{1,0:T(8,128)(2,1)}, bf16[16,2048]{1,0:T(8,128)(2,1)S(1)}, u32[]{:S(2)}, u32[]{:S(2)}) collective-permute-start(bf16[16,2048]{1,0:T(8,128)(2,1)} %get-tuple-element.139), channel_id=1, source_target_pairs={{0,0},{4,1},{8,2},{12,3},{16,4},{20,5},{24,6},{28,7},{32,8},{36,9}... | collective-permute-start | bytes 196616 | tf_op jit(solution)/shard_map/ppermute | solution.py:120
  295.2 1.9 collective-permute-start.45
  297.1 1.9 fusion.15
  299.6 2.1 collective-permute-start.43
  304.0 9.8 %collective-permute-done.41.refs_1_ = bf16[2,64,1024]{2,1,0:T(8,128)(2,1)S(1)} collective-permute-done((bf16[2,64,1024]{2,1,0:T(8,128)(2,1)S(1)}, bf16[2,64,1024]{2,1,0:T(8,128)(2,1)S(1)}, u32[]{:S(2)}, u32[]{:S(2)}) %collective-permute-start.41) | collective-permute-done | bytes 262176 | tf_op jit(solution)/shard_map/ppermute | solution.py:29
  314.8 2.8 spread.1
  (275 shorter events, 65.0 us)
Async XLA Ops:
  7.2 112.1 %all-gather.3.cloned.1.call-start = ((), (), s32[]{:S(2)}) async-start(), calls=%async_computation.2 | async-start | bytes 13369344 | tf_op jit(solution)/shard_map/all_gather | solution.py:81
  11.2 12.6 %collective-permute-start.1 = (bf16[32,1792]{1,0:T(8,128)(2,1)S(1)}, bf16[32,1792]{1,0:T(8,128)(2,1)S(1)}, u32[]{:S(2)}, u32[]{:S(2)}) collective-permute-start(bf16[32,1792]{1,0:T(8,128)(2,1)S(1)} %get-tuple-element.191), channel_id=1, source_target_pairs={{0,64},{2,66},{64,0},{66,2},{1,65},{3,67},{65,1},{67,3},{4,68},{6,... | collective-permute-start | bytes 344072 | tf_op jit(solution)/shard_map/ppermute | solution.py:68
  14.8 9.0 %collective-permute-start.2 = (bf16[32,1792]{1,0:T(8,128)(2,1)S(1)}, bf16[32,1792]{1,0:T(8,128)(2,1)S(1)}, u32[]{:S(2)}, u32[]{:S(2)}) collective-permute-start(bf16[32,1792]{1,0:T(8,128)(2,1)S(1)} %get-tuple-element.190), channel_id=1, source_target_pairs={{0,66},{2,64},{64,2},{66,0},{1,67},{3,65},{65,3},{67,1},{4,70},{6,... | collective-permute-start | bytes 344072 | tf_op jit(solution)/shard_map/ppermute | solution.py:68
  15.8 8.0 %collective-permute-start = (bf16[32,1792]{1,0:T(8,128)(2,1)S(1)}, bf16[32,1792]{1,0:T(8,128)(2,1)S(1)}, u32[]{:S(2)}, u32[]{:S(2)}) collective-permute-start(bf16[32,1792]{1,0:T(8,128)(2,1)S(1)} %get-tuple-element.192), channel_id=1, source_target_pairs={{0,2},{2,0},{64,66},{66,64},{1,3},{3,1},{65,67},{67,65},{4,6},{6,4... | collective-permute-start | bytes 344072 | tf_op jit(solution)/shard_map/ppermute | solution.py:68
  15.8 7.9 %collective-permute-start.3 = (bf16[16,2048]{1,0:T(8,128)(2,1)S(1)}, bf16[16,2048]{1,0:T(8,128)(2,1)S(1)}, u32[]{:S(2)}, u32[]{:S(2)}) collective-permute-start(bf16[16,2048]{1,0:T(8,128)(2,1)S(1)} %constant_dynamic-slice_fusion.13), channel_id=1, source_target_pairs={{0,0},{1,4},{2,8},{3,12},{4,16},{5,20},{6,24},{7,28},{8,32},{9,36}... | collective-permute-start | bytes 196616 | tf_op jit(solution)/shard_map/ppermute | solution.py:120
  25.1 258.7 %reduce-scatter.2.cloned.1.call-start = ((), (), s32[]{:S(2)}) async-start(), calls=%async_computation.1 | async-start | bytes 13369344 | tf_op jit(solution)/shard_map/reduce_scatter | solution.py:86
  26.8 14.8 %collective-permute-start.5 = (bf16[128,2048]{1,0:T(8,128)(2,1)}, bf16[128,2048]{1,0:T(8,128)(2,1)S(1)}, u32[]{:S(2)}, u32[]{:S(2)}) collective-permute-start(bf16[128,2048]{1,0:T(8,128)(2,1)} %copy.63), channel_id=1, source_target_pairs={{0,1},{1,64},{64,65},{65,0},{2,3},{3,66},{66,67},{67,2},{4,5},{5,6... | collective-permute-start | bytes 1572872 | tf_op jit(solution)/shard_map/ppermute | solution.py:29
  29.5 13.5 %collective-permute-start.6 = (bf16[128,2048]{1,0:T(8,128)(2,1)}, bf16[128,2048]{1,0:T(8,128)(2,1)S(1)}, u32[]{:S(2)}, u32[]{:S(2)}) collective-permute-start(bf16[128,2048]{1,0:T(8,128)(2,1)} %copy.63), channel_id=1, source_target_pairs={{0,65},{1,0},{64,1},{65,64},{2,67},{3,2},{66,3},{67,66},{4,69},{5,... | collective-permute-start | bytes 1572872 | tf_op jit(solution)/shard_map/ppermute | solution.py:29
  43.0 4.0 %collective-permute-start.7 = (bf16[2,352]{1,0:T(2,128)(2,1)S(1)}, bf16[2,352]{1,0:T(2,128)(2,1)S(1)}, u32[]{:S(2)}, u32[]{:S(2)}) collective-permute-start(bf16[2,352]{1,0:T(2,128)(2,1)S(1)} %pad_maximum_fusion.15), channel_id=1, source_target_pairs={{0,4},{4,0},{8,12},{12,8},{1,5},{5,1},{9,13},{13,9},{2,6},{6,2},{1... | collective-permute-start | bytes 4232 | tf_op jit(solution)/shard_map/ppermute | solution.py:94
  44.1 9.1 %collective-permute-start.8 = (bf16[64,2048]{1,0:T(8,128)(2,1)S(1)}, bf16[64,2048]{1,0:T(8,128)(2,1)S(1)}, u32[]{:S(2)}, u32[]{:S(2)}) collective-permute-start(bf16[64,2048]{1,0:T(8,128)(2,1)S(1)} %slice.213), channel_id=1, source_target_pairs={{0,1},{1,64},{64,65},{65,0},{2,3},{3,66},{66,67},{67,2},{4,5},{5,6... | collective-permute-start | bytes 786440 | tf_op jit(solution)/shard_map/ppermute | solution.py:29
  45.5 7.7 %collective-permute-start.9 = (bf16[64,2048]{1,0:T(8,128)(2,1)S(1)}, bf16[64,2048]{1,0:T(8,128)(2,1)S(1)}, u32[]{:S(2)}, u32[]{:S(2)}) collective-permute-start(bf16[64,2048]{1,0:T(8,128)(2,1)S(1)} %slice.214), channel_id=1, source_target_pairs={{0,65},{1,0},{64,1},{65,64},{2,67},{3,2},{66,3},{67,66},{4,69},{5,... | collective-permute-start | bytes 786440 | tf_op jit(solution)/shard_map/ppermute | solution.py:29
  53.2 13.6 %collective-permute-start.12 = (bf16[128,2048]{1,0:T(8,128)(2,1)S(1)}, bf16[128,2048]{1,0:T(8,128)(2,1)S(1)}, u32[]{:S(2)}, u32[]{:S(2)}) collective-permute-start(bf16[128,2048]{1,0:T(8,128)(2,1)S(1)} %bitcast.144), channel_id=1, source_target_pairs={{0,1},{1,64},{64,65},{65,0},{2,3},{3,66},{66,67},{67,2},{4,5},{5,6... | collective-permute-start | bytes 1572872 | tf_op jit(solution)/shard_map/ppermute | solution.py:29
  53.4 13.4 %collective-permute-start.13 = (bf16[128,2048]{1,0:T(8,128)(2,1)S(1)}, bf16[128,2048]{1,0:T(8,128)(2,1)S(1)}, u32[]{:S(2)}, u32[]{:S(2)}) collective-permute-start(bf16[128,2048]{1,0:T(8,128)(2,1)S(1)} %bitcast.145), channel_id=1, source_target_pairs={{0,65},{1,0},{64,1},{65,64},{2,67},{3,2},{66,3},{67,66},{4,69},{5,... | collective-permute-start | bytes 1572872 | tf_op jit(solution)/shard_map/ppermute | solution.py:29
  55.9 6.8 %collective-permute-start.11 = (bf16[4,352]{1,0:T(4,128)(2,1)S(1)}, bf16[4,352]{1,0:T(4,128)(2,1)S(1)}, u32[]{:S(2)}, u32[]{:S(2)}) collective-permute-start(bf16[4,352]{1,0:T(4,128)(2,1)S(1)} %pad_maximum_fusion.14), channel_id=1, source_target_pairs={{0,8},{4,12},{8,0},{12,4},{1,9},{5,13},{9,1},{13,5},{2,10},{6,14},... | collective-permute-start | bytes 8456 | tf_op jit(solution)/shard_map/ppermute | solution.py:94
  60.6 40.0 %collective-permute-start.10 = (bf16[512,2048]{1,0:T(8,128)(2,1)S(1)}, bf16[512,2048]{1,0:T(8,128)(2,1)}, u32[]{:S(2)}, u32[]{:S(2)}) collective-permute-start(bf16[512,2048]{1,0:T(8,128)(2,1)S(1)} %constant_dynamic-update-slice_fusion.near_ref.hid_near_ref), channel_id=1, source_target_pairs={{0,2},{2,0},{1,3},{3,1},{4,6},{6,4},{5,7},{7,5},{8,10},{10,8},{9,1... | collective-permute-start | bytes 6291464 | tf_op jit(solution)/shard_map/ppermute | solution.py:29
  66.8 7.2 %collective-permute-start.15 = (bf16[64,2048]{1,0:T(8,128)(2,1)S(1)}, bf16[64,2048]{1,0:T(8,128)(2,1)S(1)}, u32[]{:S(2)}, u32[]{:S(2)}) collective-permute-start(bf16[64,2048]{1,0:T(8,128)(2,1)S(1)} %slice.215), channel_id=1, source_target_pairs={{0,1},{1,64},{64,65},{65,0},{2,3},{3,66},{66,67},{67,2},{4,5},{5,6... | collective-permute-start | bytes 786440 | tf_op jit(solution)/shard_map/ppermute | solution.py:29
  67.1 7.0 %collective-permute-start.16 = (bf16[64,2048]{1,0:T(8,128)(2,1)S(1)}, bf16[64,2048]{1,0:T(8,128)(2,1)S(1)}, u32[]{:S(2)}, u32[]{:S(2)}) collective-permute-start(bf16[64,2048]{1,0:T(8,128)(2,1)S(1)} %slice.216), channel_id=1, source_target_pairs={{0,65},{1,0},{64,1},{65,64},{2,67},{3,2},{66,3},{67,66},{4,69},{5,... | collective-permute-start | bytes 786440 | tf_op jit(solution)/shard_map/ppermute | solution.py:29
  69.7 3.0 collective-permute-start.14
  74.0 4.8 %collective-permute-start.18 = (s32[2,128]{1,0:T(2,128)S(1)}, s32[2,128]{1,0:T(2,128)S(1)}, u32[]{:S(2)}, u32[]{:S(2)}) collective-permute-start(s32[2,128]{1,0:T(2,128)S(1)} %pad_add_fusion.4), channel_id=1, source_target_pairs={{0,1},{1,0},{2,3},{3,2},{4,5},{5,4},{6,7},{7,6},{8,9},{9,8},{10,11... | collective-permute-start | bytes 3080 | tf_op jit(solution)/shard_map/ppermute | solution.py:29
  74.4 4.5 %collective-permute-start.17 = (bf16[16,352]{1,0:T(8,128)(2,1)S(1)}, bf16[16,352]{1,0:T(8,128)(2,1)S(1)}, u32[]{:S(2)}, u32[]{:S(2)}) collective-permute-start(bf16[16,352]{1,0:T(8,128)(2,1)S(1)} %pad_maximum_fusion.12), channel_id=1, source_target_pairs={{0,32},{16,48},{32,0},{48,16},{1,33},{17,49},{33,1},{49,17},{2,34}... | collective-permute-start | bytes 33800 | tf_op jit(solution)/shard_map/ppermute | solution.py:94
  78.9 9.0 %collective-permute-start.21 = (s32[2,2,128]{2,1,0:T(2,128)S(1)}, s32[2,2,128]{2,1,0:T(2,128)S(1)}, u32[]{:S(2)}, u32[]{:S(2)}) collective-permute-start(s32[2,2,128]{2,1,0:T(2,128)S(1)} %reverse_select_fusion.3), channel_id=1, source_target_pairs={{0,64},{64,0},{1,65},{65,1},{2,66},{66,2},{3,67},{67,3},{4,68},{68... | collective-permute-start | bytes 6152 | tf_op jit(solution)/shard_map/ppermute | solution.py:29
  83.1 25.3 %collective-permute-start.20 = (bf16[512,2048]{1,0:T(8,128)(2,1)}, bf16[512,2048]{1,0:T(8,128)(2,1)}, u32[]{:S(2)}, u32[]{:S(2)}) collective-permute-start(bf16[512,2048]{1,0:T(8,128)(2,1)} %constant_dynamic-update-slice_fusion.5.near_hbm), channel_id=1, source_target_pairs={{0,2},{2,0},{1,3},{3,1},{4,6},{6,4},{5,7},{7,5},{8,10},{10,8},{9,1... | collective-permute-start | bytes 6291464 | tf_op jit(solution)/shard_map/ppermute | solution.py:29
  87.9 4.0 %collective-permute-start.22 = (s32[4,2,128]{2,0,1:T(4,128)S(1)}, s32[4,2,128]{2,0,1:T(4,128)S(1)}, u32[]{:S(2)}, u32[]{:S(2)}) collective-permute-start(s32[4,2,128]{2,0,1:T(4,128)S(1)} %get-tuple-element.211), channel_id=1, source_target_pairs={{0,2},{2,0},{1,3},{3,1},{4,6},{6,4},{5,7},{7,5},{8,10},{10,8},{9,1... | collective-permute-start | bytes 12296 | tf_op jit(solution)/shard_map/ppermute | solution.py:29
  89.0 7.8 %collective-permute-start.19 = (bf16[32,352]{1,0:T(8,128)(2,1)S(1)}, bf16[32,352]{1,0:T(8,128)(2,1)S(1)}, u32[]{:S(2)}, u32[]{:S(2)}) collective-permute-start(bf16[32,352]{1,0:T(8,128)(2,1)S(1)} %pad_maximum_fusion.11), channel_id=1, source_target_pairs={{0,64},{64,0},{1,65},{65,1},{2,66},{66,2},{3,67},{67,3},{4,68},{68... | collective-permute-start | bytes 67592 | tf_op jit(solution)/shard_map/ppermute | solution.py:94
  191.9 21.8 %collective-permute-start.24 = (bf16[512,2048]{1,0:T(8,128)(2,1)}, bf16[512,2048]{1,0:T(8,128)(2,1)S(1)}, u32[]{:S(2)}, u32[]{:S(2)}) collective-permute-start(bf16[512,2048]{1,0:T(8,128)(2,1)} %get-tuple-element.114), channel_id=1, source_target_pairs={{0,2},{2,0},{1,3},{3,1},{4,6},{6,4},{5,7},{7,5},{8,10},{10,8},{9,1... | collective-permute-start | bytes 6291464 | tf_op jit(solution)/shard_map/ppermute | solution.py:29
  199.1 13.9 %collective-permute-start.23 = (f32[32,320]{1,0:T(8,128)S(1)}, f32[32,320]{1,0:T(8,128)S(1)}, u32[]{:S(2)}, u32[]{:S(2)}) collective-permute-start(f32[32,320]{1,0:T(8,128)S(1)} %dynamic-slice_bitcast_fusion.4), channel_id=1, source_target_pairs={{0,64},{64,0},{1,65},{65,1},{2,66},{66,2},{3,67},{67,3},{4,68},{68... | collective-permute-start | bytes 122888 | tf_op jit(solution)/shard_map/ppermute | solution.py:94
  213.7 14.0 %collective-permute-start.26 = (bf16[512,2048]{1,0:T(8,128)(2,1)}, bf16[512,2048]{1,0:T(8,128)(2,1)}, u32[]{:S(2)}, u32[]{:S(2)}) collective-permute-start(bf16[512,2048]{1,0:T(8,128)(2,1)} %get-tuple-element.116), channel_id=1, source_target_pairs={{0,2},{2,0},{1,3},{3,1},{4,6},{6,4},{5,7},{7,5},{8,10},{10,8},{9,1... | collective-permute-start | bytes 6291464 | tf_op jit(solution)/shard_map/ppermute | solution.py:29
  218.5 9.1 %collective-permute-start.27 = (bf16[64,2048]{1,0:T(8,128)(2,1)}, bf16[64,2048]{1,0:T(8,128)(2,1)S(1)}, u32[]{:S(2)}, u32[]{:S(2)}) collective-permute-start(bf16[64,2048]{1,0:T(8,128)(2,1)} %get-tuple-element.182), channel_id=1, source_target_pairs={{0,1},{1,64},{64,65},{65,0},{2,3},{3,66},{66,67},{67,2},{4,5},{5,6... | collective-permute-start | bytes 786440 | tf_op jit(solution)/shard_map/ppermute | solution.py:29
  218.9 8.8 %collective-permute-start.28 = (bf16[64,2048]{1,0:T(8,128)(2,1)}, bf16[64,2048]{1,0:T(8,128)(2,1)}, u32[]{:S(2)}, u32[]{:S(2)}) collective-permute-start(bf16[64,2048]{1,0:T(8,128)(2,1)} %get-tuple-element.181), channel_id=1, source_target_pairs={{0,65},{1,0},{64,1},{65,64},{2,67},{3,2},{66,3},{67,66},{4,69},{5,... | collective-permute-start | bytes 786440 | tf_op jit(solution)/shard_map/ppermute | solution.py:29
  221.2 4.6 %collective-permute-start.25 = (f32[16,320]{1,0:T(8,128)S(1)}, f32[16,320]{1,0:T(8,128)S(1)}, u32[]{:S(2)}, u32[]{:S(2)}) collective-permute-start(f32[16,320]{1,0:T(8,128)S(1)} %dynamic-slice_bitcast_fusion.5), channel_id=1, source_target_pairs={{0,32},{16,48},{32,0},{48,16},{1,33},{17,49},{33,1},{49,17},{2,34}... | collective-permute-start | bytes 61448 | tf_op jit(solution)/shard_map/ppermute | solution.py:94
  229.6 22.1 %collective-permute-start.33 = (bf16[128,2048]{1,0:T(8,128)(2,1)}, bf16[128,2048]{1,0:T(8,128)(2,1)S(1)}, u32[]{:S(2)}, u32[]{:S(2)}) collective-permute-start(bf16[128,2048]{1,0:T(8,128)(2,1)} %pad_maximum_fusion.4), channel_id=1, source_target_pairs={{0,65},{1,0},{64,1},{65,64},{2,67},{3,2},{66,3},{67,66},{4,69},{5,... | collective-permute-start | bytes 1572872 | tf_op jit(solution)/shard_map/ppermute | solution.py:29
  232.8 18.9 %collective-permute-start.32 = (bf16[128,2048]{1,0:T(8,128)(2,1)}, bf16[128,2048]{1,0:T(8,128)(2,1)}, u32[]{:S(2)}, u32[]{:S(2)}) collective-permute-start(bf16[128,2048]{1,0:T(8,128)(2,1)} %pad_maximum_fusion.3), channel_id=1, source_target_pairs={{0,1},{1,64},{64,65},{65,0},{2,3},{3,66},{66,67},{67,2},{4,5},{5,6... | collective-permute-start | bytes 1572872 | tf_op jit(solution)/shard_map/ppermute | solution.py:29
  236.6 15.0 %collective-permute-start.30 = (bf16[64,2048]{1,0:T(8,128)(2,1)}, bf16[64,2048]{1,0:T(8,128)(2,1)}, u32[]{:S(2)}, u32[]{:S(2)}) collective-permute-start(bf16[64,2048]{1,0:T(8,128)(2,1)} %get-tuple-element.180), channel_id=1, source_target_pairs={{0,1},{1,64},{64,65},{65,0},{2,3},{3,66},{66,67},{67,2},{4,5},{5,6... | collective-permute-start | bytes 786440 | tf_op jit(solution)/shard_map/ppermute | solution.py:29
  236.6 15.0 %collective-permute-start.31 = (bf16[64,2048]{1,0:T(8,128)(2,1)}, bf16[64,2048]{1,0:T(8,128)(2,1)}, u32[]{:S(2)}, u32[]{:S(2)}) collective-permute-start(bf16[64,2048]{1,0:T(8,128)(2,1)} %get-tuple-element.179), channel_id=1, source_target_pairs={{0,65},{1,0},{64,1},{65,64},{2,67},{3,2},{66,3},{67,66},{4,69},{5,... | collective-permute-start | bytes 786440 | tf_op jit(solution)/shard_map/ppermute | solution.py:29
  239.3 3.7 %collective-permute-start.29 = (f32[8,320]{1,0:T(8,128)S(1)}, f32[8,320]{1,0:T(8,128)S(1)}, u32[]{:S(2)}, u32[]{:S(2)}) collective-permute-start(f32[8,320]{1,0:T(8,128)S(1)} %dynamic-slice_bitcast_fusion.6), channel_id=1, source_target_pairs={{0,16},{16,0},{32,48},{48,32},{1,17},{17,1},{33,49},{49,33},{2,18}... | collective-permute-start | bytes 30728 | tf_op jit(solution)/shard_map/ppermute | solution.py:94
  257.1 11.1 %collective-permute-start.36 = (bf16[128,2048]{1,0:T(8,128)(2,1)}, bf16[128,2048]{1,0:T(8,128)(2,1)}, u32[]{:S(2)}, u32[]{:S(2)}) collective-permute-start(bf16[128,2048]{1,0:T(8,128)(2,1)} %pad_maximum_fusion.6), channel_id=1, source_target_pairs={{0,65},{1,0},{64,1},{65,64},{2,67},{3,2},{66,3},{67,66},{4,69},{5,... | collective-permute-start | bytes 1572872 | tf_op jit(solution)/shard_map/ppermute | solution.py:29
  259.0 12.3 %collective-permute-start.35 = (bf16[128,2048]{1,0:T(8,128)(2,1)}, bf16[128,2048]{1,0:T(8,128)(2,1)}, u32[]{:S(2)}, u32[]{:S(2)}) collective-permute-start(bf16[128,2048]{1,0:T(8,128)(2,1)} %pad_maximum_fusion.5), channel_id=1, source_target_pairs={{0,1},{1,64},{64,65},{65,0},{2,3},{3,66},{66,67},{67,2},{4,5},{5,6... | collective-permute-start | bytes 1572872 | tf_op jit(solution)/shard_map/ppermute | solution.py:29
  260.5 4.2 %collective-permute-start.34 = (f32[4,320]{1,0:T(4,128)S(1)}, f32[4,320]{1,0:T(4,128)S(1)}, u32[]{:S(2)}, u32[]{:S(2)}) collective-permute-start(f32[4,320]{1,0:T(4,128)S(1)} %fusion.25), channel_id=1, source_target_pairs={{0,8},{4,12},{8,0},{12,4},{1,9},{5,13},{9,1},{13,5},{2,10},{6,14},... | collective-permute-start | bytes 15368 | tf_op jit(solution)/shard_map/ppermute | solution.py:94
  271.3 2.9 collective-permute-start.37
  274.3 5.2 %collective-permute-start.38 = (f32[1,320]{1,0:T(1,128)S(1)}, f32[1,320]{1,0:T(1,128)S(1)}, u32[]{:S(2)}, u32[]{:S(2)}) collective-permute-start(f32[1,320]{1,0:T(1,128)S(1)} %constant_dynamic-slice_fusion.1), channel_id=1, source_target_pairs={{0,2},{2,0},{1,3},{3,1},{4,6},{6,4},{5,7},{7,5},{8,10},{10,8},{9,1... | collective-permute-start | bytes 3848 | tf_op jit(solution)/shard_map/ppermute | solution.py:94
  279.5 4.3 %collective-permute-start.39 = (f32[1,320]{1,0:T(1,128)S(1)}, f32[1,320]{1,0:T(1,128)S(1)}, u32[]{:S(2)}, u32[]{:S(2)}) collective-permute-start(f32[1,320]{1,0:T(1,128)S(1)} %fusion.29), channel_id=1, source_target_pairs={{0,1},{1,0},{2,3},{3,2},{4,5},{5,4},{6,7},{7,6},{8,9},{9,8},{10,11... | collective-permute-start | bytes 3848 | tf_op jit(solution)/shard_map/ppermute | solution.py:29
  285.9 2.0 collective-permute-start.40
  287.9 7.3 %collective-permute-start.44 = (bf16[16,2048]{1,0:T(8,128)(2,1)}, bf16[16,2048]{1,0:T(8,128)(2,1)S(1)}, u32[]{:S(2)}, u32[]{:S(2)}) collective-permute-start(bf16[16,2048]{1,0:T(8,128)(2,1)} %get-tuple-element.139), channel_id=1, source_target_pairs={{0,0},{4,1},{8,2},{12,3},{16,4},{20,5},{24,6},{28,7},{32,8},{36,9}... | collective-permute-start | bytes 196616 | tf_op jit(solution)/shard_map/ppermute | solution.py:120
  292.7 10.0 %collective-permute-start.46 = (bf16[64,2048]{1,0:T(8,128)(2,1)}, bf16[64,2048]{1,0:T(8,128)(2,1)S(1)}, u32[]{:S(2)}, u32[]{:S(2)}) collective-permute-start(bf16[64,2048]{1,0:T(8,128)(2,1)} %get-tuple-element.141), channel_id=1, source_target_pairs={{0,1},{1,0},{2,3},{3,2},{4,5},{5,4},{6,7},{7,6},{8,9},{9,8},{10,11... | collective-permute-start | bytes 786440 | tf_op jit(solution)/shard_map/ppermute | solution.py:29
  295.2 6.7 %collective-permute-start.45 = (bf16[16,2048]{1,0:T(8,128)(2,1)S(1)}, bf16[16,2048]{1,0:T(8,128)(2,1)S(1)}, u32[]{:S(2)}, u32[]{:S(2)}) collective-permute-start(bf16[16,2048]{1,0:T(8,128)(2,1)S(1)} %collective-permute-done.44), channel_id=1, source_target_pairs={{0,1},{1,0},{2,3},{3,2},{4,5},{5,4},{6,7},{7,6},{8,9},{9,8},{10,11... | collective-permute-start | bytes 196616 | tf_op jit(solution)/shard_map/ppermute | solution.py:29
  299.0 14.7 %collective-permute-start.41 = (bf16[2,64,1024]{2,1,0:T(8,128)(2,1)S(1)}, bf16[2,64,1024]{2,1,0:T(8,128)(2,1)S(1)}, u32[]{:S(2)}, u32[]{:S(2)}) collective-permute-start(bf16[2,64,1024]{2,1,0:T(8,128)(2,1)S(1)} %get-tuple-element.177), channel_id=1, source_target_pairs={{0,1},{1,64},{64,65},{65,0},{2,3},{3,66},{66,67},{67,2},{4,5},{5,6... | collective-permute-start | bytes 786440 | tf_op jit(solution)/shard_map/ppermute | solution.py:29
  299.0 14.7 %collective-permute-start.42 = (bf16[2,64,1024]{2,1,0:T(8,128)(2,1)S(1)}, bf16[2,64,1024]{2,1,0:T(8,128)(2,1)S(1)}, u32[]{:S(2)}, u32[]{:S(2)}) collective-permute-start(bf16[2,64,1024]{2,1,0:T(8,128)(2,1)S(1)} %get-tuple-element.178), channel_id=1, source_target_pairs={{0,64},{1,65},{64,0},{65,1},{2,66},{3,67},{66,2},{67,3},{4,68},{5,... | collective-permute-start | bytes 786440 | tf_op jit(solution)/shard_map/ppermute | solution.py:29
  299.6 14.5 %collective-permute-start.43 = (bf16[2,64,1024]{2,1,0:T(8,128)(2,1)S(1)}, bf16[2,64,1024]{2,1,0:T(8,128)(2,1)S(1)}, u32[]{:S(2)}, u32[]{:S(2)}) collective-permute-start(bf16[2,64,1024]{2,1,0:T(8,128)(2,1)S(1)} %get-tuple-element.175), channel_id=1, source_target_pairs={{0,65},{1,0},{64,1},{65,64},{2,67},{3,2},{66,3},{67,66},{4,69},{5,... | collective-permute-start | bytes 786440 | tf_op jit(solution)/shard_map/ppermute | solution.py:29
  (32 other events, 240.6 us)
Sparse Core Ops, SparseCore 0:
  25.2 94.0 all-gather.2
  176.8 94.3 reduce-scatter.1

commit v3 on v2

--- a/solution.py
+++ b/solution.py
@@ -37,6 +37,10 @@
     return lax.optimization_barrier(values)
 
 
+def across(value, step):
+    return lax.ppermute(value, ("xh", "xl"), [(i, i ^ step) for i in range(4)])
+
+
 def ring_first(value):
     return shift(value, "x", 1), shift(value, "x", -1)
 
@@ -108,20 +112,16 @@
     return pick(parts, mine) + toward(pick(parts, 1 - mine), axis, bit)
 
 
-def rehome(value, back=False):
+def rehome(value, back=False, other=False):
     pairs = []
     for z in range(4):
         for y in range(4):
             for core in range(2):
                 for xl in range(2):
-                    owner = ((z * 4 + y) * 2 + core) * 2 + xl
+                    owner = ((z * 4 + y) * 2 + core) * 2 + (xl ^ 1 if other else xl)
                     user = ((y * 4 + 2 * core + xl) * 2 + z // 2) * 2 + z % 2
                     pairs.append((user, owner) if back else (owner, user))
     return lax.ppermute(value, ("z", "y", "core", "xl"), pairs)
-
-
-def after(value, *others):
-    return lax.optimization_barrier((value, *others))[0]
 
 
 def owner_order(vector):
@@ -181,70 +181,85 @@
 
 
 def spread_body(place_ref, *refs):
-    pieces, up_ref, qkv_ref, held = refs[:4], refs[4], refs[5], refs[6]
-    place, core = place_ref[0], place_ref[1]
+    pieces, other_ref, down_own, proj_refs = refs[:4], refs[4], refs[5], refs[6:8]
+    up_ref, qkv_ref, down_ref, proj_ref, held = refs[8:]
+    place, core, xl = place_ref[0], place_ref[1], place_ref[2]
     for step in range(4):
-        source = lax.rem(place - step + 4, 4)
-        for side in range(2):
-            held[source, core ^ side] = pieces[step][side]
+        held[place ^ step, core] = pieces[step][:64]
+        held[place ^ step, 1 - core] = other_ref[step]
+    rows = pl.ds(pl.multiple_of(xl * 64, 64), 64)
+    down_ref[rows, :1024] = down_own[:64].astype(F32)
+    down_ref[rows, 1024:] = down_own[64:].astype(F32)
+    rows = pl.ds(pl.multiple_of((1 - xl) * 64, 64), 64)
+    down_ref[rows, :1024] = pieces[1][128:192].astype(F32)
+    down_ref[rows, 1024:] = pieces[1][192:].astype(F32)
+    for side in range(2):
+        start = pl.multiple_of((xl ^ side) * 16, 16)
+        proj_ref[pl.ds(start, 16), :] = proj_refs[side][...].astype(F32)
     for xh in range(2):
         for unit in range(16):
-            for core in range(2):
+            for side in range(2):
                 block = [
-                    held[2 * xh + xl, core, :32, unit * 64 : (unit + 1) * 64].astype(F32) for xl in range(2)
+                    held[2 * xh + x, side, :32, unit * 64 : (unit + 1) * 64].astype(F32) for x in range(2)
                 ]
-                start = xh * 4096 + unit * 256 + core * 128
+                start = xh * 4096 + unit * 256 + side * 128
                 up_ref[:, start : start + 128] = jnp.concatenate(block, axis=1)
-        for core in range(2):
-            for xl in range(2):
+        for side in range(2):
+            for x in range(2):
                 for block in range(3):
-                    start = block * D + xh * 1024 + core * 512 + xl * 256
+                    start = block * D + xh * 1024 + side * 512 + x * 256
                     qkv_ref[:, start : start + 256] = held[
-                        2 * xh + xl, core, 32:, block * 256 : (block + 1) * 256
+                        2 * xh + x, side, 32:, block * 256 : (block + 1) * 256
                     ].astype(F32)
 
 
-def spread(place, core, pieces):
+def spread(scalars, pieces, other, down, proj):
     vmem = pl.BlockSpec(memory_space=pltpu.VMEM)
     return pl.pallas_call(
         spread_body,
-        in_specs=[pl.BlockSpec(memory_space=pltpu.SMEM)] + [vmem] * 4,
-        out_specs=[vmem] * 2,
-        out_shape=[jax.ShapeDtypeStruct((32, FF), F32), jax.ShapeDtypeStruct((32, 3 * D), F32)],
+        in_specs=[pl.BlockSpec(memory_space=pltpu.SMEM)] + [vmem] * 8,
+        out_specs=[vmem] * 4,
+        out_shape=[
+            jax.ShapeDtypeStruct((32, FF), F32),
+            jax.ShapeDtypeStruct((32, 3 * D), F32),
+            jax.ShapeDtypeStruct((128, D), F32),
+            jax.ShapeDtypeStruct((32, D), F32),
+        ],
         scratch_shapes=[pltpu.VMEM((4, 2, 64, 1024), BF)],
         name="spread",
-    )(jnp.stack([place, core]).astype(jnp.int32), *pieces)
-
-
-def sort_body(core_ref, in_ref, near_ref, far_ref, down_ref, proj_ref):
-    core = core_ref[0]
-    for xh in range(2):
-        for ref, which in ((near_ref, core), (far_ref, 1 - core)):
-            start = pl.multiple_of(xh * 64 + which * 32, 32)
-            ref[xh, :32] = in_ref[pl.ds(start, 32), :]
-            ref[xh, 32:] = in_ref[pl.ds(pl.multiple_of(start + 256, 32), 32), :]
-    down_ref[:, :1024] = in_ref[128:192, :]
-    down_ref[:, 1024:] = in_ref[192:256, :]
+    )(scalars, *pieces, other, down, *proj)
+
+
+def sort_body(place_ref, in_ref, *refs):
+    down_ref, proj_ref = refs[4], refs[5]
+    place, core = place_ref[0], place_ref[1]
+    for step in range(4):
+        xh = lax.div(place ^ step, 2)
+        for side in range(2):
+            start = pl.multiple_of(xh * 64 + (core ^ side) * 32, 32)
+            at = side * 64
+            refs[step][at : at + 32] = in_ref[pl.ds(start, 32), :]
+            refs[step][at + 32 : at + 64] = in_ref[pl.ds(pl.multiple_of(start + 256, 32), 32), :]
+    refs[1][128:] = in_ref[128:256, :]
+    down_ref[...] = in_ref[128:256, :]
     for block in range(8):
         proj_ref[:, block * 256 : (block + 1) * 256] = in_ref[
             256 + block * 16 : 272 + block * 16, 768:
         ]
 
 
-def sort(core, summed):
+def sort(scalars, summed):
     vmem = pl.BlockSpec(memory_space=pltpu.VMEM)
     return pl.pallas_call(
         sort_body,
         in_specs=[pl.BlockSpec(memory_space=pltpu.SMEM), vmem],
-        out_specs=[vmem] * 4,
+        out_specs=[vmem] * 6,
         out_shape=[
-            jax.ShapeDtypeStruct((2, 64, 1024), BF),
-            jax.ShapeDtypeStruct((2, 64, 1024), BF),
-            jax.ShapeDtypeStruct((64, D), BF),
-            jax.ShapeDtypeStruct((16, D), BF),
-        ],
+            jax.ShapeDtypeStruct((256 if step == 1 else 128, 1024), BF) for step in range(4)
+        ]
+        + [jax.ShapeDtypeStruct((128, 1024), BF), jax.ShapeDtypeStruct((16, D), BF)],
         name="sort",
-    )(core.reshape(1).astype(jnp.int32), summed)
+    )(scalars, summed)
 
 
 def norm_body(near_ref, far_ref, gain_ref, shift_ref, normed_ref, turned_ref, mean_ref, rstd_ref):
@@ -286,10 +301,12 @@
     )(near, far, gain.reshape(1, D), shift_row.reshape(1, D))
 
 
-def heads_body(odd_ref, normed_hbm, turned_hbm, near_hbm, far_hbm, weights_hbm, bias_ref, cos_hbm,
-               sin1_hbm, sin2_hbm, row_ref, col_hbm, ctx_hbm, out_hbm, pack_hbm,
-               cos_ref, sin1_ref, sin2_ref, col_ref, normed, turned, cot, ctx_ref, out_ref, weights, proj, merged, queries, keys, values, grads, mask, raw, pulled,
-               probs, slopes, back_q, back_k, packed, sem, out_sems):
+def work_body(odd_ref, normed_hbm, turned_hbm, near_hbm, far_hbm, weights_hbm, bias_ref, up_bias_ref,
+              cos_hbm, sin1_hbm, sin2_hbm, row_ref, col_hbm, ctx_hbm, out_hbm, act_hbm, grad_hbm, pack_hbm,
+              cos_ref, sin1_ref, sin2_ref, col_ref, normed, turned, cot, ctx_ref, out_ref, weights, proj, merged, queries, keys, values, grads, mask, raw, pulled,
+               probs, slopes, back_q, back_k, packed, sem, out_sems,
+              up, down, act, units, upper_ref, slope_ref, up_out, down_out,
+              act_sems, grad_sems, up_sems, down_sems):
     width = 4 * HD
     half = ROT // 2
     loads = [
@@ -305,6 +322,10 @@
     ]
     for place in (0, 1, 5, 6, 7, 8, 2, 3, 4):
         loads[place].start()
+    up_load = pltpu.make_async_copy(weights_hbm.at[:, pl.ds(0, 128), :], up, sem.at[9])
+    down_load = pltpu.make_async_copy(weights_hbm.at[:, pl.ds(128, 128), :], down, sem.at[10])
+    up_load.start()
+    down_load.start()
     odd = odd_ref[0]
     for k in range(2):
         probs[k, :128, 128:] = jnp.zeros((128, 128), BF)
@@ -437,6 +458,85 @@
         packed[pl.ds(step * 2, 2), :, :768] = total.reshape(2, 128, 768)
         store(step).start()
 
+    def act_store(step):
+        rows = pl.ds(pl.multiple_of(step * 256, 256), 256)
+        return pltpu.make_async_copy(act.at[rows, :], act_hbm.at[rows, :], act_sems.at[step])
+
+    def grad_store(step):
+        rows = pl.ds(pl.multiple_of(step * 256, 256), 256)
+        return pltpu.make_async_copy(units.at[rows, :], grad_hbm.at[rows, :], grad_sems.at[step])
+
+    def up_store(step):
+        owners = pl.ds(step * 2, 2)
+        return pltpu.make_async_copy(
+            up_out.at[owners], pack_hbm.at[owners, pl.ds(0, 128), :], up_sems.at[step]
+        )
+
+    def down_store(step):
+        owners = pl.ds(step * 4, 4)
+        return pltpu.make_async_copy(
+            down_out.at[owners], pack_hbm.at[owners, pl.ds(128, 128), :], down_sems.at[step]
+        )
+
+    root = math.sqrt(2.0 / math.pi)
+    up_load.wait()
+
+    @pl.loop(0, 4)
+    def _(step):
+        rows = pl.ds(pl.multiple_of(step * 256, 256), 256)
+        upper_ref[rows, :] = dot(normed[rows, :], up[...].reshape(D, 1024)) + up_bias_ref[...]
+
+    down_load.wait()
+
+    @pl.loop(0, 4)
+    def _(step):
+        rows = pl.ds(pl.multiple_of(step * 256, 256), 256)
+        slope_ref[...] = dot_cols(cot[rows, :1024], down[:, :64].reshape(1024, 1024)) + dot_cols(
+            cot[rows, 1024:], down[:, 64:].reshape(1024, 1024)
+        )
+
+        @pl.loop(0, 16)
+        def _(part):
+            here = pl.ds(pl.multiple_of(part * 16, 16), 16)
+            there = pl.ds(pl.multiple_of(step * 256 + part * 16, 16), 16)
+            for side in range(2):
+                lanes = slice(side * 512, side * 512 + 512)
+                upper = upper_ref[there, lanes]
+                square = upper * upper
+                bend = jnp.tanh(upper * (root + (root * 0.044715) * square))
+                half = 0.5 + 0.5 * bend
+                slope = half + upper * (0.5 - 0.5 * (bend * bend)) * (root + (root * 3 * 0.044715) * square)
+                act[there, lanes] = (upper * half).astype(BF)
+                units[there, lanes] = (slope_ref[here, lanes] * slope).astype(BF)
+
+        act_store(step).start()
+        grad_store(step).start()
+
+    @pl.loop(0, 8)
+    def _(step):
+        rows = pl.ds(pl.multiple_of(step * 256, 256), 256)
+        total = dot(turned[rows, :], units[...]).astype(BF)
+        up_out[pl.ds(step * 2, 2)] = total.reshape(2, 128, 1024)
+        up_store(step).start()
+
+    @pl.loop(0, 4)
+    def _(step):
+        lanes = pl.ds(pl.multiple_of(step * 256, 256), 256)
+        total = dot_rows(act[:, lanes], cot[...]).astype(BF)
+        down_out[pl.ds(step * 4, 4), :64] = total[:, :1024].reshape(4, 64, 1024)
+        down_out[pl.ds(step * 4, 4), 64:] = total[:, 1024:].reshape(4, 64, 1024)
+        down_store(step).start()
+
+    @pl.loop(0, 4)
+    def _(step):
+        act_store(step).wait()
+        grad_store(step).wait()
+        down_store(step).wait()
+
+    @pl.loop(0, 8)
+    def _(step):
+        up_store(step).wait()
+
     ctx_store.wait()
     out_store.wait()
 
@@ -445,20 +545,28 @@
         store(step).wait()
 
 
-def heads(odd, normed, turned, near, far, weights, bias, cosine, sin1, sin2, segment):
+def work(odd, normed, turned, near, far, weights, bias, up_bias, cosine, sin1, sin2, segment):
     blocks = segment.reshape(2, 4, 128)
     rows = jnp.where(odd == 0, blocks, jnp.roll(blocks, 1, axis=1)).reshape(4, 1, SEQ)
     vmem, hbm = pl.BlockSpec(memory_space=pltpu.VMEM), pl.BlockSpec(memory_space=pltpu.HBM)
     table = pltpu.VMEM((TOKENS, 128), F32)
     head_b = pltpu.VMEM((2, TOKENS, 128), BF)
     head_f = pltpu.VMEM((SEQ, 128), F32)
+    slab = pltpu.VMEM((16, 128, 1024), BF)
+    square = pltpu.VMEM((TOKENS, 1024), BF)
     return pl.pallas_call(
-        heads_body,
-        in_specs=[pl.BlockSpec(memory_space=pltpu.SMEM)] + [hbm] * 5 + [vmem] + [hbm] * 3 + [vmem, hbm],
-        out_specs=[hbm] * 3,
+        work_body,
+        in_specs=[pl.BlockSpec(memory_space=pltpu.SMEM)]
+        + [hbm] * 5
+        + [vmem] * 2
+        + [hbm] * 3
+        + [vmem, hbm],
+        out_specs=[hbm] * 5,
         out_shape=[
             jax.ShapeDtypeStruct((TOKENS, 4 * HD), BF),
             jax.ShapeDtypeStruct((TOKENS, 12 * HD), BF),
+            jax.ShapeDtypeStruct((TOKENS, 1024), BF),
+            jax.ShapeDtypeStruct((TOKENS, 1024), BF),
             jax.ShapeDtypeStruct((16, 384, 1024), BF),
         ],
         scratch_shapes=[
@@ -471,7 +579,7 @@
             pltpu.VMEM((TOKENS, D), BF),
             pltpu.VMEM((TOKENS, 4 * HD), BF),
             pltpu.VMEM((TOKENS, 12 * HD), BF),
-            pltpu.VMEM((16, 128, 1024), BF),
+            slab,
             pltpu.VMEM((256, D), BF),
             pltpu.VMEM((256, 12 * HD), F32),
             head_b,
@@ -485,144 +593,17 @@
             pltpu.VMEM((2, SEQ, SEQ), BF),
             head_f,
             head_f,
-            pltpu.VMEM((16, 128, 1024), BF),
-            pltpu.SemaphoreType.DMA((9,)),
+            slab,
+            pltpu.SemaphoreType.DMA((11,)),
             pltpu.SemaphoreType.DMA((8,)),
-        ],
-        compiler_params=pltpu.CompilerParams(vmem_limit_bytes=VMEM),
-        cost_estimate=pl.CostEstimate(
-            flops=14 << 30, bytes_accessed=40 << 20, transcendentals=16 * SEQ * SEQ
-        ),
-        name="heads",
-    )(
-        odd.reshape(1), normed, turned, near, far, weights, bias, cosine, sin1, sin2, rows,
-        segment.reshape(TOKENS, 1),
-    )
-
-
-def feed_body(normed_hbm, turned_hbm, near_hbm, far_hbm, weights_hbm, bias_ref, pack_in,
-              act_hbm, grad_hbm, pack_hbm,
-              normed, turned, cot, up, down, act, grads, upper_ref, slope_ref, up_out, down_out,
-              sems, act_sems, grad_sems, up_sems, down_sems):
-    up_load = pltpu.make_async_copy(weights_hbm.at[:, pl.ds(0, 128), :], up, sems.at[0])
-    down_load = pltpu.make_async_copy(weights_hbm.at[:, pl.ds(128, 128), :], down, sems.at[1])
-    normed_load = pltpu.make_async_copy(normed_hbm, normed, sems.at[2])
-    near_load = pltpu.make_async_copy(near_hbm, cot.at[pl.ds(0, 512)], sems.at[3])
-    far_load = pltpu.make_async_copy(far_hbm, cot.at[pl.ds(512, 512)], sems.at[4])
-    turned_load = pltpu.make_async_copy(turned_hbm, turned, sems.at[5])
-    for load in (up_load, normed_load, down_load, near_load, far_load, turned_load):
-        load.start()
-
-    def act_store(step):
-        rows = pl.ds(pl.multiple_of(step * 256, 256), 256)
-        return pltpu.make_async_copy(act.at[rows, :], act_hbm.at[rows, :], act_sems.at[step])
-
-    def grad_store(step):
-        rows = pl.ds(pl.multiple_of(step * 256, 256), 256)
-        return pltpu.make_async_copy(grads.at[rows, :], grad_hbm.at[rows, :], grad_sems.at[step])
-
-    def up_store(step):
-        owners = pl.ds(step * 2, 2)
-        return pltpu.make_async_copy(
-            up_out.at[owners], pack_hbm.at[owners, pl.ds(0, 128), :], up_sems.at[step]
-        )
-
-    def down_store(step):
-        owners = pl.ds(step * 4, 4)
-        return pltpu.make_async_copy(
-            down_out.at[owners], pack_hbm.at[owners, pl.ds(128, 128), :], down_sems.at[step]
-        )
-
-    root = math.sqrt(2.0 / math.pi)
-    up_load.wait()
-    normed_load.wait()
-
-    @pl.loop(0, 4)
-    def _(step):
-        rows = pl.ds(pl.multiple_of(step * 256, 256), 256)
-        upper_ref[rows, :] = dot(normed[rows, :], up[...].reshape(D, 1024)) + bias_ref[...]
-
-    down_load.wait()
-    near_load.wait()
-    far_load.wait()
-
-    @pl.loop(0, 4)
-    def _(step):
-        rows = pl.ds(pl.multiple_of(step * 256, 256), 256)
-        slope_ref[...] = dot_cols(cot[rows, :1024], down[:, :64].reshape(1024, 1024)) + dot_cols(
-            cot[rows, 1024:], down[:, 64:].reshape(1024, 1024)
-        )
-
-        @pl.loop(0, 16)
-        def _(part):
-            here = pl.ds(pl.multiple_of(part * 16, 16), 16)
-            there = pl.ds(pl.multiple_of(step * 256 + part * 16, 16), 16)
-            for side in range(2):
-                lanes = slice(side * 512, side * 512 + 512)
-                upper = upper_ref[there, lanes]
-                square = upper * upper
-                bend = jnp.tanh(upper * (root + (root * 0.044715) * square))
-                half = 0.5 + 0.5 * bend
-                slope = half + upper * (0.5 - 0.5 * (bend * bend)) * (root + (root * 3 * 0.044715) * square)
-                act[there, lanes] = (upper * half).astype(BF)
-                grads[there, lanes] = (slope_ref[here, lanes] * slope).astype(BF)
-
-        act_store(step).start()
-        grad_store(step).start()
-
-    turned_load.wait()
-
-    @pl.loop(0, 8)
-    def _(step):
-        rows = pl.ds(pl.multiple_of(step * 256, 256), 256)
-        total = dot(turned[rows, :], grads[...]).astype(BF)
-        up_out[pl.ds(step * 2, 2)] = total.reshape(2, 128, 1024)
-        up_store(step).start()
-
-    @pl.loop(0, 4)
-    def _(step):
-        lanes = pl.ds(pl.multiple_of(step * 256, 256), 256)
-        total = dot_rows(act[:, lanes], cot[...]).astype(BF)
-        down_out[pl.ds(step * 4, 4), :64] = total[:, :1024].reshape(4, 64, 1024)
-        down_out[pl.ds(step * 4, 4), 64:] = total[:, 1024:].reshape(4, 64, 1024)
-        down_store(step).start()
-
-    @pl.loop(0, 4)
-    def _(step):
-        act_store(step).wait()
-        grad_store(step).wait()
-        down_store(step).wait()
-
-    @pl.loop(0, 8)
-    def _(step):
-        up_store(step).wait()
-
-
-def feed(normed, turned, near, far, weights, bias, pack):
-    vmem, hbm = pl.BlockSpec(memory_space=pltpu.VMEM), pl.BlockSpec(memory_space=pltpu.HBM)
-    return pl.pallas_call(
-        feed_body,
-        in_specs=[hbm] * 5 + [vmem, hbm],
-        out_specs=[hbm] * 3,
-        out_shape=[
-            jax.ShapeDtypeStruct((TOKENS, 1024), BF),
-            jax.ShapeDtypeStruct((TOKENS, 1024), BF),
-            jax.ShapeDtypeStruct((16, 384, 1024), BF),
-        ],
-        input_output_aliases={6: 2},
-        scratch_shapes=[
-            pltpu.VMEM((TOKENS, D), BF),
-            pltpu.VMEM((D, TOKENS), BF),
-            pltpu.VMEM((TOKENS, D), BF),
-            pltpu.VMEM((16, 128, 1024), BF),
-            pltpu.VMEM((16, 128, 1024), BF),
-            pltpu.VMEM((TOKENS, 1024), BF),
-            pltpu.VMEM((TOKENS, 1024), BF),
+            slab,
+            slab,
+            square,
+            square,
             pltpu.VMEM((TOKENS, 1024), F32),
             pltpu.VMEM((256, 1024), F32),
-            pltpu.VMEM((16, 128, 1024), BF),
-            pltpu.VMEM((16, 128, 1024), BF),
-            pltpu.SemaphoreType.DMA((6,)),
+            slab,
+            slab,
             pltpu.SemaphoreType.DMA((4,)),
             pltpu.SemaphoreType.DMA((4,)),
             pltpu.SemaphoreType.DMA((8,)),
@@ -630,10 +611,13 @@
         ],
         compiler_params=pltpu.CompilerParams(vmem_limit_bytes=VMEM),
         cost_estimate=pl.CostEstimate(
-            flops=8 * TOKENS * D * 1024, bytes_accessed=32 << 20, transcendentals=TOKENS * 1024
+            flops=30 << 30, bytes_accessed=64 << 20, transcendentals=2 * TOKENS * 1024
         ),
-        name="feed",
-    )(normed, turned, near, far, weights, bias, pack)
+        name="work",
+    )(
+        odd.reshape(1), normed, turned, near, far, weights, bias, up_bias, cosine, sin1, sin2, rows,
+        segment.reshape(TOKENS, 1),
+    )
 
 
 def branch_body(context_ref, proj_ref, act_ref, down_ref, near_ref, far_ref):
@@ -724,6 +708,7 @@
 ):
     xh, core, xl = lax.axis_index("xh"), lax.axis_index("core"), lax.axis_index("xl")
     place = 2 * xh + xl
+    scalars = jnp.stack([place, core, xl]).astype(jnp.int32)
     hidden_own = hidden_in.reshape(128, D)
     cot_own = cotangent.reshape(128, D)
 
@@ -788,10 +773,9 @@
     sin1 = jnp.where(lane < 16, sine, 0.0)
     sin2 = jnp.where((lane >= 16) & (lane < ROT), sine, 0.0)
 
-    context, grad_merged, pack = heads(
-        xl, normed, turned, cot, cot_far, weights, qkv_b, cosine, sin1, sin2, segment_all
-    )
-    active, grad_upper, pack = feed(normed, turned, cot, cot_far, weights, up_b, pack)
+    context, grad_merged, active, grad_upper, pack = work(
+        xl, normed, turned, cot, cot_far, weights, qkv_b, up_b, cosine, sin1, sin2, segment_all
+    )
     back = scatter_plane_whole(pack)
 
     pulled, pulled_far, gain_sum, shift_sum, up_sum, qkv_sum = pull(
@@ -811,20 +795,20 @@
     )
     pulled_far = shift(pulled_far, "core", 1)
     sums = reduce_step(sums, 5)
-    branch, branch_far = branch_out(context, after(active, gain_sum), weights)
+    branch, branch_far = branch_out(context, active, weights)
     sums, branch_far, pulled_far = tie(sums, branch_far, pulled_far)
     pulled = sum_parts(pulled, pulled_far)
     low, high = fold_first(pulled)
     branch_far = shift(branch_far, "core", 1)
-    sums = reduce_step(sums, 4)
+    sums = reduce_step(reduce_step(reduce_step(sums, 4), 3), 2)
     sums, branch_far, low, high = tie(sums, branch_far, low, high)
     from_below, from_above = fold_second(pulled, low, high)
     branch = sum_parts(branch, branch_far)
     low, high = fold_first(branch)
-    sums = reduce_step(sums, 3)
+    sums = reduce_step(reduce_step(sums, 1), 0)
+    sums = (sums + shift(sums, "xl", 1))[0]
     sums, low, high, from_below, from_above = tie(sums, low, high, from_below, from_above)
     branch_below, branch_above = fold_second(branch, low, high)
-    sums = reduce_step(sums, 2)
     grad_own = pulled[0] + from_below.astype(F32) + from_above.astype(F32)
 
     own = owner_order(hidden_own).astype(F32)
@@ -837,24 +821,17 @@
     lifted = (scaled - jnp.mean(scaled, axis=-1, keepdims=True) - normal_own * inner) * rstd
     grad_hidden = (cot_own.astype(F32) + plain_order(lifted)).reshape(1, 128, D)
 
-    sums, branch_below, branch_above, grad_hidden = tie(sums, branch_below, branch_above, grad_hidden)
-    sums = reduce_step(reduce_step(sums, 1), 0)
-    sums = (sums + shift(sums, "xl", 1))[0]
     branch = branch[0] + branch_below.astype(F32) + branch_above.astype(F32)
     block_out = hidden_own.astype(F32) + branch + out_bias
     block_out = block_out.astype(BF).reshape(1, 128, D)
 
-    back = after(back, grad_hidden, block_out, sums)
-    near, far, down_rows, proj_rows = sort(core, back)
-    far = shift(far, "core", 1)
-    down_rows, proj_rows = after((down_rows, proj_rows), far)
-    pair = jnp.stack([near, far], axis=1)
-    pieces = [pick(pair, xh)]
-    for step in (1, 2, 3):
-        pieces.append(shift(pick(pair, ((place + step) % 4) // 2), "x", step))
-    grad_up, grad_qkv = spread(place, core, pieces)
-    grad_down = pair_gather(down_rows, "xl").reshape(128, D)
-    grad_proj = pair_gather(rehome(proj_rows, back=True), "xl").reshape(32, D)
+    back, grad_hidden, block_out, sums = tie(back, grad_hidden, block_out, sums)
+    *pieces, down_rows, proj_rows = sort(scalars, back)
+    pieces = [pieces[0]] + [across(pieces[step], step) for step in (1, 2, 3)]
+    proj = (rehome(proj_rows, back=True), rehome(proj_rows, back=True, other=True))
+    pieces, proj = tie(pieces, proj)
+    other = shift(jnp.stack([piece[64:128] for piece in pieces]), "core", 1)
+    grad_up, grad_qkv, grad_down, grad_proj = spread(scalars, pieces, other, down_rows, proj)
     return (
         block_out,
         grad_hidden,
@@ -862,11 +839,11 @@
         sums[32:64],
         grad_qkv,
         sums[96:192],
-        grad_proj.astype(F32),
+        grad_proj,
         sums[64:96],
         grad_up,
         sums[192:320],
-        grad_down.astype(F32),
+        grad_down,
         sums[64:96],
     )
 

time: 327 us -> 309 us (0.945)
  waiting for transfers between devices: 74 us -> 65.7 us
  other arithmetic: 33.5 us -> 26.4 us
  Pallas kernels: 98.5 us -> 94.7 us
    ppermute x30 -> x25, waiting for transfers between devices: 51.3 us -> 36 us  [shift(): lax.ppermute(value, names, [(i, (i + step) % size) for i in range(size)])]
    pallas_call x2 -> x1, Pallas kernels: 57.4 us -> 52.4 us  [work(): pl.pallas_call(work_body, in_specs=[pl.BlockSpec(memory_space=pltpu.SMEM)...]
    ppermute x2 -> x3, waiting for transfers between devices: 3.96 us -> 8.79 us  [rehome(): return lax.ppermute(value, ('z', 'y', 'core', 'xl'), pairs)]
    ppermute x2 -> x3, starting transfers between devices: 9.56 us -> 14.4 us  [rehome(): return lax.ppermute(value, ('z', 'y', 'core', 'xl'), pairs)]
    ppermute x12, starting transfers between devices: 24.5 us -> 20.3 us  [toward(): return lax.ppermute(value, axis, [(i, i ^ bit) for i in range(size)])]
    reduce_scatter x1, waiting for transfers between devices: 0.01 us -> 3.97 us  [scatter_plane_whole(): return lax.psum_scatter(flat, PLANE, scatter_dimension=0, tiled=True)]
    ppermute x0 -> x3, starting transfers between devices: none -> 3.86 us  [across(): return lax.ppermute(value, ('xh', 'xl'), [(i, i ^ step) for i in range(4)])]
    ppermute x30 -> x25, starting transfers between devices: 39.6 us -> 37.9 us  [shift(): lax.ppermute(value, names, [(i, (i + step) % size) for i in range(size)])]
  transfers between devices with their start and end apart: 49 -> 48, of which waited for: 21 -> 18; matrix products, arithmetic and copies ran while one was open for 16% -> 15% of each run, Pallas kernels for 10% -> 11%
where the time goes in v3:
time: 309 us; the launch traced here: 308 us
  Pallas kernels  94.7 us (31%)
  starting transfers between devices  80.9 us (26%)
  waiting for transfers between devices  65.7 us (21%)
  other arithmetic  26.4 us (9%)
  local copies, waits for them, and re-layouts  24.9 us (8%)
  between operations  15.1 us (5%)
    pallas_call x1, Pallas kernels, work(): pl.pallas_call(work_body, in_specs=[pl.BlockSpec(memory_space=pltpu.SMEM)...  52.4 us
    ppermute x25, starting transfers between devices, shift(): lax.ppermute(value, names, [(i, (i + step) % size) for i in range(size)])  37.9 us
    ppermute x25, waiting for transfers between devices, shift(): lax.ppermute(value, names, [(i, (i + step) % size) for i in range(size)])  36 us
    ppermute x12, starting transfers between devices, toward(): return lax.ppermute(value, axis, [(i, i ^ bit) for i in range(size)])  20.3 us
    pallas_call x1, Pallas kernels, pull(): pl.pallas_call(pull_body, grid=(8,), in_specs=[whole(1024), whole(768), p...  15.3 us
    ppermute x3, starting transfers between devices, rehome(): return lax.ppermute(value, ('z', 'y', 'core', 'xl'), pairs)  14.4 us
    pallas_call x1, Pallas kernels, branch_out(): pl.pallas_call(branch_body, grid=(8,), in_specs=[pl.BlockSpec((TOKENS, 25...  11.1 us
    all_gather x1, waiting for transfers between devices, gather_plane(): return lax.all_gather(value, PLANE, axis=0, tiled=False)  11 us
  transfers between devices with their start and end apart: 48, of which 18 were waited for; matrix products, arithmetic and copies ran while one was open for 15% of the time, Pallas kernels for 11%

profile of v3, /device:TPU:1, one launch (start us, length us, event | category | flops | bytes accessed | tf_op | source)
XLA Modules:
  0.0 307.7 jit_solution(7151223014457330812)
XLA Ops:
  7.8 2.2 deal.1
  11.2 4.2 %collective-permute-start.2 = (bf16[32,1792]{1,0:T(8,128)(2,1)S(1)}, bf16[32,1792]{1,0:T(8,128)(2,1)S(1)}, u32[]{:S(2)}, u32[]{:S(2)}) collective-permute-start(bf16[32,1792]{1,0:T(8,128)(2,1)S(1)} %get-tuple-element.196), channel_id=1, source_target_pairs={{0,66},{2,64},{64,2},{66,0},{1,67},{3,65},{65,3},{67,1},{4,70},{6,... | collective-permute-start | bytes 344072 | tf_op jit(solution)/shard_map/ppermute | solution.py:72
  15.6 5.5 %collective-permute-start.3 = (bf16[16,2048]{1,0:T(8,128)(2,1)S(1)}, bf16[16,2048]{1,0:T(8,128)(2,1)S(1)}, u32[]{:S(2)}, u32[]{:S(2)}) collective-permute-start(bf16[16,2048]{1,0:T(8,128)(2,1)S(1)} %constant_dynamic-slice_fusion.12), channel_id=1, source_target_pairs={{0,0},{1,4},{2,8},{3,12},{4,16},{5,20},{6,24},{7,28},{8,32},{9,36}... | collective-permute-start | bytes 196616 | tf_op jit(solution)/shard_map/ppermute | solution.py:124
  21.2 2.6 collective-permute-done.3
  26.8 3.8 %collective-permute-start.5 = (bf16[128,2048]{1,0:T(8,128)(2,1)}, bf16[128,2048]{1,0:T(8,128)(2,1)S(1)}, u32[]{:S(2)}, u32[]{:S(2)}) collective-permute-start(bf16[128,2048]{1,0:T(8,128)(2,1)} %copy.62), channel_id=1, source_target_pairs={{0,1},{1,64},{64,65},{65,0},{2,3},{3,66},{66,67},{67,2},{4,5},{5,6... | collective-permute-start | bytes 1572872 | tf_op jit(solution)/shard_map/ppermute | solution.py:29
  31.9 9.7 %collective-permute-done.5 = bf16[128,2048]{1,0:T(8,128)(2,1)S(1)} collective-permute-done((bf16[128,2048]{1,0:T(8,128)(2,1)}, bf16[128,2048]{1,0:T(8,128)(2,1)S(1)}, u32[]{:S(2)}, u32[]{:S(2)}) %collective-permute-start.5) | collective-permute-done | bytes 524320 | tf_op jit(solution)/shard_map/ppermute | solution.py:29
  41.6 1.9 collective-permute-done.6
  47.0 6.5 %collective-permute-done.8 = bf16[64,2048]{1,0:T(8,128)(2,1)S(1)} collective-permute-done((bf16[64,2048]{1,0:T(8,128)(2,1)S(1)}, bf16[64,2048]{1,0:T(8,128)(2,1)S(1)}, u32[]{:S(2)}, u32[]{:S(2)}) %collective-permute-start.8) | collective-permute-done | bytes 262176 | tf_op jit(solution)/shard_map/ppermute | solution.py:29
  54.2 1.9 collective-permute-start.13
  56.2 3.2 %collective-permute-start.11 = (bf16[4,352]{1,0:T(4,128)(2,1)S(1)}, bf16[4,352]{1,0:T(4,128)(2,1)S(1)}, u32[]{:S(2)}, u32[]{:S(2)}) collective-permute-start(bf16[4,352]{1,0:T(4,128)(2,1)S(1)} %pad_maximum_fusion.13), channel_id=1, source_target_pairs={{0,8},{4,12},{8,0},{12,4},{1,9},{5,13},{9,1},{13,5},{2,10},{6,14},... | collective-permute-start | bytes 8456 | tf_op jit(solution)/shard_map/ppermute | solution.py:98
  60.3 2.2 collective-permute-start.10
  62.6 4.8 %collective-permute-done.12 = bf16[128,2048]{1,0:T(8,128)(2,1)S(1)} collective-permute-done((bf16[128,2048]{1,0:T(8,128)(2,1)S(1)}, bf16[128,2048]{1,0:T(8,128)(2,1)S(1)}, u32[]{:S(2)}, u32[]{:S(2)}) %collective-permute-start.12) | collective-permute-done | bytes 524320 | tf_op jit(solution)/shard_map/ppermute | solution.py:29
  71.6 1.6 collective-permute-done.14
  73.3 1.7 collective-permute-done.15
  75.5 2.1 collective-permute-start.17
  79.9 3.2 %collective-permute-start.21 = (s32[2,2,128]{2,1,0:T(2,128)S(1)}, s32[2,2,128]{2,1,0:T(2,128)S(1)}, u32[]{:S(2)}, u32[]{:S(2)}) collective-permute-start(s32[2,2,128]{2,1,0:T(2,128)S(1)} %reverse_select_fusion.1), channel_id=1, source_target_pairs={{0,64},{64,0},{1,65},{65,1},{2,66},{66,2},{3,67},{67,3},{4,68},{68... | collective-permute-start | bytes 6152 | tf_op jit(solution)/shard_map/ppermute | solution.py:29
  83.9 4.4 %collective-permute-start.20 = (bf16[512,2048]{1,0:T(8,128)(2,1)}, bf16[512,2048]{1,0:T(8,128)(2,1)}, u32[]{:S(2)}, u32[]{:S(2)}) collective-permute-start(bf16[512,2048]{1,0:T(8,128)(2,1)} %constant_dynamic-update-slice_fusion.5.near_hbm), channel_id=1, source_target_pairs={{0,2},{2,0},{1,3},{3,1},{4,6},{6,4},{5,7},{7,5},{8,10},{10,8},{9,1... | collective-permute-start | bytes 6291464 | tf_op jit(solution)/shard_map/ppermute | solution.py:29
  89.1 3.2 %collective-permute-start.19 = (bf16[32,352]{1,0:T(8,128)(2,1)S(1)}, bf16[32,352]{1,0:T(8,128)(2,1)S(1)}, u32[]{:S(2)}, u32[]{:S(2)}) collective-permute-start(bf16[32,352]{1,0:T(8,128)(2,1)S(1)} %pad_maximum_fusion.10), channel_id=1, source_target_pairs={{0,64},{64,0},{1,65},{65,1},{2,66},{66,2},{3,67},{67,3},{4,68},{68... | collective-permute-start | bytes 67592 | tf_op jit(solution)/shard_map/ppermute | solution.py:98
  92.4 3.2 %fusion.6 = (f32[1024,128]{1,0:T(8,128)}, f32[1024,128]{1,0:T(8,128)}, f32[1024,128]{1,0:T(8,128)}) fusion(f32[128]{0:T(128)S(1)} %fusion.25, f32[1024]{0:T(1024)S(1)} %bitcast.148, pred[128]{0:T(512)(128)(4,1)S(1)} %get-tuple-element.229, pred[128]{0:T(512)(128)(4,1)S(1)} %get-tuple-element.230, pred[128]{0:T(512)(128)(4,1)S(1)} %broadcast_compare_fusion.1), kind=kLoop, calls=%fused_computation.26 | loop fusion | flops 524288 | bytes 1577856 | tf_op jit(solution)/shard_map/jit(_where)/select_n | solution.py:774
  100.5 7.8 %norm.1 = (bf16[1024,2048]{1,0:T(8,128)(2,1)}, bf16[2048,1024]{1,0:T(8,128)(2,1)}, f32[1024,1]{1,0:T(8,128)}, f32[1024,1]{1,0:T(8,128)}) custom-call(bf16[512,2048]{1,0:T(8,128)(2,1)} %copy-done.2, bf16[512,2048]{1,0:T(8,128)(2,1)} %collective-permute-done.10.far_ref.hid_far_ref, f32[1,2048]{1,0:T(1,128)} %reshape_reshape.26.gain_ref, ...), custom_call_target="tpu_custom_call" | custom-call | flops 20971520 | bytes 12582912 | tf_op jit(solution)/shard_map/norm/pallas_call | solution.py:282
  108.3 11.0 %all-gather.3.cloned.1.call-done = bf16[6144,1024]{1,0:T(8,128)(2,1)} async-done(((bf16[384,1024]{1,0:T(8,128)(2,1)}), bf16[6144,1024]{1,0:T(8,128)(2,1)}) %all-gather.3.cloned.1.call-update) | async-done | bytes 12582928 | tf_op jit(solution)/shard_map/all_gather | solution.py:85
  119.3 52.4 %work.1 = (bf16[1024,256]{1,0:T(8,128)(2,1)}, bf16[1024,768]{1,0:T(8,128)(2,1)}, bf16[1024,1024]{1,0:T(8,128)(2,1)}, bf16[1024,1024]{1,0:T(8,128)(2,1)}, bf16[16,384,1024]{2,1,0:T(8,128)(2,1)}) custom-call(s32[1]{0:T(128)} %bitcast.odd_ref, bf16[1024,2048]{1,0:T(8,128)(2,1)} %get-tuple-element.100.normed_hbm, ...), custom_call_target="tpu_custom_call" | custom-call | flops 32212254720 | bytes 67108864 | tf_op jit(solution)/shard_map/work/pallas_call | solution.py:557
  171.7 15.3 %pull.1 = (bf16[512,2048]{1,0:T(8,128)(2,1)}, bf16[512,2048]{1,0:T(8,128)(2,1)}, f32[1,2048]{1,0:T(1,128)}, f32[1,2048]{1,0:T(1,128)}, f32[1,1024]{1,0:T(1,128)}, /*index=5*/f32[1,768]{1,0:T(1,128)}) custom-call(bf16[1024,1024]{1,0:T(8,128)(2,1)} %get-tuple-element.106.grad_ref, bf16[1024,768]{1,0:T(8,128)(2,1)} %get-tuple-element.107.merged_ref, ...), custom_call_target="tpu_custom_call" | custom-call | flops 7516192768 | bytes 16777216 | tf_op jit(solution)/shard_map/pull/pallas_call | solution.py:674
  194.1 2.8 collective-permute-start.23
  196.9 11.1 %branch.1 = (bf16[512,2048]{1,0:T(8,128)(2,1)}, bf16[512,2048]{1,0:T(8,128)(2,1)}) custom-call(bf16[1024,256]{1,0:T(8,128)(2,1)} %get-tuple-element.115.context_ref, bf16[16,384,1024]{2,1,0:T(8,128)(2,1)} %bitcast.118, bf16[1024,1024]{1,0:T(8,128)(2,1)} %get-tuple-element.116.act_ref, bf16[16,384,1024]{2,1,0:T(8,128)(2,1)} %bitcast.119), custom_call_target="tpu_custom_call" | custom-call | flops 5368709120 | bytes 12582912 | tf_op jit(solution)/shard_map/branch/pallas_call | solution.py:631
  208.5 2.5 collective-permute-start.25
  210.9 2.4 convert_add_fusion.3
  215.6 2.4 collective-permute-start.30
  218.1 1.7 collective-permute-start.27
  219.8 2.4 collective-permute-done.27
  224.6 2.2 collective-permute-start.37
  227.8 3.5 %convert_add_fusion.2 = (f32[128,2048]{1,0:T(8,128)}, f32[128,2048]{1,0:T(8,128)S(1)}, bf16[128,2048]{1,0:T(8,128)(2,1)S(1)}) fusion(bf16[512,2048]{1,0:T(8,128)(2,1)} %collective-permute-done.28, bf16[512,2048]{1,0:T(8,128)(2,1)} %get-tuple-element.123), kind=kLoop, calls=%fused_computation.8 | loop fusion | flops 2621440 | bytes 5767168 | tf_op jit(solution)/shard_map/add | solution.py:65
  231.4 2.5 collective-permute-start.32
  234.7 3.0 collective-permute-start.35
  241.0 2.5 collective-permute-done.33
  243.5 2.4 collective-permute-done.34
  248.7 2.7 collective-permute-start.39
  251.4 2.1 fusion.28
  255.0 4.4 %collective-permute-done.38 = bf16[128,2048]{1,0:T(8,128)(2,1)} collective-permute-done((bf16[128,2048]{1,0:T(8,128)(2,1)}, bf16[128,2048]{1,0:T(8,128)(2,1)}, u32[]{:S(2)}, u32[]{:S(2)}) %collective-permute-start.38) | collective-permute-done | bytes 524320 | tf_op jit(solution)/shard_map/ppermute | solution.py:29
  259.5 2.8 fusion.9
  262.3 4.0 %reduce-scatter.2.cloned.1.call-done.in_ref = bf16[384,1024]{1,0:T(8,128)(2,1)} async-done(((bf16[6144,1024]{1,0:T(8,128)(2,1)}), bf16[384,1024]{1,0:T(8,128)(2,1)}) %reduce-scatter.2.cloned.1.call-update) | async-done | bytes 786448 | tf_op jit(solution)/shard_map/reduce_scatter | solution.py:90
  266.2 2.4 sort.1
  269.8 2.4 collective-permute-start.41
  272.4 5.4 %collective-permute-start.43 = (bf16[16,2048]{1,0:T(8,128)(2,1)}, bf16[16,2048]{1,0:T(8,128)(2,1)S(1)}, u32[]{:S(2)}, u32[]{:S(2)}) collective-permute-start(bf16[16,2048]{1,0:T(8,128)(2,1)} %get-tuple-element.140), channel_id=1, source_target_pairs={{0,0},{4,1},{8,2},{12,3},{16,4},{20,5},{24,6},{28,7},{32,8},{36,9}... | collective-permute-start | bytes 196616 | tf_op jit(solution)/shard_map/ppermute | solution.py:124
  277.9 3.5 %collective-permute-start.44 = (bf16[16,2048]{1,0:T(8,128)(2,1)}, bf16[16,2048]{1,0:T(8,128)(2,1)S(1)}, u32[]{:S(2)}, u32[]{:S(2)}) collective-permute-start(bf16[16,2048]{1,0:T(8,128)(2,1)} %get-tuple-element.140), channel_id=1, source_target_pairs={{0,1},{4,0},{8,3},{12,2},{16,5},{20,4},{24,7},{28,6},{32,9},{36,8}... | collective-permute-start | bytes 196616 | tf_op jit(solution)/shard_map/ppermute | solution.py:124
  281.3 6.2 %collective-permute-done.44.refs_7_ = bf16[16,2048]{1,0:T(8,128)(2,1)S(1)} collective-permute-done((bf16[16,2048]{1,0:T(8,128)(2,1)}, bf16[16,2048]{1,0:T(8,128)(2,1)S(1)}, u32[]{:S(2)}, u32[]{:S(2)}) %collective-permute-start.44) | collective-permute-done | bytes 65568 | tf_op jit(solution)/shard_map/ppermute | solution.py:124
  289.8 3.1 %collective-permute-start.45 = (bf16[4,64,1024]{2,1,0:T(8,128)(2,1)S(1)}, bf16[4,64,1024]{2,1,0:T(8,128)(2,1)S(1)}, u32[]{:S(2)}, u32[]{:S(2)}) collective-permute-start(bf16[4,64,1024]{2,1,0:T(8,128)(2,1)S(1)} %pad_maximum_fusion.7), channel_id=1, source_target_pairs={{0,2},{2,0},{1,3},{3,1},{4,6},{6,4},{5,7},{7,5},{8,10},{10,8},{9,1... | collective-permute-start | bytes 1572872 | tf_op jit(solution)/shard_map/ppermute | solution.py:29
  296.8 3.6 %spread.1 = (f32[32,8192]{1,0:T(8,128)}, f32[32,6144]{1,0:T(8,128)}, f32[128,2048]{1,0:T(8,128)}, f32[32,2048]{1,0:T(8,128)}) custom-call(s32[3]{0:T(128)} %pad_add_fusion.6.place_ref, bf16[128,1024]{1,0:T(8,128)(2,1)} %get-tuple-element.141.refs_0_, bf16[256,1024]{1,0:T(8,128)(2,1)} %copy-done.11, bf16[128,1024]{1,0:T(8,128)(2,1)} %copy-done.12, ...), custom_call_target="tpu_custom_call" | custom-call | tf_op jit(solution)/shard_map/spread/pallas_call | solution.py:218
  (264 shorter events, 54.1 us)
Async XLA Ops:
  7.2 112.1 %all-gather.3.cloned.1.call-start = ((), (), s32[]{:S(2)}) async-start(), calls=%async_computation.2 | async-start | bytes 13369344 | tf_op jit(solution)/shard_map/all_gather | solution.py:85
  11.2 12.6 %collective-permute-start.2 = (bf16[32,1792]{1,0:T(8,128)(2,1)S(1)}, bf16[32,1792]{1,0:T(8,128)(2,1)S(1)}, u32[]{:S(2)}, u32[]{:S(2)}) collective-permute-start(bf16[32,1792]{1,0:T(8,128)(2,1)S(1)} %get-tuple-element.196), channel_id=1, source_target_pairs={{0,66},{2,64},{64,2},{66,0},{1,67},{3,65},{65,3},{67,1},{4,70},{6,... | collective-permute-start | bytes 344072 | tf_op jit(solution)/shard_map/ppermute | solution.py:72
  15.4 8.4 %collective-permute-start = (bf16[32,1792]{1,0:T(8,128)(2,1)S(1)}, bf16[32,1792]{1,0:T(8,128)(2,1)S(1)}, u32[]{:S(2)}, u32[]{:S(2)}) collective-permute-start(bf16[32,1792]{1,0:T(8,128)(2,1)S(1)} %get-tuple-element.198), channel_id=1, source_target_pairs={{0,2},{2,0},{64,66},{66,64},{1,3},{3,1},{65,67},{67,65},{4,6},{6,4... | collective-permute-start | bytes 344072 | tf_op jit(solution)/shard_map/ppermute | solution.py:72
  15.4 8.4 %collective-permute-start.1 = (bf16[32,1792]{1,0:T(8,128)(2,1)S(1)}, bf16[32,1792]{1,0:T(8,128)(2,1)S(1)}, u32[]{:S(2)}, u32[]{:S(2)}) collective-permute-start(bf16[32,1792]{1,0:T(8,128)(2,1)S(1)} %get-tuple-element.197), channel_id=1, source_target_pairs={{0,64},{2,66},{64,0},{66,2},{1,65},{3,67},{65,1},{67,3},{4,68},{6,... | collective-permute-start | bytes 344072 | tf_op jit(solution)/shard_map/ppermute | solution.py:72
  15.6 8.1 %collective-permute-start.3 = (bf16[16,2048]{1,0:T(8,128)(2,1)S(1)}, bf16[16,2048]{1,0:T(8,128)(2,1)S(1)}, u32[]{:S(2)}, u32[]{:S(2)}) collective-permute-start(bf16[16,2048]{1,0:T(8,128)(2,1)S(1)} %constant_dynamic-slice_fusion.12), channel_id=1, source_target_pairs={{0,0},{1,4},{2,8},{3,12},{4,16},{5,20},{6,24},{7,28},{8,32},{9,36}... | collective-permute-start | bytes 196616 | tf_op jit(solution)/shard_map/ppermute | solution.py:124
  25.1 241.1 %reduce-scatter.2.cloned.1.call-start = ((), (), s32[]{:S(2)}) async-start(), calls=%async_computation.1 | async-start | bytes 13369344 | tf_op jit(solution)/shard_map/reduce_scatter | solution.py:90
  26.8 14.8 %collective-permute-start.5 = (bf16[128,2048]{1,0:T(8,128)(2,1)}, bf16[128,2048]{1,0:T(8,128)(2,1)S(1)}, u32[]{:S(2)}, u32[]{:S(2)}) collective-permute-start(bf16[128,2048]{1,0:T(8,128)(2,1)} %copy.62), channel_id=1, source_target_pairs={{0,1},{1,64},{64,65},{65,0},{2,3},{3,66},{66,67},{67,2},{4,5},{5,6... | collective-permute-start | bytes 1572872 | tf_op jit(solution)/shard_map/ppermute | solution.py:29
  30.7 12.9 %collective-permute-start.6 = (bf16[128,2048]{1,0:T(8,128)(2,1)}, bf16[128,2048]{1,0:T(8,128)(2,1)S(1)}, u32[]{:S(2)}, u32[]{:S(2)}) collective-permute-start(bf16[128,2048]{1,0:T(8,128)(2,1)} %copy.62), channel_id=1, source_target_pairs={{0,65},{1,0},{64,1},{65,64},{2,67},{3,2},{66,3},{67,66},{4,69},{5,... | collective-permute-start | bytes 1572872 | tf_op jit(solution)/shard_map/ppermute | solution.py:29
  30.7 1.2 collective-permute-start.4
  43.6 3.4 %collective-permute-start.7 = (bf16[2,352]{1,0:T(2,128)(2,1)S(1)}, bf16[2,352]{1,0:T(2,128)(2,1)S(1)}, u32[]{:S(2)}, u32[]{:S(2)}) collective-permute-start(bf16[2,352]{1,0:T(2,128)(2,1)S(1)} %pad_maximum_fusion.14), channel_id=1, source_target_pairs={{0,4},{4,0},{8,12},{12,8},{1,5},{5,1},{9,13},{13,9},{2,6},{6,2},{1... | collective-permute-start | bytes 4232 | tf_op jit(solution)/shard_map/ppermute | solution.py:98
  44.1 9.4 %collective-permute-start.8 = (bf16[64,2048]{1,0:T(8,128)(2,1)S(1)}, bf16[64,2048]{1,0:T(8,128)(2,1)S(1)}, u32[]{:S(2)}, u32[]{:S(2)}) collective-permute-start(bf16[64,2048]{1,0:T(8,128)(2,1)S(1)} %slice.210), channel_id=1, source_target_pairs={{0,1},{1,64},{64,65},{65,0},{2,3},{3,66},{66,67},{67,2},{4,5},{5,6... | collective-permute-start | bytes 786440 | tf_op jit(solution)/shard_map/ppermute | solution.py:29
  45.5 8.0 %collective-permute-start.9 = (bf16[64,2048]{1,0:T(8,128)(2,1)S(1)}, bf16[64,2048]{1,0:T(8,128)(2,1)S(1)}, u32[]{:S(2)}, u32[]{:S(2)}) collective-permute-start(bf16[64,2048]{1,0:T(8,128)(2,1)S(1)} %slice.211), channel_id=1, source_target_pairs={{0,65},{1,0},{64,1},{65,64},{2,67},{3,2},{66,3},{67,66},{4,69},{5,... | collective-permute-start | bytes 786440 | tf_op jit(solution)/shard_map/ppermute | solution.py:29
  53.5 13.9 %collective-permute-start.12 = (bf16[128,2048]{1,0:T(8,128)(2,1)S(1)}, bf16[128,2048]{1,0:T(8,128)(2,1)S(1)}, u32[]{:S(2)}, u32[]{:S(2)}) collective-permute-start(bf16[128,2048]{1,0:T(8,128)(2,1)S(1)} %bitcast.124), channel_id=1, source_target_pairs={{0,1},{1,64},{64,65},{65,0},{2,3},{3,66},{66,67},{67,2},{4,5},{5,6... | collective-permute-start | bytes 1572872 | tf_op jit(solution)/shard_map/ppermute | solution.py:29
  54.2 13.2 %collective-permute-start.13 = (bf16[128,2048]{1,0:T(8,128)(2,1)S(1)}, bf16[128,2048]{1,0:T(8,128)(2,1)S(1)}, u32[]{:S(2)}, u32[]{:S(2)}) collective-permute-start(bf16[128,2048]{1,0:T(8,128)(2,1)S(1)} %bitcast.125), channel_id=1, source_target_pairs={{0,65},{1,0},{64,1},{65,64},{2,67},{3,2},{66,3},{67,66},{4,69},{5,... | collective-permute-start | bytes 1572872 | tf_op jit(solution)/shard_map/ppermute | solution.py:29
  56.2 6.4 %collective-permute-start.11 = (bf16[4,352]{1,0:T(4,128)(2,1)S(1)}, bf16[4,352]{1,0:T(4,128)(2,1)S(1)}, u32[]{:S(2)}, u32[]{:S(2)}) collective-permute-start(bf16[4,352]{1,0:T(4,128)(2,1)S(1)} %pad_maximum_fusion.13), channel_id=1, source_target_pairs={{0,8},{4,12},{8,0},{12,4},{1,9},{5,13},{9,1},{13,5},{2,10},{6,14},... | collective-permute-start | bytes 8456 | tf_op jit(solution)/shard_map/ppermute | solution.py:98
  60.3 40.2 %collective-permute-start.10 = (bf16[512,2048]{1,0:T(8,128)(2,1)S(1)}, bf16[512,2048]{1,0:T(8,128)(2,1)}, u32[]{:S(2)}, u32[]{:S(2)}) collective-permute-start(bf16[512,2048]{1,0:T(8,128)(2,1)S(1)} %constant_dynamic-update-slice_fusion.near_ref.hid_near_ref), channel_id=1, source_target_pairs={{0,2},{2,0},{1,3},{3,1},{4,6},{6,4},{5,7},{7,5},{8,10},{10,8},{9,1... | collective-permute-start | bytes 6291464 | tf_op jit(solution)/shard_map/ppermute | solution.py:29
  67.4 7.5 %collective-permute-start.15 = (bf16[64,2048]{1,0:T(8,128)(2,1)S(1)}, bf16[64,2048]{1,0:T(8,128)(2,1)S(1)}, u32[]{:S(2)}, u32[]{:S(2)}) collective-permute-start(bf16[64,2048]{1,0:T(8,128)(2,1)S(1)} %slice.212), channel_id=1, source_target_pairs={{0,1},{1,64},{64,65},{65,0},{2,3},{3,66},{66,67},{67,2},{4,5},{5,6... | collective-permute-start | bytes 786440 | tf_op jit(solution)/shard_map/ppermute | solution.py:29
  68.9 6.4 %collective-permute-start.16 = (bf16[64,2048]{1,0:T(8,128)(2,1)S(1)}, bf16[64,2048]{1,0:T(8,128)(2,1)S(1)}, u32[]{:S(2)}, u32[]{:S(2)}) collective-permute-start(bf16[64,2048]{1,0:T(8,128)(2,1)S(1)} %slice.213), channel_id=1, source_target_pairs={{0,65},{1,0},{64,1},{65,64},{2,67},{3,2},{66,3},{67,66},{4,69},{5,... | collective-permute-start | bytes 786440 | tf_op jit(solution)/shard_map/ppermute | solution.py:29
  70.3 3.0 collective-permute-start.14
  75.4 3.7 %collective-permute-start.18 = (s32[2,128]{1,0:T(2,128)S(1)}, s32[2,128]{1,0:T(2,128)S(1)}, u32[]{:S(2)}, u32[]{:S(2)}) collective-permute-start(s32[2,128]{1,0:T(2,128)S(1)} %pad_add_fusion.4), channel_id=1, source_target_pairs={{0,1},{1,0},{2,3},{3,2},{4,5},{5,4},{6,7},{7,6},{8,9},{9,8},{10,11... | collective-permute-start | bytes 3080 | tf_op jit(solution)/shard_map/ppermute | solution.py:29
  75.5 4.3 %collective-permute-start.17 = (bf16[16,352]{1,0:T(8,128)(2,1)S(1)}, bf16[16,352]{1,0:T(8,128)(2,1)S(1)}, u32[]{:S(2)}, u32[]{:S(2)}) collective-permute-start(bf16[16,352]{1,0:T(8,128)(2,1)S(1)} %pad_maximum_fusion.11), channel_id=1, source_target_pairs={{0,32},{16,48},{32,0},{48,16},{1,33},{17,49},{33,1},{49,17},{2,34}... | collective-permute-start | bytes 33800 | tf_op jit(solution)/shard_map/ppermute | solution.py:98
  79.9 8.4 %collective-permute-start.21 = (s32[2,2,128]{2,1,0:T(2,128)S(1)}, s32[2,2,128]{2,1,0:T(2,128)S(1)}, u32[]{:S(2)}, u32[]{:S(2)}) collective-permute-start(s32[2,2,128]{2,1,0:T(2,128)S(1)} %reverse_select_fusion.1), channel_id=1, source_target_pairs={{0,64},{64,0},{1,65},{65,1},{2,66},{66,2},{3,67},{67,3},{4,68},{68... | collective-permute-start | bytes 6152 | tf_op jit(solution)/shard_map/ppermute | solution.py:29
  83.9 24.4 %collective-permute-start.20 = (bf16[512,2048]{1,0:T(8,128)(2,1)}, bf16[512,2048]{1,0:T(8,128)(2,1)}, u32[]{:S(2)}, u32[]{:S(2)}) collective-permute-start(bf16[512,2048]{1,0:T(8,128)(2,1)} %constant_dynamic-update-slice_fusion.5.near_hbm), channel_id=1, source_target_pairs={{0,2},{2,0},{1,3},{3,1},{4,6},{6,4},{5,7},{7,5},{8,10},{10,8},{9,1... | collective-permute-start | bytes 6291464 | tf_op jit(solution)/shard_map/ppermute | solution.py:29
  88.4 4.0 %collective-permute-start.22 = (s32[4,2,128]{2,0,1:T(4,128)S(1)}, s32[4,2,128]{2,0,1:T(4,128)S(1)}, u32[]{:S(2)}, u32[]{:S(2)}) collective-permute-start(s32[4,2,128]{2,0,1:T(4,128)S(1)} %get-tuple-element.217), channel_id=1, source_target_pairs={{0,2},{2,0},{1,3},{3,1},{4,6},{6,4},{5,7},{7,5},{8,10},{10,8},{9,1... | collective-permute-start | bytes 12296 | tf_op jit(solution)/shard_map/ppermute | solution.py:29
  89.1 8.1 %collective-permute-start.19 = (bf16[32,352]{1,0:T(8,128)(2,1)S(1)}, bf16[32,352]{1,0:T(8,128)(2,1)S(1)}, u32[]{:S(2)}, u32[]{:S(2)}) collective-permute-start(bf16[32,352]{1,0:T(8,128)(2,1)S(1)} %pad_maximum_fusion.10), channel_id=1, source_target_pairs={{0,64},{64,0},{1,65},{65,1},{2,66},{66,2},{3,67},{67,3},{4,68},{68... | collective-permute-start | bytes 67592 | tf_op jit(solution)/shard_map/ppermute | solution.py:98
  187.0 21.0 %collective-permute-start.24 = (bf16[512,2048]{1,0:T(8,128)(2,1)}, bf16[512,2048]{1,0:T(8,128)(2,1)S(1)}, u32[]{:S(2)}, u32[]{:S(2)}) collective-permute-start(bf16[512,2048]{1,0:T(8,128)(2,1)} %get-tuple-element.118), channel_id=1, source_target_pairs={{0,2},{2,0},{1,3},{3,1},{4,6},{6,4},{5,7},{7,5},{8,10},{10,8},{9,1... | collective-permute-start | bytes 6291464 | tf_op jit(solution)/shard_map/ppermute | solution.py:29
  194.1 13.9 %collective-permute-start.23 = (f32[32,320]{1,0:T(8,128)S(1)}, f32[32,320]{1,0:T(8,128)S(1)}, u32[]{:S(2)}, u32[]{:S(2)}) collective-permute-start(f32[32,320]{1,0:T(8,128)S(1)} %dynamic-slice_bitcast_fusion.4), channel_id=1, source_target_pairs={{0,64},{64,0},{1,65},{65,1},{2,66},{66,2},{3,67},{67,3},{4,68},{68... | collective-permute-start | bytes 122888 | tf_op jit(solution)/shard_map/ppermute | solution.py:98
  208.0 15.7 %collective-permute-start.28 = (bf16[512,2048]{1,0:T(8,128)(2,1)}, bf16[512,2048]{1,0:T(8,128)(2,1)}, u32[]{:S(2)}, u32[]{:S(2)}) collective-permute-start(bf16[512,2048]{1,0:T(8,128)(2,1)} %get-tuple-element.121), channel_id=1, source_target_pairs={{0,2},{2,0},{1,3},{3,1},{4,6},{6,4},{5,7},{7,5},{8,10},{10,8},{9,1... | collective-permute-start | bytes 6291464 | tf_op jit(solution)/shard_map/ppermute | solution.py:29
  208.5 4.9 %collective-permute-start.25 = (f32[16,320]{1,0:T(8,128)S(1)}, f32[16,320]{1,0:T(8,128)S(1)}, u32[]{:S(2)}, u32[]{:S(2)}) collective-permute-start(f32[16,320]{1,0:T(8,128)S(1)} %dynamic-slice_bitcast_fusion.5), channel_id=1, source_target_pairs={{0,32},{16,48},{32,0},{48,16},{1,33},{17,49},{33,1},{49,17},{2,34}... | collective-permute-start | bytes 61448 | tf_op jit(solution)/shard_map/ppermute | solution.py:98
  213.4 4.6 %collective-permute-start.26 = (f32[8,320]{1,0:T(8,128)S(1)}, f32[8,320]{1,0:T(8,128)S(1)}, u32[]{:S(2)}, u32[]{:S(2)}) collective-permute-start(f32[8,320]{1,0:T(8,128)S(1)} %dynamic-slice_bitcast_fusion.6), channel_id=1, source_target_pairs={{0,16},{16,0},{32,48},{48,32},{1,17},{17,1},{33,49},{49,33},{2,18}... | collective-permute-start | bytes 30728 | tf_op jit(solution)/shard_map/ppermute | solution.py:98
  215.4 8.4 %collective-permute-start.29 = (bf16[64,2048]{1,0:T(8,128)(2,1)}, bf16[64,2048]{1,0:T(8,128)(2,1)S(1)}, u32[]{:S(2)}, u32[]{:S(2)}) collective-permute-start(bf16[64,2048]{1,0:T(8,128)(2,1)} %get-tuple-element.188), channel_id=1, source_target_pairs={{0,1},{1,64},{64,65},{65,0},{2,3},{3,66},{66,67},{67,2},{4,5},{5,6... | collective-permute-start | bytes 786440 | tf_op jit(solution)/shard_map/ppermute | solution.py:29
  215.6 8.1 %collective-permute-start.30 = (bf16[64,2048]{1,0:T(8,128)(2,1)S(1)}, bf16[64,2048]{1,0:T(8,128)(2,1)S(1)}, u32[]{:S(2)}, u32[]{:S(2)}) collective-permute-start(bf16[64,2048]{1,0:T(8,128)(2,1)S(1)} %get-tuple-element.187), channel_id=1, source_target_pairs={{0,65},{1,0},{64,1},{65,64},{2,67},{3,2},{66,3},{67,66},{4,69},{5,... | collective-permute-start | bytes 786440 | tf_op jit(solution)/shard_map/ppermute | solution.py:29
  218.1 4.2 %collective-permute-start.27 = (f32[4,320]{1,0:T(4,128)S(1)}, f32[4,320]{1,0:T(4,128)S(1)}, u32[]{:S(2)}, u32[]{:S(2)}) collective-permute-start(f32[4,320]{1,0:T(4,128)S(1)} %fusion.17), channel_id=1, source_target_pairs={{0,8},{4,12},{8,0},{12,4},{1,9},{5,13},{9,1},{13,5},{2,10},{6,14},... | collective-permute-start | bytes 15368 | tf_op jit(solution)/shard_map/ppermute | solution.py:98
  224.6 21.3 %collective-permute-start.37 = (bf16[128,2048]{1,0:T(8,128)(2,1)}, bf16[128,2048]{1,0:T(8,128)(2,1)}, u32[]{:S(2)}, u32[]{:S(2)}) collective-permute-start(bf16[128,2048]{1,0:T(8,128)(2,1)} %pad_maximum_fusion.4), channel_id=1, source_target_pairs={{0,65},{1,0},{64,1},{65,64},{2,67},{3,2},{66,3},{67,66},{4,69},{5,... | collective-permute-start | bytes 1572872 | tf_op jit(solution)/shard_map/ppermute | solution.py:29
  227.7 18.2 %collective-permute-start.36 = (bf16[128,2048]{1,0:T(8,128)(2,1)}, bf16[128,2048]{1,0:T(8,128)(2,1)}, u32[]{:S(2)}, u32[]{:S(2)}) collective-permute-start(bf16[128,2048]{1,0:T(8,128)(2,1)} %pad_maximum_fusion.3), channel_id=1, source_target_pairs={{0,1},{1,64},{64,65},{65,0},{2,3},{3,66},{66,67},{67,2},{4,5},{5,6... | collective-permute-start | bytes 1572872 | tf_op jit(solution)/shard_map/ppermute | solution.py:29
  227.7 3.6 %collective-permute-start.31 = (f32[2,320]{1,0:T(2,128)S(1)}, f32[2,320]{1,0:T(2,128)S(1)}, u32[]{:S(2)}, u32[]{:S(2)}) collective-permute-start(f32[2,320]{1,0:T(2,128)S(1)} %fusion.20), channel_id=1, source_target_pairs={{0,4},{4,0},{8,12},{12,8},{1,5},{5,1},{9,13},{13,9},{2,6},{6,2},{1... | collective-permute-start | bytes 7688 | tf_op jit(solution)/shard_map/ppermute | solution.py:98
  231.4 6.3 %collective-permute-start.32 = (f32[1,320]{1,0:T(1,128)S(1)}, f32[1,320]{1,0:T(1,128)S(1)}, u32[]{:S(2)}, u32[]{:S(2)}) collective-permute-start(f32[1,320]{1,0:T(1,128)S(1)} %constant_dynamic-slice_fusion.1), channel_id=1, source_target_pairs={{0,2},{2,0},{1,3},{3,1},{4,6},{6,4},{5,7},{7,5},{8,10},{10,8},{9,1... | collective-permute-start | bytes 3848 | tf_op jit(solution)/shard_map/ppermute | solution.py:98
  234.7 11.2 %collective-permute-start.34 = (bf16[64,2048]{1,0:T(8,128)(2,1)}, bf16[64,2048]{1,0:T(8,128)(2,1)}, u32[]{:S(2)}, u32[]{:S(2)}) collective-permute-start(bf16[64,2048]{1,0:T(8,128)(2,1)} %get-tuple-element.186), channel_id=1, source_target_pairs={{0,1},{1,64},{64,65},{65,0},{2,3},{3,66},{66,67},{67,2},{4,5},{5,6... | collective-permute-start | bytes 786440 | tf_op jit(solution)/shard_map/ppermute | solution.py:29
  234.7 11.2 %collective-permute-start.35 = (bf16[64,2048]{1,0:T(8,128)(2,1)}, bf16[64,2048]{1,0:T(8,128)(2,1)S(1)}, u32[]{:S(2)}, u32[]{:S(2)}) collective-permute-start(bf16[64,2048]{1,0:T(8,128)(2,1)} %get-tuple-element.185), channel_id=1, source_target_pairs={{0,65},{1,0},{64,1},{65,64},{2,67},{3,2},{66,3},{67,66},{4,69},{5,... | collective-permute-start | bytes 786440 | tf_op jit(solution)/shard_map/ppermute | solution.py:29
  237.7 5.7 %collective-permute-start.33 = (f32[1,320]{1,0:T(1,128)S(1)}, f32[1,320]{1,0:T(1,128)S(1)}, u32[]{:S(2)}, u32[]{:S(2)}) collective-permute-start(f32[1,320]{1,0:T(1,128)S(1)} %fusion.21), channel_id=1, source_target_pairs={{0,1},{1,0},{2,3},{3,2},{4,5},{5,4},{6,7},{7,6},{8,9},{9,8},{10,11... | collective-permute-start | bytes 3848 | tf_op jit(solution)/shard_map/ppermute | solution.py:29
  247.8 11.7 %collective-permute-start.38 = (bf16[128,2048]{1,0:T(8,128)(2,1)}, bf16[128,2048]{1,0:T(8,128)(2,1)}, u32[]{:S(2)}, u32[]{:S(2)}) collective-permute-start(bf16[128,2048]{1,0:T(8,128)(2,1)} %pad_maximum_fusion.5), channel_id=1, source_target_pairs={{0,1},{1,64},{64,65},{65,0},{2,3},{3,66},{66,67},{67,2},{4,5},{5,6... | collective-permute-start | bytes 1572872 | tf_op jit(solution)/shard_map/ppermute | solution.py:29
  248.7 10.8 %collective-permute-start.39 = (bf16[128,2048]{1,0:T(8,128)(2,1)}, bf16[128,2048]{1,0:T(8,128)(2,1)}, u32[]{:S(2)}, u32[]{:S(2)}) collective-permute-start(bf16[128,2048]{1,0:T(8,128)(2,1)} %pad_maximum_fusion.6), channel_id=1, source_target_pairs={{0,65},{1,0},{64,1},{65,64},{2,67},{3,2},{66,3},{67,66},{4,69},{5,... | collective-permute-start | bytes 1572872 | tf_op jit(solution)/shard_map/ppermute | solution.py:29
  268.6 20.0 %collective-permute-start.40 = (bf16[256,1024]{1,0:T(8,128)(2,1)}, bf16[256,1024]{1,0:T(8,128)(2,1)S(1)}, u32[]{:S(2)}, u32[]{:S(2)}) collective-permute-start(bf16[256,1024]{1,0:T(8,128)(2,1)} %get-tuple-element.137), channel_id=1, source_target_pairs={{0,1},{1,0},{64,65},{65,64},{2,3},{3,2},{66,67},{67,66},{4,5},{5,4... | collective-permute-start | bytes 1572872 | tf_op jit(solution)/shard_map/ppermute | solution.py:41
  269.8 18.8 %collective-permute-start.41 = (bf16[128,1024]{1,0:T(8,128)(2,1)}, bf16[128,1024]{1,0:T(8,128)(2,1)S(1)}, u32[]{:S(2)}, u32[]{:S(2)}) collective-permute-start(bf16[128,1024]{1,0:T(8,128)(2,1)} %get-tuple-element.138), channel_id=1, source_target_pairs={{0,64},{1,65},{64,0},{65,1},{2,66},{3,67},{66,2},{67,3},{4,68},{5,... | collective-permute-start | bytes 786440 | tf_op jit(solution)/shard_map/ppermute | solution.py:41
  272.2 16.4 %collective-permute-start.42 = (bf16[128,1024]{1,0:T(8,128)(2,1)}, bf16[128,1024]{1,0:T(8,128)(2,1)S(1)}, u32[]{:S(2)}, u32[]{:S(2)}) collective-permute-start(bf16[128,1024]{1,0:T(8,128)(2,1)} %get-tuple-element.139), channel_id=1, source_target_pairs={{0,65},{1,64},{64,1},{65,0},{2,67},{3,66},{66,3},{67,2},{4,69},{5,... | collective-permute-start | bytes 786440 | tf_op jit(solution)/shard_map/ppermute | solution.py:41
  272.4 8.9 %collective-permute-start.43 = (bf16[16,2048]{1,0:T(8,128)(2,1)}, bf16[16,2048]{1,0:T(8,128)(2,1)S(1)}, u32[]{:S(2)}, u32[]{:S(2)}) collective-permute-start(bf16[16,2048]{1,0:T(8,128)(2,1)} %get-tuple-element.140), channel_id=1, source_target_pairs={{0,0},{4,1},{8,2},{12,3},{16,4},{20,5},{24,6},{28,7},{32,8},{36,9}... | collective-permute-start | bytes 196616 | tf_op jit(solution)/shard_map/ppermute | solution.py:124
  277.9 9.7 %collective-permute-start.44 = (bf16[16,2048]{1,0:T(8,128)(2,1)}, bf16[16,2048]{1,0:T(8,128)(2,1)S(1)}, u32[]{:S(2)}, u32[]{:S(2)}) collective-permute-start(bf16[16,2048]{1,0:T(8,128)(2,1)} %get-tuple-element.140), channel_id=1, source_target_pairs={{0,1},{4,0},{8,3},{12,2},{16,5},{20,4},{24,7},{28,6},{32,9},{36,8}... | collective-permute-start | bytes 196616 | tf_op jit(solution)/shard_map/ppermute | solution.py:124
  289.8 6.2 %collective-permute-start.45 = (bf16[4,64,1024]{2,1,0:T(8,128)(2,1)S(1)}, bf16[4,64,1024]{2,1,0:T(8,128)(2,1)S(1)}, u32[]{:S(2)}, u32[]{:S(2)}) collective-permute-start(bf16[4,64,1024]{2,1,0:T(8,128)(2,1)S(1)} %pad_maximum_fusion.7), channel_id=1, source_target_pairs={{0,2},{2,0},{1,3},{3,1},{4,6},{6,4},{5,7},{7,5},{8,10},{10,8},{9,1... | collective-permute-start | bytes 1572872 | tf_op jit(solution)/shard_map/ppermute | solution.py:29
  (28 other events, 181.0 us)
Sparse Core Ops, SparseCore 0:
  25.2 94.0 all-gather.2
  171.9 94.3 reduce-scatter.1
